TPU v7x, 32 devices: a whole 2x2x4 slice. The times are simulated.
32 devices in a mesh: dp: 8 (over z, y), graph: 4 (over x, core).
Axes of the slice: x: 2, y: 2, z: 4, core: 2. Of those that a mesh axis runs over, the one named last changes fastest.
Arguments:
- atoms: bfloat16 [8, 4, 1024, 128], P('dp', 'graph'), may hold values from -80 to 80, as said below
- gain: float32 [128], replicated, may hold values from 0.1 to 1.9
- w_src: bfloat16 [128, 128], replicated, may hold values from -0.5 to 0.5
- w_edge: bfloat16 [128, 128], replicated, may hold values from -0.5 to 0.5
- w_out: bfloat16 [128, 128], replicated, may hold values from -0.5 to 0.5
- send_src: int32 [8, 4, 4, 2048], P('dp', 'graph'), may hold values from 0 to 1023
- recv_dst: int32 [8, 4, 4, 2048], P('dp', 'graph'), may hold values from 0 to 1023
- edge_count: int32 [8, 4, 4], P('dp'), may hold values from 512 to 2048, as said below
- edge_feat: bfloat16 [8, 4, 4, 2048, 128], P('dp', 'graph'), may hold values from -6 to 6
- cotangent: bfloat16 [8, 4, 1024, 128], P('dp', 'graph'), may hold values from -6 to 6
Outputs:
- layer_out: bfloat16 [8, 4, 1024, 128], P('dp', 'graph')
- grad_atoms: bfloat16 [8, 4, 1024, 128], P('dp', 'graph')
- grad_w_src: float32 [128, 128], P('dp')
- grad_w_edge: float32 [128, 128], P('dp')
- grad_w_out: float32 [128, 128], P('dp')
- grad_gain: float32 [128], P('dp')
Inputs may be any that keep to these rules, and one draw needn't show every extreme that they name: `atoms`: row scales of the atom features vary. `edge_count`: every batch has one destination shard that receives more; in every draw some shard sends exactly 2048 live slots to some shard.
All inputs are finite; a program needn't handle non-finite values.
Results may differ from a plain program's by a relative error of at most 0.0059.
Values may be sent and summed in bfloat16 or wider, within the bound.
No kernel may reach another device: no remote copies, remote signals or barrier semaphores. Data moves between devices by JAX's collectives and lax.ppermute only.
A program may use at most 64 MiB of HBM per device.

v0:
```python
import jax
import jax.numpy as jnp
from jax import lax
from jax.sharding import PartitionSpec as P

DEG_NORM = 23


def silu_slope(pre):
    sig = jax.nn.sigmoid(pre)
    return sig * (1.0 + pre * (1.0 - sig))


def one_hot_table(index, atom_count):
    return (index[:, None] == jnp.arange(atom_count, dtype=jnp.int32)[None, :]).astype(jnp.bfloat16)


def pick_rows(table, index):
    selector = one_hot_table(index, table.shape[0])
    return jnp.dot(selector, table, preferred_element_type=jnp.float32).astype(table.dtype)


def add_rows(values, index, atom_count):
    selector = one_hot_table(index, atom_count)
    return lax.dot_general(
        selector, values, (((0,), (0,)), ((), ())), preferred_element_type=jnp.float32
    )


def body(atoms, gain, w_src, w_edge, w_out, send_src, recv_dst, edge_count, edge_feat, cotangent):
    shards = lax.axis_size("graph")
    myself = lax.axis_index("graph")
    atom_count = atoms.shape[2]
    chans = atoms.shape[3]
    slots = send_src.shape[3]
    width = w_src.shape[1]
    hfull = atoms.reshape(atom_count, chans).astype(jnp.float32)
    inv = lax.rsqrt(jnp.mean(hfull * hfull, axis=-1) + 1e-06)
    normed = (hfull * inv[:, None] * gain).astype(jnp.bfloat16)
    src_local = send_src.reshape(shards, slots)
    dst_local = recv_dst.reshape(shards, slots)
    counts = edge_count[0]
    send_counts = lax.dynamic_index_in_dim(counts, myself, 0, keepdims=False)
    valid = (
        (jnp.arange(slots, dtype=jnp.int32)[None, :] < send_counts[:, None])
        .astype(jnp.float32)
        .reshape(-1, 1)
    )
    rows = jnp.concatenate([pick_rows(normed, src_local[peer]) for peer in range(shards)], axis=0)
    edge_rows = edge_feat.reshape(-1, edge_feat.shape[4])
    pre = jnp.dot(rows, w_src, preferred_element_type=jnp.float32) + jnp.dot(
        edge_rows, w_edge, preferred_element_type=jnp.float32
    )
    msg = (jax.nn.silu(pre) * valid).astype(jnp.bfloat16).reshape(shards, slots, width)
    arrived = lax.all_to_all(msg, "graph", split_axis=0, concat_axis=0, tiled=True)
    summed = add_rows(arrived[0], dst_local[0], atom_count)
    for peer in range(1, shards):
        summed = summed + add_rows(arrived[peer], dst_local[peer], atom_count)
    agg = (summed / DEG_NORM).astype(jnp.bfloat16)
    layer_out = (hfull + jnp.dot(agg, w_out, preferred_element_type=jnp.float32)).astype(
        jnp.bfloat16
    )
    cot_flat = cotangent.reshape(atom_count, chans)
    back = (
        lax.dot_general(
            cot_flat, w_out, (((1,), (1,)), ((), ())), preferred_element_type=jnp.float32
        )
        / DEG_NORM
    ).astype(jnp.bfloat16)
    outgoing = jnp.stack([pick_rows(back, dst_local[peer]) for peer in range(shards)], axis=0)
    slot_back = lax.all_to_all(outgoing, "graph", split_axis=0, concat_axis=0, tiled=True).reshape(
        -1, width
    )
    dpre = (slot_back.astype(jnp.float32) * silu_slope(pre) * valid).astype(jnp.bfloat16)
    grad_src = lax.dot_general(
        rows, dpre, (((0,), (0,)), ((), ())), preferred_element_type=jnp.float32
    )
    grad_edge = lax.dot_general(
        edge_rows, dpre, (((0,), (0,)), ((), ())), preferred_element_type=jnp.float32
    )
    grad_out = lax.dot_general(
        agg, cot_flat, (((0,), (0,)), ((), ())), preferred_element_type=jnp.float32
    )
    dpre_peers = dpre.reshape(shards, slots, width)
    dpre_atoms = add_rows(dpre_peers[0], src_local[0], atom_count)
    for peer in range(1, shards):
        dpre_atoms = dpre_atoms + add_rows(dpre_peers[peer], src_local[peer], atom_count)
    dnorm = lax.dot_general(
        dpre_atoms,
        w_src.astype(jnp.float32),
        (((1,), (1,)), ((), ())),
        precision=lax.Precision.HIGHEST,
        preferred_element_type=jnp.float32,
    )
    scaled = gain * dnorm
    grad_g = jnp.sum(dnorm * hfull * inv[:, None], axis=0)
    grad_h = (
        cot_flat.astype(jnp.float32)
        + inv[:, None] * scaled
        - hfull * (inv**3)[:, None] * jnp.mean(hfull * scaled, axis=-1, keepdims=True)
    )
    grad_atoms = grad_h.astype(jnp.bfloat16).reshape(atoms.shape)
    totals = lax.psum((grad_src, grad_edge, grad_out, grad_g), "graph")
    final = (
        lax.psum_scatter(totals[0], "dp", scatter_dimension=0, tiled=True),
        lax.psum_scatter(totals[1], "dp", scatter_dimension=0, tiled=True),
        lax.psum_scatter(totals[2], "dp", scatter_dimension=0, tiled=True),
        lax.psum_scatter(totals[3], "dp", scatter_dimension=0, tiled=True),
    )
    return (layer_out.reshape(atoms.shape), grad_atoms, final[0], final[1], final[2], final[3])


def solution(mesh):
    in_specs = (
        P("dp", "graph", None, None),
        P(),
        P(),
        P(),
        P(),
        P("dp", "graph", None, None),
        P("dp", "graph", None, None),
        P("dp", None, None),
        P("dp", "graph", None, None, None),
        P("dp", "graph", None, None),
    )
    out_specs = (
        P("dp", "graph", None, None),
        P("dp", "graph", None, None),
        P("dp", None),
        P("dp", None),
        P("dp", None),
        P("dp"),
    )
    return jax.shard_map(body, mesh=mesh, in_specs=in_specs, out_specs=out_specs, check_vma=False)
```

profile of v0, /device:TPU:0, one launch (start us, length us, event | category | flops | bytes accessed | tf_op | source)
XLA Modules:
  0.0 284.0 jit_solution(8981270773959917927)
XLA Ops:
  7.2 0.0 copy-start
  7.2 1.0 fusion.82
  8.2 1.2 fusion.55
  9.4 1.7 fusion.42
  11.1 1.7 fusion.43
  12.8 1.7 fusion.44
  14.5 1.7 fusion.45
  16.2 1.6 pad_maximum_fusion.1
  17.8 4.8 %all-to-all-start.1 = ((bf16[4,2048,128]{2,1,0:T(8,128)(2,1)}), bf16[4,2048,128]{2,1,0:T(8,128)(2,1)}, u32[]{:S(2)}, u32[]{:S(2)}) async-start(bf16[4,2048,128]{2,1,0:T(8,128)(2,1)} %pad_maximum_fusion.1), calls=%async_computation.1 | async-start | bytes 4194304 | tf_op jit(solution)/shard_map/all_to_all | solution.py:71
  22.6 0.0 copy-done.7
  22.6 0.7 dynamic-slice_bitcast_fusion
  23.3 0.1 convert_bitcast_fusion
  23.4 0.2 fusion.57
  23.6 0.6 dynamic-slice.1
  24.9 1.7 fusion.35
  26.5 1.7 fusion.36
  28.2 1.7 fusion.37
  29.9 0.0 copy-start.6
  29.9 1.7 fusion.38
  31.6 0.8 copy-done.15
  32.4 2.6 fusion.71
  35.0 13.9 %all-to-all-done.1 = bf16[4,2048,128]{2,1,0:T(8,128)(2,1)} async-done(((bf16[4,2048,128]{2,1,0:T(8,128)(2,1)}), bf16[4,2048,128]{2,1,0:T(8,128)(2,1)}, u32[]{:S(2)}, u32[]{:S(2)}) %all-to-all-start.1) | async-done | bytes 2097184 | tf_op jit(solution)/shard_map/all_to_all | solution.py:71
  49.0 0.0 copy-done
  49.0 7.1 %fusion.17 = (bf16[8192,128]{1,0:T(8,128)(2,1)S(1)}, bf16[8192,128]{1,0:T(8,128)(2,1)}) fusion(bf16[4,2048,128]{2,1,0:T(8,128)(2,1)} %all-to-all-done.1, f32[8192]{0:T(1024)S(1)} %bitcast.83, f32[8192,128]{1,0:T(8,128)} %fusion.71, bf16[8192,128]{1,0:T(8,128)(2,1)S(1)} %bitcast.80, bf16[128,128]{1,0:T(8,128)(2,1)S(1)} %copy-done.9), kind=kOutput, calls=%fused_computation.27 | convolution fusion | flops 284164096 | bytes 12648448 | tf_op jit(solution)/shard_map/dot_general | solution.py:51
  56.0 0.0 copy-start.3
  56.0 3.5 %fusion.10 = f32[1024,128]{1,0:T(8,128)} fusion(s32[2048]{0:T(1024)S(1)} %bitcast.99, bf16[8192,128]{1,0:T(8,128)(2,1)S(1)} %get-tuple-element.24), kind=kOutput, calls=%fused_computation.17 | convolution fusion | flops 538968064 | bytes 1056768 | tf_op jit(solution)/shard_map/dot_general | solution.py:25
  59.5 3.5 %fusion.6 = f32[1024,128]{1,0:T(8,128)} fusion(s32[2048]{0:T(1024)S(1)} %bitcast.97, bf16[8192,128]{1,0:T(8,128)(2,1)S(1)} %get-tuple-element.24), kind=kOutput, calls=%fused_computation.11 | convolution fusion | flops 538968064 | bytes 1056768 | tf_op jit(solution)/shard_map/dot_general | solution.py:25
  63.0 0.0 copy-done.3
  63.0 0.7 convolution_bitcast_fusion
  63.8 4.5 %all-to-all-start = ((bf16[4,2048,128]{2,1,0:T(8,128)(2,1)}), bf16[4,2048,128]{2,1,0:T(8,128)(2,1)}, u32[]{:S(2)}, u32[]{:S(2)}) async-start(bf16[4,2048,128]{2,1,0:T(8,128)(2,1)} %bitcast.82), calls=%async_computation | async-start | bytes 4194304 | tf_op jit(solution)/shard_map/all_to_all | solution.py:55
  68.3 0.0 reduce-scatter.10.cloned.1.call-start
  68.3 0.7 copy.18
  69.0 0.0 reduce-scatter.10.cloned.1.call-update
  69.1 0.0 reduce-scatter.6.cloned.1.call-start
  69.1 0.0 copy-start.4
  69.1 0.0 copy-start.17
  69.1 0.0 copy-start.18
  69.1 3.9 %fusion.8 = f32[1024,128]{1,0:T(8,128)S(1)} fusion(s32[2048]{0:T(1024)S(1)} %bitcast.95, bf16[8192,128]{1,0:T(8,128)(2,1)} %copy-done.3), kind=kOutput, calls=%fused_computation.14 | convolution fusion | flops 538968064 | bytes 1056768 | tf_op jit(solution)/shard_map/dot_general | solution.py:25
  73.1 3.5 %fusion.52 = f32[1024,128]{1,0:T(8,128)} fusion(f32[1024,128]{1,0:T(8,128)S(1)} %copy-done.18, f32[1024,128]{1,0:T(8,128)S(1)} %fusion.8, f32[1024,128]{1,0:T(8,128)S(1)} %copy-done.17, s32[2048]{0:T(1024)S(1)} %bitcast.93, bf16[8192,128]{1,0:T(8,128)(2,1)S(1)} %copy-done.4), kind=kOutput, calls=%fused_computation.68 | convolution fusion | flops 539361280 | bytes 2629632 | tf_op jit(solution)/shard_map/dot_general | solution.py:25
  76.6 0.0 copy-done.12
  76.6 0.0 copy-done.16
  76.6 1.4 fusion.70
  78.0 1.6 fusion.65
  79.6 22.5 %all-reduce = f32[128]{0:T(128)S(1)} all-reduce(f32[128]{0:T(128)S(1)} %get-tuple-element.18), channel_id=5, replica_groups=mesh['dp'=8,'graph'=4] {'dp'}, use_global_device_ids=true, to_apply=%region_10.11.clone | all-reduce | flops 128 | bytes 1024
  102.1 0.1 dynamic-slice.2
  102.1 0.0 reduce-scatter.6.cloned.1.call-update
  102.2 0.3 reduce-scatter.8.cloned.1.call-start
  102.5 0.0 copy-done.2
  102.5 1.2 fusion.72
  103.7 33.1 %reduce-scatter.10.cloned.1.call-done = f32[16,128]{1,0:T(8,128)} async-done(((f32[128,128]{1,0:T(8,128)}), f32[16,128]{1,0:T(8,128)}) %reduce-scatter.10.cloned.1.call-update) | async-done | bytes 8208
  136.8 0.8 copy.19
  137.6 0.0 all-to-all-done
  137.6 3.7 %fusion.3 = f32[1024,128]{1,0:T(8,128)S(1)} fusion(s32[2048]{0:T(1024)S(1)} %bitcast.91, bf16[4,2048,128]{2,1,0:T(8,128)(2,1)} %all-to-all-done), kind=kOutput, calls=%fused_computation.6 | convolution fusion | flops 538968064 | bytes 1056768 | tf_op jit(solution)/shard_map/dot_general | solution.py:25
  141.3 3.7 %fusion.5 = f32[1024,128]{1,0:T(8,128)S(1)} fusion(s32[2048]{0:T(1024)S(1)} %bitcast.89, bf16[4,2048,128]{2,1,0:T(8,128)(2,1)} %all-to-all-done), kind=kOutput, calls=%fused_computation.9 | convolution fusion | flops 538968064 | bytes 1056768 | tf_op jit(solution)/shard_map/dot_general | solution.py:25
  145.1 3.7 %fusion.1 = f32[1024,128]{1,0:T(8,128)S(1)} fusion(s32[2048]{0:T(1024)S(1)} %bitcast.87, bf16[4,2048,128]{2,1,0:T(8,128)(2,1)} %all-to-all-done), kind=kOutput, calls=%fused_computation.3 | convolution fusion | flops 538968064 | bytes 1056768 | tf_op jit(solution)/shard_map/dot_general | solution.py:25
  148.8 0.0 copy-start.5
  148.8 3.8 %fusion.53 = bf16[1024,128]{1,0:T(8,128)(2,1)S(1)} fusion(f32[1024,128]{1,0:T(8,128)S(1)} %fusion.1, f32[1024,128]{1,0:T(8,128)S(1)} %fusion.3, f32[1024,128]{1,0:T(8,128)S(1)} %fusion.5, s32[2048]{0:T(1024)S(1)} %bitcast.85, bf16[4,2048,128]{2,1,0:T(8,128)(2,1)} %all-to-all-done), kind=kOutput, calls=%fused_computation.69 | convolution fusion | flops 539623424 | bytes 2367488 | tf_op jit(solution)/shard_map/dot_general | solution.py:25
  152.6 0.9 fusion.73
  153.5 0.0 reduce-scatter.8.cloned.1.call-update
  153.5 0.9 fusion.56
  154.5 46.0 %reduce-scatter.6.cloned.1.call-done = f32[16,128]{1,0:T(8,128)} async-done(((f32[128,128]{1,0:T(8,128)}), f32[16,128]{1,0:T(8,128)}) %reduce-scatter.6.cloned.1.call-update) | async-done | bytes 8208 | tf_op jit(solution)/shard_map/reduce_scatter | solution.py:105
  200.5 63.7 %reduce-scatter.8.cloned.1.call-done = f32[16,128]{1,0:T(8,128)} async-done(((f32[128,128]{1,0:T(8,128)}), f32[16,128]{1,0:T(8,128)}) %reduce-scatter.8.cloned.1.call-update) | async-done | bytes 8208 | tf_op jit(solution)/shard_map/reduce_scatter | solution.py:107
  264.2 12.1 %all-reduce.1 = (f32[16,128]{1,0:T(8,128)}, f32[16,128]{0,1:T(8,128)S(1)}, f32[16,128]{1,0:T(8,128)}, f32[16]{0:T(128)}) all-reduce(f32[16,128]{1,0:T(8,128)} %reduce-scatter.6.cloned.1.call-done, f32[16,128]{0,1:T(8,128)S(1)} %copy.19, f32[16,128]{1,0:T(8,128)} %reduce-scatter.8.cloned.1.call-done, ...), channel_id=1, replica_groups=mesh['dp'=8,'graph'=4] {'graph'}, use_global_device_ids=true, to_apply=%region_2.3 | all-reduce | flops 6160 | bytes 49280 | tf_op jit(solution)/shard_map/psum | solution.py:103
  276.3 0.7 copy.17
  (28 shorter events, 0.1 us)
Async XLA Ops:
  7.2 41.8 %copy-start = (bf16[1,1,4,2048,128]{4,3,2,1,0:T(8,128)(2,1)S(1)}, bf16[1,1,4,2048,128]{4,3,2,1,0:T(8,128)(2,1)}, u32[]{:S(2)}) copy-start(bf16[1,1,4,2048,128]{4,3,2,1,0:T(8,128)(2,1)} %param.18) | copy-start | bytes 6291460
  17.8 4.8 %copy-start.7 = (s32[1,1,4,2048]{3,2,1,0:T(4,128)S(1)}, s32[1,1,4,2048]{3,2,1,0:T(4,128)}, u32[]{:S(2)}) copy-start(s32[1,1,4,2048]{3,2,1,0:T(4,128)} %param.15) | copy-start | bytes 98308
  17.8 5.6 %copy-start.1 = (bf16[1,1,1024,128]{3,2,1,0:T(8,128)(2,1)S(1)}, bf16[1,1,1024,128]{3,2,1,0:T(8,128)(2,1)}, u32[]{:S(2)}) copy-start(bf16[1,1,1024,128]{3,2,1,0:T(8,128)(2,1)} %param.10) | copy-start | bytes 786436
  17.8 5.8 %copy-start.10 = (u32[32]{0:T(128)S(1)}, u32[32]{0:T(128)}, u32[]{:S(2)}) copy-start(u32[32]{0:T(128)} %constant.36) | copy-start | bytes 388
  17.8 7.1 %copy-start.8 = (f32[128]{0:T(128)S(1)}, f32[128]{0:T(128)}, u32[]{:S(2)}) copy-start(f32[128]{0:T(128)} %param.11) | copy-start | bytes 1540
  17.8 31.2 %all-to-all-start.1 = ((bf16[4,2048,128]{2,1,0:T(8,128)(2,1)}), bf16[4,2048,128]{2,1,0:T(8,128)(2,1)}, u32[]{:S(2)}, u32[]{:S(2)}) async-start(bf16[4,2048,128]{2,1,0:T(8,128)(2,1)} %pad_maximum_fusion.1), calls=%async_computation.1 | async-start | bytes 4194304 | tf_op jit(solution)/shard_map/all_to_all | solution.py:71
  28.2 3.3 %copy-start.11 = (bf16[2048,128]{1,0:T(8,128)(2,1)}, bf16[2048,128]{1,0:T(8,128)(2,1)S(1)}, u32[]{:S(2)}) copy-start(bf16[2048,128]{1,0:T(8,128)(2,1)S(1)} %fusion.36) | copy-start | bytes 1572868
  29.9 1.7 copy-start.13
  29.9 2.5 copy-start.6
  31.6 0.8 copy-start.15
  32.4 16.6 %copy-start.9 = (bf16[128,128]{1,0:T(8,128)(2,1)S(1)}, bf16[128,128]{1,0:T(8,128)(2,1)}, u32[]{:S(2)}) copy-start(bf16[128,128]{1,0:T(8,128)(2,1)} %param.13) | copy-start | bytes 98308
  56.0 7.0 %copy-start.3 = (bf16[8192,128]{1,0:T(8,128)(2,1)}, bf16[8192,128]{1,0:T(8,128)(2,1)S(1)}, u32[]{:S(2)}) copy-start(bf16[8192,128]{1,0:T(8,128)(2,1)S(1)} %get-tuple-element.24) | copy-start | bytes 6291460
  63.8 73.8 %all-to-all-start = ((bf16[4,2048,128]{2,1,0:T(8,128)(2,1)}), bf16[4,2048,128]{2,1,0:T(8,128)(2,1)}, u32[]{:S(2)}, u32[]{:S(2)}) async-start(bf16[4,2048,128]{2,1,0:T(8,128)(2,1)} %bitcast.82), calls=%async_computation | async-start | bytes 4194304 | tf_op jit(solution)/shard_map/all_to_all | solution.py:55
  68.3 68.5 %reduce-scatter.10.cloned.1.call-start = ((), (), s32[]{:S(2)}) async-start(), calls=%async_computation.7 | async-start | bytes 73728
  69.1 131.4 %reduce-scatter.6.cloned.1.call-start = ((), (), s32[]{:S(2)}) async-start(), calls=%async_computation.5 | async-start | bytes 73728 | tf_op jit(solution)/shard_map/reduce_scatter | solution.py:105
  69.1 3.9 %copy-start.4 = (bf16[8192,128]{1,0:T(8,128)(2,1)S(1)}, bf16[8192,128]{1,0:T(8,128)(2,1)}, u32[]{:S(2)}) copy-start(bf16[8192,128]{1,0:T(8,128)(2,1)} %copy-done.3) | copy-start | bytes 6291460
  69.1 3.9 %copy-start.17 = (f32[1024,128]{1,0:T(8,128)S(1)}, f32[1024,128]{1,0:T(8,128)}, u32[]{:S(2)}) copy-start(f32[1024,128]{1,0:T(8,128)} %fusion.10) | copy-start | bytes 1572868
  69.1 3.9 %copy-start.18 = (f32[1024,128]{1,0:T(8,128)S(1)}, f32[1024,128]{1,0:T(8,128)}, u32[]{:S(2)}) copy-start(f32[1024,128]{1,0:T(8,128)} %fusion.6) | copy-start | bytes 1572868
  73.1 3.5 %copy-start.12 = (bf16[2048,128]{1,0:T(8,128)(2,1)S(1)}, bf16[2048,128]{1,0:T(8,128)(2,1)}, u32[]{:S(2)}) copy-start(bf16[2048,128]{1,0:T(8,128)(2,1)} %copy-done.11) | copy-start | bytes 1572868
  73.1 3.5 %copy-start.14 = (bf16[2048,128]{1,0:T(8,128)(2,1)S(1)}, bf16[2048,128]{1,0:T(8,128)(2,1)}, u32[]{:S(2)}) copy-start(bf16[2048,128]{1,0:T(8,128)(2,1)} %copy-done.13) | copy-start | bytes 1572868
  73.1 3.5 %copy-start.16 = (bf16[2048,128]{1,0:T(8,128)(2,1)S(1)}, bf16[2048,128]{1,0:T(8,128)(2,1)}, u32[]{:S(2)}) copy-start(bf16[2048,128]{1,0:T(8,128)(2,1)} %copy-done.15) | copy-start | bytes 1572868
  76.6 25.9 %copy-start.2 = (bf16[1,1,1024,128]{3,2,1,0:T(8,128)(2,1)S(1)}, bf16[1,1,1024,128]{3,2,1,0:T(8,128)(2,1)}, u32[]{:S(2)}) copy-start(bf16[1,1,1024,128]{3,2,1,0:T(8,128)(2,1)} %param.19) | copy-start | bytes 786436
  102.2 162.1 %reduce-scatter.8.cloned.1.call-start = ((), (), s32[]{:S(2)}) async-start(), calls=%async_computation.6 | async-start | bytes 73728 | tf_op jit(solution)/shard_map/reduce_scatter | solution.py:107
  148.8 4.7 %copy-start.5 = (bf16[128,128]{1,0:T(8,128)(2,1)S(1)}, bf16[128,128]{1,0:T(8,128)(2,1)}, u32[]{:S(2)}) copy-start(bf16[128,128]{1,0:T(8,128)(2,1)} %param.14) | copy-start | bytes 98308
Sparse Core Ops, SparseCore 0:
  73.1 63.6 reduce-scatter.9
  140.2 60.2 reduce-scatter.5
  203.9 60.2 reduce-scatter.7
where the time goes:
time: 288 us; the launch traced here: 284 us
  waiting for transfers between devices  157 us (55%)
  matrix products  59.2 us (21%)
  blocking collectives  34.6 us (12%)
  between operations  15.2 us (5%)
  starting transfers between devices  9.6 us (3%)
  local copies, waits for them, and re-layouts  5.46 us (2%)
  other arithmetic  3.08 us (1%)
    reduce_scatter x1, waiting for transfers between devices, body(): lax.psum_scatter(totals[2], 'dp', scatter_dimension=0, tiled=True)  63.7 us
    reduce_scatter x1, waiting for transfers between devices, body(): lax.psum_scatter(totals[0], 'dp', scatter_dimension=0, tiled=True)  46 us
    unnamed x4, waiting for transfers between devices  33.2 us
    dot_general x8, matrix products, add_rows(): lax.dot_general(selector, values, (((0,), (0,)), ((), ())), preferred_ele...  29.4 us
    unnamed x1, blocking collectives  22.5 us
    all_to_all x1, waiting for transfers between devices, body(): lax.all_to_all(outgoing, 'graph', split_axis=0, concat_axis=0, tiled=True)  13.9 us
    dot_general x8, matrix products, pick_rows(): jnp.dot(selector, table, preferred_element_type=jnp.float32)  13.4 us
    psum x1, blocking collectives, body(): totals = lax.psum((grad_src, grad_edge, grad_out, grad_g), 'graph')  12.1 us
  transfers between devices with their start and end apart: 5, of which 4 were waited for; matrix products, arithmetic and copies ran while one was open for 14% of the time, Pallas kernels for 0%

commit v1 on v0

v1 whole, which is shorter than its diff:
```python
import functools

import jax
import jax.numpy as jnp
from jax import lax
from jax.experimental import pallas as pl
from jax.experimental.pallas import tpu as pltpu
from jax.sharding import PartitionSpec as P

DEG_NORM = 23
GROUP = 256
BLOCK = 1024
F32 = jnp.float32
BF16 = jnp.bfloat16
FAR_VMEM_BYTES = 24 * 1024 * 1024
NEAR_VMEM_BYTES = 56 * 1024 * 1024


def dot(a, b):
    return jnp.dot(a, b, preferred_element_type=F32)


def dot_nt(a, b):
    return lax.dot_general(a, b, (((1,), (1,)), ((), ())), preferred_element_type=F32)


def split(x):
    high = x.astype(BF16)
    return high, (x - high.astype(F32)).astype(BF16)


def stack_groups(x, groups):
    return jnp.concatenate([x[:, g * GROUP : (g + 1) * GROUP] for g in range(groups)], axis=0)


def unstack_groups(x, groups):
    rows = x.shape[0] // groups
    return jnp.concatenate([x[g * rows : (g + 1) * rows, :] for g in range(groups)], axis=1)


def spread(x, which, groups):
    return jnp.concatenate([x * (which == g).astype(F32).astype(BF16) for g in range(groups)], axis=0)


def choose(x, which, groups):
    rows = x.shape[0] // groups
    out = x[:rows, :]
    for g in range(1, groups):
        out = jnp.where(which == g, x[g * rows : (g + 1) * rows, :], out)
    return out


def one_hot(low):
    place = lax.broadcasted_iota(jnp.int32, (GROUP, low.shape[1]), 0)
    return jnp.where(place == low, 1.0, 0.0).astype(BF16)


def column(gain):
    return jnp.broadcast_to(gain[...], (gain.shape[1], gain.shape[1])).T[:, :1]


def norm_parts(atoms):
    feats = atoms.astype(F32).T
    inv = lax.rsqrt(jnp.mean(feats * feats, axis=0, keepdims=True) + 1e-06)
    return feats, inv


def peer_of(k):
    return lax.axis_index("graph") ^ k


class Fetched:
    def __init__(self, source, held, sem):
        self.held = held
        self.copy = pltpu.make_async_copy(source, held, sem)
        self.copy.start()

    def take(self):
        if self.copy is not None:
            self.copy.wait()
            self.copy = None
        return self.held


class Many:
    def __init__(self, moves, held):
        self.held = held
        self.parts = [Fetched(*move) for move in moves]

    def take(self):
        for part in self.parts:
            part.take()
        return self.held


def with_fetches(kernel, kinds, ks, outs, *refs):
    refs = list(refs)
    count = sum(len(ks) if kind == "many" else 1 for kind in kinds)
    ins, refs = refs[:count], refs[count:]
    results, refs = refs[:outs], refs[outs:]
    given = []
    ins = iter(ins)
    for kind in kinds:
        ref = next(ins)
        if kind == "many":
            held, sems = refs.pop(0), refs.pop(0)
            sources = [ref] + [next(ins) for _ in ks[1:]]
            given.append(Many([(x, held.at[i], sems.at[i]) for i, x in enumerate(sources)], held))
        elif kind == "edges":
            held, sems = refs.pop(0), refs.pop(0)
            given.append(Many([(ref.at[peer_of(k)], held.at[i], sems.at[i]) for i, k in enumerate(ks)], held))
        elif kind == "copy":
            given.append(Fetched(ref, refs.pop(0), refs.pop(0)))
        else:
            given.append(ref)
    kernel(ks, *given, *results, *refs)


def back_table(w_out, cot, groups):
    back_t = (dot_nt(w_out[...], cot[...]) * (1.0 / DEG_NORM)).astype(BF16)
    return stack_groups(back_t, groups)


def run_blocks(ks, counts, src, dsts, edges, table, back, w_src_t, w_edge_t, agg_sum, src_sum, edge_sum, hold):
    groups = back.shape[1] // edge_sum.shape[0]
    me = lax.axis_index("graph")
    sizes = [counts[me, peer_of(k)] for k in ks]
    firsts = [0]
    for size in sizes:
        firsts.append(firsts[-1] + (size + BLOCK - 1) // BLOCK)
    total = firsts[-1]

    def locate(item):
        i = jnp.int32(0)
        first = jnp.int32(0)
        peer = peer_of(ks[0])
        size = sizes[0]
        for j in range(1, len(ks)):
            past = item >= firsts[j]
            i = jnp.where(past, j, i)
            first = jnp.where(past, firsts[j], first)
            peer = jnp.where(past, peer_of(ks[j]), peer)
            size = jnp.where(past, sizes[j], size)
        start = pl.multiple_of((item - first) * BLOCK, BLOCK)
        span = pl.ds(start, BLOCK)
        live = lax.broadcasted_iota(jnp.int32, (1, BLOCK), 1) + start < size
        s = src[pl.ds(peer, 1), span]
        d = dsts[i, pl.ds(me, 1), span]
        s_low = jnp.where(live, s % GROUP, -1)
        d_low = jnp.where(live, d % GROUP, -1)
        return i, span, s_low, s // GROUP, d_low, d // GROUP

    def gather(item):
        i, span, s_low, s_high, d_low, d_high = locate(item)
        rows = choose(dot(table[...], one_hot(s_low)), s_high, groups).astype(BF16)
        pre = dot(w_src_t, rows) + dot_nt(w_edge_t, edges[i, span, :])
        slot_back = choose(dot(back[i], one_hot(d_low)), d_high, groups)
        sig = 0.5 * jnp.tanh(0.5 * pre) + 0.5
        act = pre * sig
        slope = sig + act - act * sig
        return act.astype(BF16), (slot_back * slope).astype(BF16)

    def scatter(item, msg, dpre):
        i, span, s_low, s_high, d_low, d_high = locate(item)
        agg_sum[i] += dot_nt(spread(msg, d_high, groups), one_hot(d_low))
        edge_sum[...] += dot(dpre, edges[i, span, :])
        src_sum[...] += dot_nt(spread(dpre, s_high, groups), one_hot(s_low))

    def step(item, carry):
        msg, dpre = hold[0], hold[1]
        next_msg, next_dpre = gather(item)
        scatter(item - 1, msg, dpre)
        hold[0] = next_msg
        hold[1] = next_dpre
        return carry

    @pl.when(total > 0)
    def _():
        msg, dpre = gather(0)
        hold[0] = msg
        hold[1] = dpre

    lax.fori_loop(1, total, step, 0)

    @pl.when(total > 0)
    def _():
        scatter(total - 1, hold[0], hold[1])


def slots_of(ks, refs, table, back, parts, agg_sum, src_sum, edge_sum, out_sum, hold):
    w_out, cots, w_src, w_edge, counts, src, dsts, edges = refs
    groups = back.shape[1] // edge_sum.shape[0]
    w_out = w_out.take()
    cots = cots.take()
    for i in range(len(ks)):
        back[i] = back_table(w_out, cots.at[i], groups)
    agg_sum[...] = jnp.zeros_like(agg_sum)
    w_src_t, w_edge_t = w_src.take()[...].T, w_edge.take()[...].T
    counts, src = counts.take(), src.take()
    dsts, edges = dsts.take(), edges.take()
    run_blocks(
        ks, counts, src, dsts, edges, table, back, w_src_t, w_edge_t, agg_sum, src_sum, edge_sum, hold
    )
    for i in range(len(ks)):
        part = (unstack_groups(agg_sum[i], groups) * (1.0 / DEG_NORM)).astype(BF16)
        parts[i] = part
        out_sum[...] += dot(part, cots[i])


def three_sums(sums, chans):
    tall = sums.shape[0] - chans
    return sums.at[:tall], sums.at[tall:, :chans], sums.at[tall:, chans:]


def near_kernel(ks, *refs):
    atoms, gain, *fetched = refs[:10]
    sums, parts, table, back, agg_sum, hold = refs[10:]
    sums[...] = jnp.zeros_like(sums)
    feats, inv = norm_parts(atoms.take()[...])
    table[...] = stack_groups((feats * inv * column(gain.take())).astype(BF16), back.shape[1] // parts.shape[1])
    slots_of(ks, fetched, table, back, parts, agg_sum, *three_sums(sums, parts.shape[1]), hold)


def far_kernel(ks, *refs):
    atoms, gain, *fetched = refs[:10]
    sums, parts, chunks, dnorm_out, table, back, agg_sum, hold = refs[10:]
    chans = parts.shape[1]
    groups = back.shape[1] // chans
    feats, inv = norm_parts(atoms.take()[...])
    normed = (feats * inv * column(gain.take())).astype(BF16)
    table[...] = stack_groups(normed, groups)
    src_sum, edge_sum, out_sum = three_sums(sums.take(), chans)
    slots_of(ks, fetched, table, back, parts, agg_sum, src_sum, edge_sum, out_sum, hold)
    w_src = fetched[2].take()
    high, low = split(unstack_groups(src_sum[...], groups))
    grad_src = dot_nt(normed, high) + dot_nt(normed, low)
    dnorm = dot(w_src[...], high) + dot(w_src[...], low)
    dnorm_out[...] = dnorm
    grad_gain = jnp.sum(dnorm * feats * inv, axis=1, keepdims=True)
    grad_gain = jnp.broadcast_to(grad_gain, (chans, chans)).T
    grad_edge = edge_sum[...].T
    grad_out = out_sum[...]
    batches = chunks.shape[0]
    rows = chans // batches
    mine = lax.axis_index("dp")
    for j in range(batches):
        place = j ^ mine
        for n, grad in enumerate((grad_src, grad_edge, grad_out)):
            chunks[place, n * rows : (n + 1) * rows, :] = grad[j * rows : (j + 1) * rows, :]
        chunks[place, 3 * rows :, :] = grad_gain[: chunks.shape[1] - 3 * rows, :]


def atom_kernel(ks, atoms, gain, w_out, cot, dnorm, agg_a, agg_b, layer_out, grad_atoms):
    feats_rows = atoms.take()[...]
    feats, inv = norm_parts(feats_rows)
    scaled = column(gain.take()) * dnorm.take()[...]
    mean = jnp.mean(feats * scaled, axis=0, keepdims=True)
    rest = inv * scaled - feats * (inv * inv * inv * mean)
    grad_atoms[...] = (cot.take()[...].astype(F32) + rest.T).astype(BF16)
    agg = (agg_a.take()[...].astype(F32) + agg_b.take()[...].astype(F32)).T.astype(BF16)
    layer_out[...] = (feats_rows.astype(F32) + dot(agg, w_out.take()[...])).astype(BF16)


def move(x, axis, bit):
    size = lax.axis_size(axis)
    return lax.ppermute(x, axis, [(i, i ^ bit) for i in range(size)])


def reduce_batches(chunks, bits):
    for _ in range(bits):
        batches, rows, width = chunks.shape
        bit = lax.axis_size("dp") // batches
        pair = chunks.reshape(batches // 2, 2, rows, width)
        chunks = pair[:, 0] + move(pair[:, 1], "dp", bit)
    return chunks


def body(atoms, gain, w_src, w_edge, w_out, send_src, recv_dst, edge_count, edge_feat, cotangent):
    shards = lax.axis_size("graph")
    batches = lax.axis_size("dp")
    batch = lax.axis_index("dp")
    atom_count, chans = atoms.shape[2:]
    slots = send_src.shape[3]
    groups = atom_count // GROUP
    feats = atoms.reshape(atom_count, chans)
    src = send_src.reshape(shards, slots)
    dst_here = recv_dst.reshape(shards, slots)
    cot = cotangent.reshape(atom_count, chans)
    gain_row = gain.reshape(1, chans)
    edges = edge_feat.reshape(shards, slots, edge_feat.shape[4])
    counts = edge_count.reshape(shards, shards)

    far_dst = move(dst_here, "graph", 2)
    far = move(cot, "graph", 2)
    dst = [dst_here, move(dst_here, "graph", 1)]
    src, far_dst = lax.optimization_barrier((src, far_dst))
    cots = [cot, move(cot, "graph", 1), far]

    vmem = pl.BlockSpec(memory_space=pltpu.VMEM)
    hbm = pl.BlockSpec(memory_space=pltpu.HBM)

    def call(kernel, ks, outs, ins, scratch, name, flops, limit):
        kinds, flat, buffers = [], [], []
        for x in ins:
            if isinstance(x, list):
                kinds.append("many")
                flat += x
                buffers += [pltpu.VMEM((len(x),) + x[0].shape, x[0].dtype), pltpu.SemaphoreType.DMA((len(x),))]
            elif x is edges:
                kinds.append("edges")
                flat.append(x)
                buffers += [pltpu.VMEM((len(ks),) + x.shape[1:], x.dtype), pltpu.SemaphoreType.DMA((len(ks),))]
            elif id(x) in here:
                kinds.append("here")
                flat.append(x)
            else:
                kinds.append("copy")
                flat.append(x)
                space = pltpu.SMEM if x is counts else pltpu.VMEM
                buffers += [space(x.shape, x.dtype), pltpu.SemaphoreType.DMA]
        return pl.pallas_call(
            functools.partial(with_fetches, kernel, kinds, ks, len(outs)),
            out_shape=tuple(jax.ShapeDtypeStruct(shape, kind) for shape, kind in outs),
            in_specs=[vmem if id(x) in here else hbm for x in flat],
            out_specs=(vmem,) * len(outs),
            scratch_shapes=buffers + scratch,
            compiler_params=pltpu.CompilerParams(vmem_limit_bytes=limit),
            cost_estimate=pl.CostEstimate(flops=flops, bytes_accessed=1 << 20, transcendentals=0),
            name=name,
        )(*flat)

    here = set()
    tall = (groups * chans, GROUP)
    sums_shape = (groups * chans + chans, GROUP)
    part_shape = (chans, atom_count)
    unit = 2 * slots * atom_count * chans

    def work(ks):
        return [
            pltpu.VMEM(tall, BF16),
            pltpu.VMEM((len(ks),) + tall, BF16),
            pltpu.VMEM((len(ks),) + tall, F32),
            pltpu.VMEM((2, chans, BLOCK), BF16),
        ]

    near, distant = (0, 1), (2, 3)
    sums, near_parts = call(
        near_kernel,
        near,
        [(sums_shape, F32), ((2,) + part_shape, BF16)],
        [feats, gain_row, w_out, cots[:2], w_src, w_edge, counts, src, dst[:2], edges],
        work(near),
        "near_edges",
        8 * unit,
        NEAR_VMEM_BYTES,
    )
    far, far_dst, sums = lax.optimization_barrier((far, far_dst, sums))
    dst = dst + [far_dst, move(far_dst, "graph", 1)]
    cots = cots[:2] + [far, move(far, "graph", 1)]
    rows = chans // batches
    chunk_rows = -(-(3 * rows + 1) // 8) * 8
    far_parts, chunks, dnorm = call(
        far_kernel,
        distant,
        [((2,) + part_shape, BF16), ((batches, chunk_rows, chans), F32), ((chans, atom_count), F32)],
        [feats, gain_row, w_out, cots[2:], w_src, w_edge, counts, src, dst[2:], edges, sums],
        work(distant),
        "far_edges",
        8 * unit,
        FAR_VMEM_BYTES,
    )

    given_far = move(far_parts[1], "graph", 1)
    chunks = reduce_batches(chunks, 1)
    chunks, given_far = lax.optimization_barrier((chunks, given_far))
    far_part = (far_parts[0].astype(F32) + given_far.astype(F32)).astype(BF16)
    arrived = move(far_part, "graph", 2)
    own_part = near_parts[0].astype(F32) + move(near_parts[1], "graph", 1).astype(F32)
    chunks = reduce_batches(chunks, batches.bit_length() - 2)
    chunks, arrived = lax.optimization_barrier((chunks, arrived))
    total = chunks.reshape(chunk_rows, chans)
    total = total + move(total, "graph", 2)

    layer_out, grad_atoms = call(
        atom_kernel,
        (),
        [(feats.shape, BF16)] * 2,
        [feats, gain_row, w_out, cot, dnorm, own_part, arrived],
        [],
        "atoms",
        unit // 8,
        FAR_VMEM_BYTES,
    )

    total, layer_out, grad_atoms = lax.optimization_barrier((total, layer_out, grad_atoms))
    reduced = total + move(total, "graph", 1)
    grad_gain = lax.dynamic_slice_in_dim(reduced[3 * rows], batch * rows, rows, 0)
    return (
        layer_out.reshape(atoms.shape),
        grad_atoms.reshape(atoms.shape),
        reduced[:rows],
        reduced[rows : 2 * rows],
        reduced[2 * rows : 3 * rows],
        grad_gain,
    )


def solution(mesh):
    in_specs = (
        P("dp", "graph", None, None),
        P(),
        P(),
        P(),
        P(),
        P("dp", "graph", None, None),
        P("dp", "graph", None, None),
        P("dp", None, None),
        P("dp", "graph", None, None, None),
        P("dp", "graph", None, None),
    )
    out_specs = (
        P("dp", "graph", None, None),
        P("dp", "graph", None, None),
        P("dp", None),
        P("dp", None),
        P("dp", None),
        P("dp"),
    )
    return jax.shard_map(body, mesh=mesh, in_specs=in_specs, out_specs=out_specs, check_vma=False)
```

time: 288 us -> 46.8 us (0.16); the launches traced: 284 us -> 47.1 us
  waiting for transfers between devices: 157 us -> 9.84 us
  matrix products: 59.2 us -> 0 us
  blocking collectives: 34.6 us -> 0 us
  Pallas kernels: 0 us -> 16.2 us
  between operations: 15.2 us -> 0.89 us
  starting transfers between devices: 9.6 us -> 17 us
  other arithmetic: 3.08 us -> 0.17 us
    reduce_scatter x2 -> x0, waiting for transfers between devices: 110 us -> none  [the longest x1 63.7 us: body(): lax.psum_scatter(totals[2], 'dp', scatter_dimension=0, tiled=True)]
    dot_general x24 -> x0, matrix products: 59.2 us -> none  [the longest x8 29.4 us: add_rows(): lax.dot_general(selector, values, (((0,), (0,)), ((), ())), preferred_ele...]
    unnamed x4 -> x0, waiting for transfers between devices: 33.2 us -> none
    unnamed x1 -> x0, blocking collectives: 22.5 us -> none
    ppermute x0 -> x14, starting transfers between devices: none -> 17 us  [move(): return lax.ppermute(x, axis, [(i, i ^ bit) for i in range(size)])]
    pallas_call x0 -> x3, Pallas kernels: none -> 16.2 us  [call(): pl.pallas_call(functools.partial(with_fetches, kernel, kinds, ks, len(out...]
    all_to_all x2 -> x0, waiting for transfers between devices: 13.9 us -> none  [the longest x1 13.9 us: body(): lax.all_to_all(outgoing, 'graph', split_axis=0, concat_axis=0, tiled=True)]
    psum x1 -> x0, blocking collectives: 12.1 us -> none  [body(): totals = lax.psum((grad_src, grad_edge, grad_out, grad_g), 'graph')]
  transfers between devices with their start and end apart: 5 -> 14, of which waited for: 4 -> 7; matrix products, arithmetic and copies ran while one was open for 14% -> 0% of each run, Pallas kernels for 0% -> 22%
where the time goes in v1:
time: 46.8 us; the launch traced here: 47.1 us
  starting transfers between devices  17 us (36%)
  Pallas kernels  16.2 us (35%)
  waiting for transfers between devices  9.84 us (21%)
  local copies, waits for them, and re-layouts  3.07 us (7%)
  between operations  0.89 us (2%)
    ppermute x14, starting transfers between devices, move(): return lax.ppermute(x, axis, [(i, i ^ bit) for i in range(size)])  17 us
    pallas_call x3, Pallas kernels, call(): pl.pallas_call(functools.partial(with_fetches, kernel, kinds, ks, len(out...  16.2 us
    ppermute x14, waiting for transfers between devices, move(): return lax.ppermute(x, axis, [(i, i ^ bit) for i in range(size)])  9.84 us
    unnamed x26, local copies, waits for them, and re-layouts  1.82 us
  transfers between devices with their start and end apart: 14, of which 7 were waited for; matrix products, arithmetic and copies ran while one was open for 0% of the time, Pallas kernels for 22%

profile of v1, /device:TPU:0, one launch (start us, length us, event | category | flops | bytes accessed | tf_op | source)
XLA Modules:
  0.0 47.1 jit_solution(17894309107882596051)
XLA Ops:
  0.6 0.5 %collective-permute-start.2 = (bf16[1024,128]{1,0:T(8,128)(2,1)}, bf16[1024,128]{1,0:T(8,128)(2,1)S(1)}, u32[]{:S(2)}, u32[]{:S(2)}) collective-permute-start(bf16[1024,128]{1,0:T(8,128)(2,1)} %bitcast.56), channel_id=1, source_target_pairs={{0,1},{1,0},{2,3},{3,2},{4,5},{5,4},{6,7},{7,6},{8,9},{9,8},{10,11... | collective-permute-start | bytes 786440 | tf_op jit(solution)/shard_map/ppermute | solution.py:266
  1.2 2.6 %collective-permute-start.1 = (s32[4,2048]{1,0:T(4,128)}, s32[4,2048]{1,0:T(4,128)S(1)}, u32[]{:S(2)}, u32[]{:S(2)}) collective-permute-start(s32[4,2048]{1,0:T(4,128)} %bitcast.76), channel_id=1, source_target_pairs={{0,2},{1,3},{2,0},{3,1},{4,6},{5,7},{6,4},{7,5},{8,10},{9,11},{10,... | collective-permute-start | bytes 98312 | tf_op jit(solution)/shard_map/ppermute | solution.py:266
  3.7 0.2 collective-permute-start.3
  3.9 0.3 collective-permute-start
  4.2 1.8 %collective-permute-done.1.refs_9_ = s32[4,2048]{1,0:T(4,128)S(1)} collective-permute-done((s32[4,2048]{1,0:T(4,128)}, s32[4,2048]{1,0:T(4,128)S(1)}, u32[]{:S(2)}, u32[]{:S(2)}) %collective-permute-start.1) | collective-permute-done | bytes 32800 | tf_op jit(solution)/shard_map/ppermute | solution.py:266
  5.9 0.0 collective-permute-done.3.refs_10_
  5.9 0.0 copy-start.12
  5.9 0.0 collective-permute-done.2.refs_4_
  5.9 0.0 copy-start.11
  5.9 0.6 %copy-done.12 = s32[4,2048]{1,0:T(4,128)} copy-done((s32[4,2048]{1,0:T(4,128)}, s32[4,2048]{1,0:T(4,128)S(1)}, u32[]{:S(2)}) %copy-start.12) | copy-done | bytes 32792
  6.5 0.1 copy-done.11
  6.6 0.0 copy-start
  6.6 0.0 copy-start.2
  6.6 0.0 copy-start.3
  6.6 0.0 copy-start.4
  6.6 0.0 copy-start.5
  6.7 0.0 copy-start.6
  6.7 0.0 copy-start.7
  6.7 0.0 copy-start.8
  6.7 8.5 %near_edges.1 = (f32[640,256]{1,0:T(8,128)}, bf16[2,128,1024]{2,1,0:T(8,128)(2,1)}) custom-call(bf16[1024,128]{1,0:T(8,128)(2,1)} %bitcast.53, f32[1,128]{1,0:T(1,128)} %bitcast.62, bf16[128,128]{1,0:T(8,128)(2,1)} %refs_2_.5, bf16[1024,128]{1,0:T(8,128)(2,1)} %bitcast.58, bf16[1024,128]{1,0:T(8,128)(2,1)} %copy-done.11, bf16[128,128]{1,0:T(8,128)(2,1)} %refs_5_.3, ...), custom_call_target="tpu_custom_call" | custom-call | flops 4294967296 | bytes 1048576 | tf_op jit(solution)/shard_map/near_edges/pallas_call | solution.py:321
  15.2 0.0 collective-permute-done.refs_3_
  15.2 0.1 collective-permute-start.4
  15.2 0.5 %collective-permute-start.5 = (s32[4,2048]{1,0:T(4,128)S(1)}, s32[4,2048]{1,0:T(4,128)S(1)}, u32[]{:S(2)}, u32[]{:S(2)}) collective-permute-start(s32[4,2048]{1,0:T(4,128)S(1)} %collective-permute-done.1.refs_9_), channel_id=1, source_target_pairs={{0,1},{1,0},{2,3},{3,2},{4,5},{5,4},{6,7},{7,6},{8,9},{9,8},{10,11... | collective-permute-start | bytes 98312 | tf_op jit(solution)/shard_map/ppermute | solution.py:266
  15.7 1.1 %collective-permute-done.5.refs_10_ = s32[4,2048]{1,0:T(4,128)S(1)} collective-permute-done((s32[4,2048]{1,0:T(4,128)S(1)}, s32[4,2048]{1,0:T(4,128)S(1)}, u32[]{:S(2)}, u32[]{:S(2)}) %collective-permute-start.5) | collective-permute-done | bytes 32800 | tf_op jit(solution)/shard_map/ppermute | solution.py:266
  16.8 0.0 collective-permute-done.4.refs_4_
  16.8 0.0 copy-done
  16.8 0.0 copy-done.2
  16.8 0.0 copy-done.3
  16.8 0.0 copy-done.4
  16.9 0.0 copy-done.5
  16.9 0.0 copy-done.6
  16.9 0.0 copy-done.7
  16.9 0.0 copy-done.8
  16.9 0.0 copy-start.9
  16.9 1.1 %copy-done.9 = f32[640,256]{1,0:T(8,128)S(1)} copy-done((f32[640,256]{1,0:T(8,128)S(1)}, f32[640,256]{1,0:T(8,128)}, u32[]{:S(2)}) %copy-start.9) | copy-done | bytes 655384
  18.0 0.0 copy-start.10
  18.0 5.7 %far_edges.1 = (bf16[2,128,1024]{2,1,0:T(8,128)(2,1)S(1)}, f32[8,56,128]{2,1,0:T(8,128)S(1)}, f32[128,1024]{1,0:T(8,128)S(1)}) custom-call(bf16[1024,128]{1,0:T(8,128)(2,1)S(1)} %bitcast.54, f32[1,128]{1,0:T(1,128)S(1)} %bitcast.63, bf16[128,128]{1,0:T(8,128)(2,1)S(1)} %copy-done.2, bf16[1024,128]{1,0:T(8,128)(2,1)S(1)} %collective-permute-done.refs_3_, ...), custom_call_target="tpu_custom_call" | custom-call | flops 4294967296 | bytes 1048576 | tf_op jit(solution)/shard_map/far_edges/pallas_call | solution.py:321
  23.7 0.0 copy-start.1
  23.8 0.2 collective-permute-start.7
  24.0 2.0 %collective-permute-start.6 = (f32[4,56,128]{2,1,0:T(8,128)S(1)}, f32[4,56,128]{2,1,0:T(8,128)S(1)}, u32[]{:S(2)}, u32[]{:S(2)}) collective-permute-start(f32[4,56,128]{2,1,0:T(8,128)S(1)} %slice_bitcast_fusion.2), channel_id=1, source_target_pairs={{0,4},{4,0},{8,12},{12,8},{16,20},{20,16},{24,28},{28,24},{1,5},{5... | collective-permute-start | bytes 344072 | tf_op jit(solution)/shard_map/ppermute | solution.py:266
  26.0 0.0 copy-done.10
  26.0 0.1 collective-permute-start.12
  26.2 3.5 %collective-permute-done.6 = f32[4,56,128]{2,1,0:T(8,128)S(1)} collective-permute-done((f32[4,56,128]{2,1,0:T(8,128)S(1)}, f32[4,56,128]{2,1,0:T(8,128)S(1)}, u32[]{:S(2)}, u32[]{:S(2)}) %collective-permute-start.6) | collective-permute-done | bytes 114720 | tf_op jit(solution)/shard_map/ppermute | solution.py:266
  29.7 0.0 collective-permute-done.7
  29.7 1.9 %collective-permute-start.8 = (f32[2,56,128]{2,1,0:T(8,128)S(1)}, f32[2,56,128]{2,1,0:T(8,128)S(1)}, u32[]{:S(2)}, u32[]{:S(2)}) collective-permute-start(f32[2,56,128]{2,1,0:T(8,128)S(1)} %slice_bitcast_fusion.4), channel_id=1, source_target_pairs={{0,8},{4,12},{8,0},{12,4},{16,24},{20,28},{24,16},{28,20},{1,9},{5... | collective-permute-start | bytes 172040 | tf_op jit(solution)/shard_map/ppermute | solution.py:266
  31.6 0.1 fusion
  31.7 1.9 %collective-permute-start.10 = (bf16[128,1024]{1,0:T(8,128)(2,1)S(1)}, bf16[128,1024]{1,0:T(8,128)(2,1)S(1)}, u32[]{:S(2)}, u32[]{:S(2)}) collective-permute-start(bf16[128,1024]{1,0:T(8,128)(2,1)S(1)} %fusion), channel_id=1, source_target_pairs={{0,2},{1,3},{2,0},{3,1},{4,6},{5,7},{6,4},{7,5},{8,10},{9,11},{10,... | collective-permute-start | bytes 786440 | tf_op jit(solution)/shard_map/ppermute | solution.py:266
  33.6 0.4 collective-permute-done.8
  34.0 3.8 %collective-permute-start.9 = (f32[1,56,128]{2,1,0:T(8,128)S(1)}, f32[1,56,128]{2,1,0:T(8,128)S(1)}, u32[]{:S(2)}, u32[]{:S(2)}) collective-permute-start(f32[1,56,128]{2,1,0:T(8,128)S(1)} %slice_bitcast_fusion.6), channel_id=1, source_target_pairs={{0,16},{4,20},{8,24},{12,28},{16,0},{20,4},{24,8},{28,12},{1,17},{... | collective-permute-start | bytes 86024 | tf_op jit(solution)/shard_map/ppermute | solution.py:266
  37.8 1.9 %collective-permute-done.9 = f32[1,56,128]{2,1,0:T(8,128)S(1)} collective-permute-done((f32[1,56,128]{2,1,0:T(8,128)S(1)}, f32[1,56,128]{2,1,0:T(8,128)S(1)}, u32[]{:S(2)}, u32[]{:S(2)}) %collective-permute-start.9) | collective-permute-done | bytes 28704 | tf_op jit(solution)/shard_map/ppermute | solution.py:266
  39.7 0.1 collective-permute-done.10.refs_6_
  39.8 2.8 %collective-permute-start.11 = (f32[56,128]{1,0:T(8,128)S(1)}, f32[56,128]{1,0:T(8,128)S(1)}, u32[]{:S(2)}, u32[]{:S(2)}) collective-permute-start(f32[56,128]{1,0:T(8,128)S(1)} %bitcast.73), channel_id=1, source_target_pairs={{0,2},{1,3},{2,0},{3,1},{4,6},{5,7},{6,4},{7,5},{8,10},{9,11},{10,... | collective-permute-start | bytes 86024 | tf_op jit(solution)/shard_map/ppermute | solution.py:266
  42.6 0.0 collective-permute-done.12
  42.6 0.1 convert_add_fusion.refs_5_
  42.6 0.0 copy-done.1
  42.6 2.0 %atoms.1 = (bf16[1024,128]{1,0:T(8,128)(2,1)}, bf16[1024,128]{1,0:T(8,128)(2,1)}) custom-call(bf16[1024,128]{1,0:T(8,128)(2,1)S(1)} %bitcast.55, f32[1,128]{1,0:T(1,128)S(1)} %bitcast.64, bf16[128,128]{1,0:T(8,128)(2,1)S(1)} %copy-done.2, bf16[1024,128]{1,0:T(8,128)(2,1)S(1)} %bitcast.59, f32[128,1024]{1,0:T(8,128)S(1)} %get-tuple-element.36.refs_4_, ...), custom_call_target="tpu_custom_call" | custom-call | flops 67108864 | bytes 1048576 | tf_op jit(solution)/shard_map/atoms/pallas_call | solution.py:321
  44.6 0.0 collective-permute-done.11
  44.7 0.1 collective-permute-start.13
  44.7 1.2 %collective-permute-done.13 = f32[56,128]{1,0:T(8,128)S(1)} collective-permute-done((f32[56,128]{1,0:T(8,128)S(1)}, f32[56,128]{1,0:T(8,128)S(1)}, u32[]{:S(2)}, u32[]{:S(2)}) %collective-permute-start.13) | collective-permute-done | bytes 28704 | tf_op jit(solution)/shard_map/ppermute | solution.py:266
  45.9 0.6 %fusion.5 = (f32[16,128]{1,0:T(8,128)}, f32[16,128]{1,0:T(8,128)}, f32[16,128]{1,0:T(8,128)}) fusion(f32[56,128]{1,0:T(8,128)S(1)} %add.30), kind=kLoop, calls=%fused_computation.17 | loop fusion | bytes 49152 | tf_op jit(solution)/shard_map/slice | solution.py:403
  46.5 0.6 %dynamic-slice_bitcast_fusion = f32[16]{0:T(128)} fusion(f32[1,128]{1,0:T(1,128)S(1)} %slice.65, s32[]{:T(128)S(6)} %select_n.3), kind=kLoop, calls=%fused_computation.15 | loop fusion | bytes 132 | tf_op jit(solution)/shard_map/dynamic_slice | solution.py:397
  (11 shorter events, 0.1 us)
Async XLA Ops:
  0.6 5.3 %collective-permute-start.2 = (bf16[1024,128]{1,0:T(8,128)(2,1)}, bf16[1024,128]{1,0:T(8,128)(2,1)S(1)}, u32[]{:S(2)}, u32[]{:S(2)}) collective-permute-start(bf16[1024,128]{1,0:T(8,128)(2,1)} %bitcast.56), channel_id=1, source_target_pairs={{0,1},{1,0},{2,3},{3,2},{4,5},{5,4},{6,7},{7,6},{8,9},{9,8},{10,11... | collective-permute-start | bytes 786440 | tf_op jit(solution)/shard_map/ppermute | solution.py:266
  1.2 4.8 %collective-permute-start.1 = (s32[4,2048]{1,0:T(4,128)}, s32[4,2048]{1,0:T(4,128)S(1)}, u32[]{:S(2)}, u32[]{:S(2)}) collective-permute-start(s32[4,2048]{1,0:T(4,128)} %bitcast.76), channel_id=1, source_target_pairs={{0,2},{1,3},{2,0},{3,1},{4,6},{5,7},{6,4},{7,5},{8,10},{9,11},{10,... | collective-permute-start | bytes 98312 | tf_op jit(solution)/shard_map/ppermute | solution.py:266
  3.7 2.2 %collective-permute-start.3 = (s32[4,2048]{1,0:T(4,128)}, s32[4,2048]{1,0:T(4,128)S(1)}, u32[]{:S(2)}, u32[]{:S(2)}) collective-permute-start(s32[4,2048]{1,0:T(4,128)} %bitcast.77), channel_id=1, source_target_pairs={{0,1},{1,0},{2,3},{3,2},{4,5},{5,4},{6,7},{7,6},{8,9},{9,8},{10,11... | collective-permute-start | bytes 98312 | tf_op jit(solution)/shard_map/ppermute | solution.py:266
  3.9 11.3 %collective-permute-start = (bf16[1024,128]{1,0:T(8,128)(2,1)}, bf16[1024,128]{1,0:T(8,128)(2,1)S(1)}, u32[]{:S(2)}, u32[]{:S(2)}) collective-permute-start(bf16[1024,128]{1,0:T(8,128)(2,1)} %bitcast.57), channel_id=1, source_target_pairs={{0,2},{1,3},{2,0},{3,1},{4,6},{5,7},{6,4},{7,5},{8,10},{9,11},{10,... | collective-permute-start | bytes 786440 | tf_op jit(solution)/shard_map/ppermute | solution.py:266
  5.9 0.6 %copy-start.12 = (s32[4,2048]{1,0:T(4,128)}, s32[4,2048]{1,0:T(4,128)S(1)}, u32[]{:S(2)}) copy-start(s32[4,2048]{1,0:T(4,128)S(1)} %collective-permute-done.3.refs_10_) | copy-start | bytes 98308
  5.9 0.7 %copy-start.11 = (bf16[1024,128]{1,0:T(8,128)(2,1)}, bf16[1024,128]{1,0:T(8,128)(2,1)S(1)}, u32[]{:S(2)}) copy-start(bf16[1024,128]{1,0:T(8,128)(2,1)S(1)} %collective-permute-done.2.refs_4_) | copy-start | bytes 786436
  6.6 10.2 %copy-start = (bf16[1,1,1024,128]{3,2,1,0:T(8,128)(2,1)S(1)}, bf16[1,1,1024,128]{3,2,1,0:T(8,128)(2,1)}, u32[]{:S(2)}) copy-start(bf16[1,1,1024,128]{3,2,1,0:T(8,128)(2,1)} %param.10) | copy-start | bytes 786436
  6.6 10.2 %copy-start.2 = (bf16[128,128]{1,0:T(8,128)(2,1)S(1)}, bf16[128,128]{1,0:T(8,128)(2,1)}, u32[]{:S(2)}) copy-start(bf16[128,128]{1,0:T(8,128)(2,1)} %refs_2_.5) | copy-start | bytes 98308
  6.6 10.2 %copy-start.3 = (f32[128]{0:T(128)S(1)}, f32[128]{0:T(128)}, u32[]{:S(2)}) copy-start(f32[128]{0:T(128)} %param.11) | copy-start | bytes 1540
  6.6 10.2 %copy-start.4 = (bf16[1,1,4,2048,128]{4,3,2,1,0:T(8,128)(2,1)S(1)}, bf16[1,1,4,2048,128]{4,3,2,1,0:T(8,128)(2,1)}, u32[]{:S(2)}) copy-start(bf16[1,1,4,2048,128]{4,3,2,1,0:T(8,128)(2,1)} %param.18) | copy-start | bytes 6291460
  6.6 10.2 %copy-start.5 = (bf16[128,128]{1,0:T(8,128)(2,1)S(1)}, bf16[128,128]{1,0:T(8,128)(2,1)}, u32[]{:S(2)}) copy-start(bf16[128,128]{1,0:T(8,128)(2,1)} %refs_5_.3) | copy-start | bytes 98308
  6.7 10.2 %copy-start.6 = (bf16[128,128]{1,0:T(8,128)(2,1)S(1)}, bf16[128,128]{1,0:T(8,128)(2,1)}, u32[]{:S(2)}) copy-start(bf16[128,128]{1,0:T(8,128)(2,1)} %refs_6_.3) | copy-start | bytes 98308
  6.7 10.2 %copy-start.7 = (s32[1,1,4,2048]{3,2,1,0:T(4,128)S(1)}, s32[1,1,4,2048]{3,2,1,0:T(4,128)}, u32[]{:S(2)}) copy-start(s32[1,1,4,2048]{3,2,1,0:T(4,128)} %param.15) | copy-start | bytes 98308
  6.7 10.2 %copy-start.8 = (s32[1,4,4]{2,1,0:T(4,128)S(1)}, s32[1,4,4]{2,1,0:T(4,128)}, u32[]{:S(2)}) copy-start(s32[1,4,4]{2,1,0:T(4,128)} %param.17) | copy-start | bytes 196
  15.2 1.7 %collective-permute-start.4 = (bf16[1024,128]{1,0:T(8,128)(2,1)S(1)}, bf16[1024,128]{1,0:T(8,128)(2,1)S(1)}, u32[]{:S(2)}, u32[]{:S(2)}) collective-permute-start(bf16[1024,128]{1,0:T(8,128)(2,1)S(1)} %collective-permute-done.refs_3_), channel_id=1, source_target_pairs={{0,1},{1,0},{2,3},{3,2},{4,5},{5,4},{6,7},{7,6},{8,9},{9,8},{10,11... | collective-permute-start | bytes 786440 | tf_op jit(solution)/shard_map/ppermute | solution.py:266
  15.2 1.6 %collective-permute-start.5 = (s32[4,2048]{1,0:T(4,128)S(1)}, s32[4,2048]{1,0:T(4,128)S(1)}, u32[]{:S(2)}, u32[]{:S(2)}) collective-permute-start(s32[4,2048]{1,0:T(4,128)S(1)} %collective-permute-done.1.refs_9_), channel_id=1, source_target_pairs={{0,1},{1,0},{2,3},{3,2},{4,5},{5,4},{6,7},{7,6},{8,9},{9,8},{10,11... | collective-permute-start | bytes 98312 | tf_op jit(solution)/shard_map/ppermute | solution.py:266
  16.9 1.1 %copy-start.9 = (f32[640,256]{1,0:T(8,128)S(1)}, f32[640,256]{1,0:T(8,128)}, u32[]{:S(2)}) copy-start(f32[640,256]{1,0:T(8,128)} %get-tuple-element.30.refs_12_) | copy-start | bytes 1966084
  18.0 8.0 %copy-start.10 = (bf16[2,128,1024]{2,1,0:T(8,128)(2,1)S(1)}, bf16[2,128,1024]{2,1,0:T(8,128)(2,1)}, u32[]{:S(2)}) copy-start(bf16[2,128,1024]{2,1,0:T(8,128)(2,1)} %get-tuple-element.37) | copy-start | bytes 1572868
  23.7 18.9 %copy-start.1 = (bf16[1,1,1024,128]{3,2,1,0:T(8,128)(2,1)S(1)}, bf16[1,1,1024,128]{3,2,1,0:T(8,128)(2,1)}, u32[]{:S(2)}) copy-start(bf16[1,1,1024,128]{3,2,1,0:T(8,128)(2,1)} %param.19) | copy-start | bytes 786436
  23.8 6.0 %collective-permute-start.7 = (bf16[128,1024]{1,0:T(8,128)(2,1)S(1)}, bf16[128,1024]{1,0:T(8,128)(2,1)S(1)}, u32[]{:S(2)}, u32[]{:S(2)}) collective-permute-start(bf16[128,1024]{1,0:T(8,128)(2,1)S(1)} %slice_bitcast_fusion.1), channel_id=1, source_target_pairs={{0,1},{1,0},{2,3},{3,2},{4,5},{5,4},{6,7},{7,6},{8,9},{9,8},{10,11... | collective-permute-start | bytes 786440 | tf_op jit(solution)/shard_map/ppermute | solution.py:266
  24.0 5.7 %collective-permute-start.6 = (f32[4,56,128]{2,1,0:T(8,128)S(1)}, f32[4,56,128]{2,1,0:T(8,128)S(1)}, u32[]{:S(2)}, u32[]{:S(2)}) collective-permute-start(f32[4,56,128]{2,1,0:T(8,128)S(1)} %slice_bitcast_fusion.2), channel_id=1, source_target_pairs={{0,4},{4,0},{8,12},{12,8},{16,20},{20,16},{24,28},{28,24},{1,5},{5... | collective-permute-start | bytes 344072 | tf_op jit(solution)/shard_map/ppermute | solution.py:266
  26.0 16.5 %collective-permute-start.12 = (bf16[128,1024]{1,0:T(8,128)(2,1)S(1)}, bf16[128,1024]{1,0:T(8,128)(2,1)S(1)}, u32[]{:S(2)}, u32[]{:S(2)}) collective-permute-start(bf16[128,1024]{1,0:T(8,128)(2,1)S(1)} %slice_bitcast_fusion), channel_id=1, source_target_pairs={{0,1},{1,0},{2,3},{3,2},{4,5},{5,4},{6,7},{7,6},{8,9},{9,8},{10,11... | collective-permute-start | bytes 786440 | tf_op jit(solution)/shard_map/ppermute | solution.py:266
  29.7 4.2 %collective-permute-start.8 = (f32[2,56,128]{2,1,0:T(8,128)S(1)}, f32[2,56,128]{2,1,0:T(8,128)S(1)}, u32[]{:S(2)}, u32[]{:S(2)}) collective-permute-start(f32[2,56,128]{2,1,0:T(8,128)S(1)} %slice_bitcast_fusion.4), channel_id=1, source_target_pairs={{0,8},{4,12},{8,0},{12,4},{16,24},{20,28},{24,16},{28,20},{1,9},{5... | collective-permute-start | bytes 172040 | tf_op jit(solution)/shard_map/ppermute | solution.py:266
  31.7 8.1 %collective-permute-start.10 = (bf16[128,1024]{1,0:T(8,128)(2,1)S(1)}, bf16[128,1024]{1,0:T(8,128)(2,1)S(1)}, u32[]{:S(2)}, u32[]{:S(2)}) collective-permute-start(bf16[128,1024]{1,0:T(8,128)(2,1)S(1)} %fusion), channel_id=1, source_target_pairs={{0,2},{1,3},{2,0},{3,1},{4,6},{5,7},{6,4},{7,5},{8,10},{9,11},{10,... | collective-permute-start | bytes 786440 | tf_op jit(solution)/shard_map/ppermute | solution.py:266
  34.0 5.7 %collective-permute-start.9 = (f32[1,56,128]{2,1,0:T(8,128)S(1)}, f32[1,56,128]{2,1,0:T(8,128)S(1)}, u32[]{:S(2)}, u32[]{:S(2)}) collective-permute-start(f32[1,56,128]{2,1,0:T(8,128)S(1)} %slice_bitcast_fusion.6), channel_id=1, source_target_pairs={{0,16},{4,20},{8,24},{12,28},{16,0},{20,4},{24,8},{28,12},{1,17},{... | collective-permute-start | bytes 86024 | tf_op jit(solution)/shard_map/ppermute | solution.py:266
  39.8 4.8 %collective-permute-start.11 = (f32[56,128]{1,0:T(8,128)S(1)}, f32[56,128]{1,0:T(8,128)S(1)}, u32[]{:S(2)}, u32[]{:S(2)}) collective-permute-start(f32[56,128]{1,0:T(8,128)S(1)} %bitcast.73), channel_id=1, source_target_pairs={{0,2},{1,3},{2,0},{3,1},{4,6},{5,7},{6,4},{7,5},{8,10},{9,11},{10,... | collective-permute-start | bytes 86024 | tf_op jit(solution)/shard_map/ppermute | solution.py:266
  44.7 1.3 %collective-permute-start.13 = (f32[56,128]{1,0:T(8,128)S(1)}, f32[56,128]{1,0:T(8,128)S(1)}, u32[]{:S(2)}, u32[]{:S(2)}) collective-permute-start(f32[56,128]{1,0:T(8,128)S(1)} %bitcast_add_fusion), channel_id=1, source_target_pairs={{0,1},{1,0},{2,3},{3,2},{4,5},{5,4},{6,7},{7,6},{8,9},{9,8},{10,11... | collective-permute-start | bytes 86024 | tf_op jit(solution)/shard_map/ppermute | solution.py:266

commit v2 on v1

--- a/solution.py
+++ b/solution.py
@@ -207,58 +207,61 @@
         out_sum[...] += dot(part, cots[i])
 
 
-def three_sums(sums, chans):
-    tall = sums.shape[0] - chans
-    return sums.at[:tall], sums.at[tall:, :chans], sums.at[tall:, chans:]
-
-
-def near_kernel(ks, *refs):
+def edge_kernel(ks, *refs):
     atoms, gain, *fetched = refs[:10]
-    sums, parts, table, back, agg_sum, hold = refs[10:]
-    sums[...] = jnp.zeros_like(sums)
-    feats, inv = norm_parts(atoms.take()[...])
-    table[...] = stack_groups((feats * inv * column(gain.take())).astype(BF16), back.shape[1] // parts.shape[1])
-    slots_of(ks, fetched, table, back, parts, agg_sum, *three_sums(sums, parts.shape[1]), hold)
-
-
-def far_kernel(ks, *refs):
-    atoms, gain, *fetched = refs[:10]
-    sums, parts, chunks, dnorm_out, table, back, agg_sum, hold = refs[10:]
-    chans = parts.shape[1]
+    parts, chunks, src_sum, table, back, agg_sum, edge_sum, out_sum, hold = refs[10:]
+    chans = edge_sum.shape[0]
     groups = back.shape[1] // chans
+    src_sum[...] = jnp.zeros_like(src_sum)
+    edge_sum[...] = jnp.zeros_like(edge_sum)
+    out_sum[...] = jnp.zeros_like(out_sum)
     feats, inv = norm_parts(atoms.take()[...])
     normed = (feats * inv * column(gain.take())).astype(BF16)
     table[...] = stack_groups(normed, groups)
-    src_sum, edge_sum, out_sum = three_sums(sums.take(), chans)
     slots_of(ks, fetched, table, back, parts, agg_sum, src_sum, edge_sum, out_sum, hold)
-    w_src = fetched[2].take()
     high, low = split(unstack_groups(src_sum[...], groups))
+    normed = unstack_groups(table[...], groups)
     grad_src = dot_nt(normed, high) + dot_nt(normed, low)
-    dnorm = dot(w_src[...], high) + dot(w_src[...], low)
-    dnorm_out[...] = dnorm
-    grad_gain = jnp.sum(dnorm * feats * inv, axis=1, keepdims=True)
-    grad_gain = jnp.broadcast_to(grad_gain, (chans, chans)).T
     grad_edge = edge_sum[...].T
     grad_out = out_sum[...]
     batches = chunks.shape[0]
     rows = chans // batches
+    left = chunks.shape[1] - 3 * rows
     mine = lax.axis_index("dp")
     for j in range(batches):
         place = j ^ mine
         for n, grad in enumerate((grad_src, grad_edge, grad_out)):
             chunks[place, n * rows : (n + 1) * rows, :] = grad[j * rows : (j + 1) * rows, :]
-        chunks[place, 3 * rows :, :] = grad_gain[: chunks.shape[1] - 3 * rows, :]
-
-
-def atom_kernel(ks, atoms, gain, w_out, cot, dnorm, agg_a, agg_b, layer_out, grad_atoms):
+        if left:
+            chunks[place, 3 * rows :, :] = jnp.zeros((left, chans), F32)
+
+
+def atom_kernel(ks, atoms, gain, w_src, w_out, cot, sum_a, sum_b, agg_a, agg_b, layer_out, grad_atoms):
     feats_rows = atoms.take()[...]
     feats, inv = norm_parts(feats_rows)
-    scaled = column(gain.take()) * dnorm.take()[...]
+    groups = feats_rows.shape[0] // GROUP
+    high, low = split(unstack_groups(sum_a.take()[...] + sum_b.take()[...], groups))
+    w_src = w_src.take()[...]
+    scaled = column(gain.take()) * (dot(w_src, high) + dot(w_src, low))
     mean = jnp.mean(feats * scaled, axis=0, keepdims=True)
     rest = inv * scaled - feats * (inv * inv * inv * mean)
     grad_atoms[...] = (cot.take()[...].astype(F32) + rest.T).astype(BF16)
     agg = (agg_a.take()[...].astype(F32) + agg_b.take()[...].astype(F32)).T.astype(BF16)
     layer_out[...] = (feats_rows.astype(F32) + dot(agg, w_out.take()[...])).astype(BF16)
+
+
+def weight_kernel(ks, ours, theirs, w_src, gain, grad_src, grad_edge, grad_out, grad_gain):
+    rows, chans = grad_src.shape
+    total = ours[...] + theirs[...]
+    for n, out in enumerate((grad_src, grad_edge, grad_out)):
+        out[...] = total[n * rows : (n + 1) * rows, :]
+    place = lax.broadcasted_iota(jnp.int32, (rows, chans), 1)
+    row = lax.broadcasted_iota(jnp.int32, (rows, chans), 0)
+    mine = place == row + lax.axis_index("dp") * rows
+    w_rows = dot(jnp.where(mine, 1.0, 0.0).astype(BF16), w_src.take()[...])
+    gains = jnp.sum(jnp.where(mine, gain.take()[...], 0.0), axis=1, keepdims=True)
+    value = jnp.sum(w_rows * total[:rows, :], axis=1, keepdims=True) / gains
+    grad_gain[...] = jnp.sum(jnp.where(place == row, value, 0.0), axis=0, keepdims=True)[:, :rows]
 
 
 def move(x, axis, bit):
@@ -278,7 +281,6 @@
 def body(atoms, gain, w_src, w_edge, w_out, send_src, recv_dst, edge_count, edge_feat, cotangent):
     shards = lax.axis_size("graph")
     batches = lax.axis_size("dp")
-    batch = lax.axis_index("dp")
     atom_count, chans = atoms.shape[2:]
     slots = send_src.shape[3]
     groups = atom_count // GROUP
@@ -293,7 +295,6 @@
     far_dst = move(dst_here, "graph", 2)
     far = move(cot, "graph", 2)
     dst = [dst_here, move(dst_here, "graph", 1)]
-    src, far_dst = lax.optimization_barrier((src, far_dst))
     cots = [cot, move(cot, "graph", 1), far]
 
     vmem = pl.BlockSpec(memory_space=pltpu.VMEM)
@@ -325,13 +326,12 @@
             out_specs=(vmem,) * len(outs),
             scratch_shapes=buffers + scratch,
             compiler_params=pltpu.CompilerParams(vmem_limit_bytes=limit),
-            cost_estimate=pl.CostEstimate(flops=flops, bytes_accessed=1 << 20, transcendentals=0),
+            cost_estimate=pl.CostEstimate(flops=flops, bytes_accessed=min(flops, 1 << 20), transcendentals=0),
             name=name,
         )(*flat)
 
     here = set()
     tall = (groups * chans, GROUP)
-    sums_shape = (groups * chans + chans, GROUP)
     part_shape = (chans, atom_count)
     unit = 2 * slots * atom_count * chans
 
@@ -340,35 +340,43 @@
             pltpu.VMEM(tall, BF16),
             pltpu.VMEM((len(ks),) + tall, BF16),
             pltpu.VMEM((len(ks),) + tall, F32),
+            pltpu.VMEM((chans, chans), F32),
+            pltpu.VMEM((chans, chans), F32),
             pltpu.VMEM((2, chans, BLOCK), BF16),
         ]
 
     near, distant = (0, 1), (2, 3)
-    sums, near_parts = call(
-        near_kernel,
+    rows = chans // batches
+    chunk_rows = -(-3 * rows // 8) * 8
+    outs = [
+        ((2,) + part_shape, BF16),
+        ((batches, chunk_rows, chans), F32),
+        (tall, F32),
+    ]
+    near_parts, near_chunks, near_sum = call(
+        edge_kernel,
         near,
-        [(sums_shape, F32), ((2,) + part_shape, BF16)],
+        outs,
         [feats, gain_row, w_out, cots[:2], w_src, w_edge, counts, src, dst[:2], edges],
         work(near),
         "near_edges",
-        8 * unit,
+        1,
         NEAR_VMEM_BYTES,
     )
-    far, far_dst, sums = lax.optimization_barrier((far, far_dst, sums))
+    far, far_dst, near_chunks = lax.optimization_barrier((far, far_dst, near_chunks))
     dst = dst + [far_dst, move(far_dst, "graph", 1)]
     cots = cots[:2] + [far, move(far, "graph", 1)]
-    rows = chans // batches
-    chunk_rows = -(-(3 * rows + 1) // 8) * 8
-    far_parts, chunks, dnorm = call(
-        far_kernel,
+    far_parts, far_chunks, far_sum = call(
+        edge_kernel,
         distant,
-        [((2,) + part_shape, BF16), ((batches, chunk_rows, chans), F32), ((chans, atom_count), F32)],
-        [feats, gain_row, w_out, cots[2:], w_src, w_edge, counts, src, dst[2:], edges, sums],
+        outs,
+        [feats, gain_row, w_out, cots[2:], w_src, w_edge, counts, src, dst[2:], edges],
         work(distant),
         "far_edges",
         8 * unit,
         FAR_VMEM_BYTES,
     )
+    chunks = near_chunks + far_chunks
 
     given_far = move(far_parts[1], "graph", 1)
     chunks = reduce_batches(chunks, 1)
@@ -385,7 +393,7 @@
         atom_kernel,
         (),
         [(feats.shape, BF16)] * 2,
-        [feats, gain_row, w_out, cot, dnorm, own_part, arrived],
+        [feats, gain_row, w_src, w_out, cot, near_sum, far_sum, own_part, arrived],
         [],
         "atoms",
         unit // 8,
@@ -393,15 +401,23 @@
     )
 
     total, layer_out, grad_atoms = lax.optimization_barrier((total, layer_out, grad_atoms))
-    reduced = total + move(total, "graph", 1)
-    grad_gain = lax.dynamic_slice_in_dim(reduced[3 * rows], batch * rows, rows, 0)
+    theirs = move(total, "graph", 1)
+    here |= {id(total), id(theirs)}
+    grads = call(
+        weight_kernel,
+        (),
+        [((rows, chans), F32)] * 3 + [((1, rows), F32)],
+        [total, theirs, w_src, gain_row],
+        [],
+        "weights",
+        1,
+        FAR_VMEM_BYTES,
+    )
     return (
         layer_out.reshape(atoms.shape),
         grad_atoms.reshape(atoms.shape),
-        reduced[:rows],
-        reduced[rows : 2 * rows],
-        reduced[2 * rows : 3 * rows],
-        grad_gain,
+        *grads[:3],
+        grads[3].reshape(rows),
     )
 
 

time: 46.8 us -> 42.6 us (0.910); the launches traced: 47.1 us -> 42.1 us
  local copies, waits for them, and re-layouts: 3.07 us -> 0.82 us
  waiting for transfers between devices: 9.84 us -> 8.38 us
  Pallas kernels: 16.2 us -> 15.1 us
    ppermute x14, waiting for transfers between devices: 9.84 us -> 8.38 us  [move(): return lax.ppermute(x, axis, [(i, i ^ bit) for i in range(size)])]
    pallas_call x3 -> x4, Pallas kernels: 16.2 us -> 15.1 us  [call(): pl.pallas_call(functools.partial(with_fetches, kernel, kinds, ks, len(out...]
    unnamed x26 -> x28, local copies, waits for them, and re-layouts: 1.82 us -> 0.76 us
    slice x2 -> x0, local copies, waits for them, and re-layouts: 0.61 us -> none  [the longest x1 0.61 us: body(): reduced[2 * rows:3 * rows]]
    dynamic_slice x1 -> x0, local copies, waits for them, and re-layouts: 0.58 us -> none  [body(): lax.dynamic_slice_in_dim(reduced[3 * rows], batch * rows, rows, 0)]
  transfers between devices with their start and end apart: 14 -> 14, of which waited for: 7 -> 7; matrix products, arithmetic and copies ran while one was open for 0% -> 0% of each run, Pallas kernels for 22% -> 21%
where the time goes in v2:
time: 42.6 us; the launch traced here: 42.1 us
  starting transfers between devices  16.7 us (39%)
  Pallas kernels  15.1 us (35%)
  waiting for transfers between devices  8.38 us (20%)
  between operations  0.96 us (2%)
  local copies, waits for them, and re-layouts  0.82 us (2%)
    ppermute x14, starting transfers between devices, move(): return lax.ppermute(x, axis, [(i, i ^ bit) for i in range(size)])  16.7 us
    pallas_call x4, Pallas kernels, call(): pl.pallas_call(functools.partial(with_fetches, kernel, kinds, ks, len(out...  15.1 us
    ppermute x14, waiting for transfers between devices, move(): return lax.ppermute(x, axis, [(i, i ^ bit) for i in range(size)])  8.38 us
  transfers between devices with their start and end apart: 14, of which 7 were waited for; matrix products, arithmetic and copies ran while one was open for 0% of the time, Pallas kernels for 21%

profile of v2, /device:TPU:0, one launch (start us, length us, event | category | flops | bytes accessed | tf_op | source)
XLA Modules:
  0.0 42.1 jit_solution(53314521138537266)
XLA Ops:
  0.6 0.0 copy-start.4
  0.6 0.0 copy-start.5
  0.7 0.0 copy-start.6
  0.7 0.0 copy-start
  0.7 0.0 copy-start.9
  0.7 0.0 copy-start.7
  0.7 0.0 copy-start.8
  0.7 0.0 copy-start.1
  0.7 0.5 %collective-permute-start.2 = (bf16[1024,128]{1,0:T(8,128)(2,1)}, bf16[1024,128]{1,0:T(8,128)(2,1)S(1)}, u32[]{:S(2)}, u32[]{:S(2)}) collective-permute-start(bf16[1024,128]{1,0:T(8,128)(2,1)} %bitcast.59), channel_id=1, source_target_pairs={{0,1},{1,0},{2,3},{3,2},{4,5},{5,4},{6,7},{7,6},{8,9},{9,8},{10,11... | collective-permute-start | bytes 786440 | tf_op jit(solution)/shard_map/ppermute | solution.py:269
  1.2 2.6 %collective-permute-start = (bf16[1024,128]{1,0:T(8,128)(2,1)}, bf16[1024,128]{1,0:T(8,128)(2,1)S(1)}, u32[]{:S(2)}, u32[]{:S(2)}) collective-permute-start(bf16[1024,128]{1,0:T(8,128)(2,1)} %bitcast.60), channel_id=1, source_target_pairs={{0,2},{1,3},{2,0},{3,1},{4,6},{5,7},{6,4},{7,5},{8,10},{9,11},{10,... | collective-permute-start | bytes 786440 | tf_op jit(solution)/shard_map/ppermute | solution.py:269
  3.8 0.2 collective-permute-start.3
  4.0 0.3 collective-permute-start.1
  4.2 1.0 %collective-permute-done.3.refs_10_ = s32[4,2048]{1,0:T(4,128)S(1)} collective-permute-done((s32[4,2048]{1,0:T(4,128)}, s32[4,2048]{1,0:T(4,128)S(1)}, u32[]{:S(2)}, u32[]{:S(2)}) %collective-permute-start.3) | collective-permute-done | bytes 32800 | tf_op jit(solution)/shard_map/ppermute | solution.py:269
  5.2 0.0 copy-start.13
  5.2 0.0 collective-permute-done.2.refs_4_
  5.2 0.0 copy-start.11
  5.2 0.6 %copy-done.13 = s32[4,2048]{1,0:T(4,128)} copy-done((s32[4,2048]{1,0:T(4,128)}, s32[4,2048]{1,0:T(4,128)S(1)}, u32[]{:S(2)}) %copy-start.13) | copy-done | bytes 32792
  5.8 0.1 copy-done.11
  5.9 6.8 %near_edges.1 = (bf16[2,128,1024]{2,1,0:T(8,128)(2,1)}, f32[8,48,128]{2,1,0:T(8,128)}, f32[512,256]{1,0:T(8,128)}) custom-call(bf16[1024,128]{1,0:T(8,128)(2,1)} %bitcast.56, f32[1,128]{1,0:T(1,128)} %bitcast.65, bf16[128,128]{1,0:T(8,128)(2,1)} %refs_3_.1, bf16[1024,128]{1,0:T(8,128)(2,1)} %bitcast.61, bf16[1024,128]{1,0:T(8,128)(2,1)} %copy-done.11, ...), custom_call_target="tpu_custom_call" | custom-call | flops 1 | bytes 1 | tf_op jit(solution)/shard_map/near_edges/pallas_call | solution.py:322
  12.7 0.0 collective-permute-done.1.refs_9_
  12.7 0.0 collective-permute-done.refs_3_
  12.7 0.0 copy-start.12
  12.7 0.0 copy-start.10
  12.7 1.9 %collective-permute-start.4 = (bf16[1024,128]{1,0:T(8,128)(2,1)S(1)}, bf16[1024,128]{1,0:T(8,128)(2,1)S(1)}, u32[]{:S(2)}, u32[]{:S(2)}) collective-permute-start(bf16[1024,128]{1,0:T(8,128)(2,1)S(1)} %collective-permute-done.refs_3_), channel_id=1, source_target_pairs={{0,1},{1,0},{2,3},{3,2},{4,5},{5,4},{6,7},{7,6},{8,9},{9,8},{10,11... | collective-permute-start | bytes 786440 | tf_op jit(solution)/shard_map/ppermute | solution.py:269
  14.6 0.1 collective-permute-start.5
  14.7 1.1 %collective-permute-done.5.refs_10_ = s32[4,2048]{1,0:T(4,128)S(1)} collective-permute-done((s32[4,2048]{1,0:T(4,128)S(1)}, s32[4,2048]{1,0:T(4,128)S(1)}, u32[]{:S(2)}, u32[]{:S(2)}) %collective-permute-start.5) | collective-permute-done | bytes 32800 | tf_op jit(solution)/shard_map/ppermute | solution.py:269
  15.9 0.0 collective-permute-done.4.refs_4_
  15.9 0.0 copy-done.4
  15.9 0.0 copy-done.5
  15.9 0.0 copy-done.6
  15.9 0.0 copy-done
  15.9 0.0 copy-done.9
  15.9 0.0 copy-done.7
  15.9 0.0 copy-done.8
  15.9 0.0 copy-done.1
  15.9 5.3 %far_edges.1 = (bf16[2,128,1024]{2,1,0:T(8,128)(2,1)S(1)}, f32[8,48,128]{2,1,0:T(8,128)S(1)}, f32[512,256]{1,0:T(8,128)S(1)}) custom-call(bf16[1024,128]{1,0:T(8,128)(2,1)S(1)} %bitcast.57, f32[1,128]{1,0:T(1,128)S(1)} %bitcast.66, bf16[128,128]{1,0:T(8,128)(2,1)S(1)} %copy-done.5, bf16[1024,128]{1,0:T(8,128)(2,1)S(1)} %collective-permute-done.refs_3_, ...), custom_call_target="tpu_custom_call" | custom-call | flops 4294967296 | bytes 1048576 | tf_op jit(solution)/shard_map/far_edges/pallas_call | solution.py:322
  21.2 0.0 copy-done.12
  21.2 0.0 copy-start.2
  21.2 0.0 copy-start.3
  21.3 1.8 %collective-permute-start.6 = (f32[4,48,128]{2,1,0:T(8,128)S(1)}, f32[4,48,128]{2,1,0:T(8,128)S(1)}, u32[]{:S(2)}, u32[]{:S(2)}) collective-permute-start(f32[4,48,128]{2,1,0:T(8,128)S(1)} %slice_bitcast_fusion.2), channel_id=1, source_target_pairs={{0,4},{4,0},{8,12},{12,8},{16,20},{20,16},{24,28},{28,24},{1,5},{5... | collective-permute-start | bytes 294920 | tf_op jit(solution)/shard_map/ppermute | solution.py:269
  23.1 0.1 collective-permute-start.7
  23.2 0.0 copy-done.10
  23.2 0.5 %collective-permute-start.12 = (bf16[128,1024]{1,0:T(8,128)(2,1)S(1)}, bf16[128,1024]{1,0:T(8,128)(2,1)S(1)}, u32[]{:S(2)}, u32[]{:S(2)}) collective-permute-start(bf16[128,1024]{1,0:T(8,128)(2,1)S(1)} %slice_bitcast_fusion), channel_id=1, source_target_pairs={{0,1},{1,0},{2,3},{3,2},{4,5},{5,4},{6,7},{7,6},{8,9},{9,8},{10,11... | collective-permute-start | bytes 786440 | tf_op jit(solution)/shard_map/ppermute | solution.py:269
  23.8 2.7 %collective-permute-done.6 = f32[4,48,128]{2,1,0:T(8,128)S(1)} collective-permute-done((f32[4,48,128]{2,1,0:T(8,128)S(1)}, f32[4,48,128]{2,1,0:T(8,128)S(1)}, u32[]{:S(2)}, u32[]{:S(2)}) %collective-permute-start.6) | collective-permute-done | bytes 98336 | tf_op jit(solution)/shard_map/ppermute | solution.py:269
  26.5 0.0 collective-permute-done.7
  26.5 1.6 %collective-permute-start.8 = (f32[2,48,128]{2,1,0:T(8,128)S(1)}, f32[2,48,128]{2,1,0:T(8,128)S(1)}, u32[]{:S(2)}, u32[]{:S(2)}) collective-permute-start(f32[2,48,128]{2,1,0:T(8,128)S(1)} %slice_bitcast_fusion.4), channel_id=1, source_target_pairs={{0,8},{4,12},{8,0},{12,4},{16,24},{20,28},{24,16},{28,20},{1,9},{5... | collective-permute-start | bytes 147464 | tf_op jit(solution)/shard_map/ppermute | solution.py:269
  28.1 0.1 fusion
  28.2 2.3 %collective-permute-start.10 = (bf16[128,1024]{1,0:T(8,128)(2,1)S(1)}, bf16[128,1024]{1,0:T(8,128)(2,1)S(1)}, u32[]{:S(2)}, u32[]{:S(2)}) collective-permute-start(bf16[128,1024]{1,0:T(8,128)(2,1)S(1)} %fusion), channel_id=1, source_target_pairs={{0,2},{1,3},{2,0},{3,1},{4,6},{5,7},{6,4},{7,5},{8,10},{9,11},{10,... | collective-permute-start | bytes 786440 | tf_op jit(solution)/shard_map/ppermute | solution.py:269
  30.5 0.2 collective-permute-done.8
  30.6 2.6 %collective-permute-start.9 = (f32[1,48,128]{2,1,0:T(8,128)S(1)}, f32[1,48,128]{2,1,0:T(8,128)S(1)}, u32[]{:S(2)}, u32[]{:S(2)}) collective-permute-start(f32[1,48,128]{2,1,0:T(8,128)S(1)} %slice_bitcast_fusion.6), channel_id=1, source_target_pairs={{0,16},{4,20},{8,24},{12,28},{16,0},{20,4},{24,8},{28,12},{1,17},{... | collective-permute-start | bytes 73736 | tf_op jit(solution)/shard_map/ppermute | solution.py:269
  33.3 2.1 %collective-permute-done.9 = f32[1,48,128]{2,1,0:T(8,128)S(1)} collective-permute-done((f32[1,48,128]{2,1,0:T(8,128)S(1)}, f32[1,48,128]{2,1,0:T(8,128)S(1)}, u32[]{:S(2)}, u32[]{:S(2)}) %collective-permute-start.9) | collective-permute-done | bytes 24608 | tf_op jit(solution)/shard_map/ppermute | solution.py:269
  35.4 0.1 collective-permute-done.10.refs_8_
  35.5 2.2 %collective-permute-start.11 = (f32[48,128]{1,0:T(8,128)S(1)}, f32[48,128]{1,0:T(8,128)S(1)}, u32[]{:S(2)}, u32[]{:S(2)}) collective-permute-start(f32[48,128]{1,0:T(8,128)S(1)} %bitcast.75), channel_id=1, source_target_pairs={{0,2},{1,3},{2,0},{3,1},{4,6},{5,7},{6,4},{7,5},{8,10},{9,11},{10,... | collective-permute-start | bytes 73736 | tf_op jit(solution)/shard_map/ppermute | solution.py:269
  37.7 0.0 collective-permute-done.12
  37.7 0.1 convert_add_fusion.refs_7_
  37.8 0.0 copy-done.2
  37.8 0.0 copy-done.3
  37.8 2.3 %atoms.1 = (bf16[1024,128]{1,0:T(8,128)(2,1)}, bf16[1024,128]{1,0:T(8,128)(2,1)}) custom-call(bf16[1024,128]{1,0:T(8,128)(2,1)S(1)} %bitcast.58, f32[1,128]{1,0:T(1,128)S(1)} %bitcast.67, bf16[128,128]{1,0:T(8,128)(2,1)S(1)} %copy-done.4, bf16[128,128]{1,0:T(8,128)(2,1)S(1)} %copy-done.5, bf16[1024,128]{1,0:T(8,128)(2,1)S(1)} %bitcast.62, ...), custom_call_target="tpu_custom_call" | custom-call | flops 67108864 | bytes 1048576 | tf_op jit(solution)/shard_map/atoms/pallas_call | solution.py:322
  40.1 0.0 collective-permute-done.11
  40.1 0.1 collective-permute-start.13
  40.2 1.2 %collective-permute-done.13.refs_1_ = f32[48,128]{1,0:T(8,128)S(1)} collective-permute-done((f32[48,128]{1,0:T(8,128)S(1)}, f32[48,128]{1,0:T(8,128)S(1)}, u32[]{:S(2)}, u32[]{:S(2)}) %collective-permute-start.13) | collective-permute-done | bytes 24608 | tf_op jit(solution)/shard_map/ppermute | solution.py:269
  41.4 0.8 %weights.1 = (f32[16,128]{1,0:T(8,128)}, f32[16,128]{1,0:T(8,128)}, f32[16,128]{1,0:T(8,128)}, f32[1,16]{1,0:T(1,128)}) custom-call(f32[48,128]{1,0:T(8,128)S(1)} %bitcast_add_fusion.refs_0_, f32[48,128]{1,0:T(8,128)S(1)} %collective-permute-done.13.refs_1_, bf16[128,128]{1,0:T(8,128)(2,1)S(1)} %copy-done.4, f32[1,128]{1,0:T(1,128)S(1)} %bitcast.68), custom_call_target="tpu_custom_call" | custom-call | flops 1 | bytes 1 | tf_op jit(solution)/shard_map/weights/pallas_call | solution.py:322
  (10 shorter events, 0.1 us)
Async XLA Ops:
  0.6 15.2 %copy-start.4 = (bf16[128,128]{1,0:T(8,128)(2,1)S(1)}, bf16[128,128]{1,0:T(8,128)(2,1)}, u32[]{:S(2)}) copy-start(bf16[128,128]{1,0:T(8,128)(2,1)} %refs_2_.7) | copy-start | bytes 98308
  0.6 15.2 %copy-start.5 = (bf16[128,128]{1,0:T(8,128)(2,1)S(1)}, bf16[128,128]{1,0:T(8,128)(2,1)}, u32[]{:S(2)}) copy-start(bf16[128,128]{1,0:T(8,128)(2,1)} %refs_3_.1) | copy-start | bytes 98308
  0.7 15.2 %copy-start.6 = (bf16[128,128]{1,0:T(8,128)(2,1)S(1)}, bf16[128,128]{1,0:T(8,128)(2,1)}, u32[]{:S(2)}) copy-start(bf16[128,128]{1,0:T(8,128)(2,1)} %refs_6_.3) | copy-start | bytes 98308
  0.7 15.2 %copy-start = (bf16[1,1,4,2048,128]{4,3,2,1,0:T(8,128)(2,1)S(1)}, bf16[1,1,4,2048,128]{4,3,2,1,0:T(8,128)(2,1)}, u32[]{:S(2)}) copy-start(bf16[1,1,4,2048,128]{4,3,2,1,0:T(8,128)(2,1)} %param.18) | copy-start | bytes 6291460
  0.7 15.2 %copy-start.9 = (s32[1,4,4]{2,1,0:T(4,128)S(1)}, s32[1,4,4]{2,1,0:T(4,128)}, u32[]{:S(2)}) copy-start(s32[1,4,4]{2,1,0:T(4,128)} %param.17) | copy-start | bytes 196
  0.7 15.2 %copy-start.7 = (s32[1,1,4,2048]{3,2,1,0:T(4,128)S(1)}, s32[1,1,4,2048]{3,2,1,0:T(4,128)}, u32[]{:S(2)}) copy-start(s32[1,1,4,2048]{3,2,1,0:T(4,128)} %param.15) | copy-start | bytes 98308
  0.7 15.2 %copy-start.8 = (f32[128]{0:T(128)S(1)}, f32[128]{0:T(128)}, u32[]{:S(2)}) copy-start(f32[128]{0:T(128)} %param.11) | copy-start | bytes 1540
  0.7 15.2 %copy-start.1 = (bf16[1,1,1024,128]{3,2,1,0:T(8,128)(2,1)S(1)}, bf16[1,1,1024,128]{3,2,1,0:T(8,128)(2,1)}, u32[]{:S(2)}) copy-start(bf16[1,1,1024,128]{3,2,1,0:T(8,128)(2,1)} %param.10) | copy-start | bytes 786436
  0.7 4.5 %collective-permute-start.2 = (bf16[1024,128]{1,0:T(8,128)(2,1)}, bf16[1024,128]{1,0:T(8,128)(2,1)S(1)}, u32[]{:S(2)}, u32[]{:S(2)}) collective-permute-start(bf16[1024,128]{1,0:T(8,128)(2,1)} %bitcast.59), channel_id=1, source_target_pairs={{0,1},{1,0},{2,3},{3,2},{4,5},{5,4},{6,7},{7,6},{8,9},{9,8},{10,11... | collective-permute-start | bytes 786440 | tf_op jit(solution)/shard_map/ppermute | solution.py:269
  1.2 11.5 %collective-permute-start = (bf16[1024,128]{1,0:T(8,128)(2,1)}, bf16[1024,128]{1,0:T(8,128)(2,1)S(1)}, u32[]{:S(2)}, u32[]{:S(2)}) collective-permute-start(bf16[1024,128]{1,0:T(8,128)(2,1)} %bitcast.60), channel_id=1, source_target_pairs={{0,2},{1,3},{2,0},{3,1},{4,6},{5,7},{6,4},{7,5},{8,10},{9,11},{10,... | collective-permute-start | bytes 786440 | tf_op jit(solution)/shard_map/ppermute | solution.py:269
  3.8 1.4 %collective-permute-start.3 = (s32[4,2048]{1,0:T(4,128)}, s32[4,2048]{1,0:T(4,128)S(1)}, u32[]{:S(2)}, u32[]{:S(2)}) collective-permute-start(s32[4,2048]{1,0:T(4,128)} %bitcast.76), channel_id=1, source_target_pairs={{0,1},{1,0},{2,3},{3,2},{4,5},{5,4},{6,7},{7,6},{8,9},{9,8},{10,11... | collective-permute-start | bytes 98312 | tf_op jit(solution)/shard_map/ppermute | solution.py:269
  4.0 8.7 %collective-permute-start.1 = (s32[4,2048]{1,0:T(4,128)}, s32[4,2048]{1,0:T(4,128)S(1)}, u32[]{:S(2)}, u32[]{:S(2)}) collective-permute-start(s32[4,2048]{1,0:T(4,128)} %bitcast.77), channel_id=1, source_target_pairs={{0,2},{1,3},{2,0},{3,1},{4,6},{5,7},{6,4},{7,5},{8,10},{9,11},{10,... | collective-permute-start | bytes 98312 | tf_op jit(solution)/shard_map/ppermute | solution.py:269
  5.2 0.6 %copy-start.13 = (s32[4,2048]{1,0:T(4,128)}, s32[4,2048]{1,0:T(4,128)S(1)}, u32[]{:S(2)}) copy-start(s32[4,2048]{1,0:T(4,128)S(1)} %collective-permute-done.3.refs_10_) | copy-start | bytes 98308
  5.2 0.7 %copy-start.11 = (bf16[1024,128]{1,0:T(8,128)(2,1)}, bf16[1024,128]{1,0:T(8,128)(2,1)S(1)}, u32[]{:S(2)}) copy-start(bf16[1024,128]{1,0:T(8,128)(2,1)S(1)} %collective-permute-done.2.refs_4_) | copy-start | bytes 786436
  12.7 8.5 %copy-start.12 = (f32[8,48,128]{2,1,0:T(8,128)S(1)}, f32[8,48,128]{2,1,0:T(8,128)}, u32[]{:S(2)}) copy-start(f32[8,48,128]{2,1,0:T(8,128)} %get-tuple-element.29) | copy-start | bytes 589828
  12.7 10.4 %copy-start.10 = (bf16[2,128,1024]{2,1,0:T(8,128)(2,1)S(1)}, bf16[2,128,1024]{2,1,0:T(8,128)(2,1)}, u32[]{:S(2)}) copy-start(bf16[2,128,1024]{2,1,0:T(8,128)(2,1)} %get-tuple-element.39) | copy-start | bytes 1572868
  12.7 3.1 %collective-permute-start.4 = (bf16[1024,128]{1,0:T(8,128)(2,1)S(1)}, bf16[1024,128]{1,0:T(8,128)(2,1)S(1)}, u32[]{:S(2)}, u32[]{:S(2)}) collective-permute-start(bf16[1024,128]{1,0:T(8,128)(2,1)S(1)} %collective-permute-done.refs_3_), channel_id=1, source_target_pairs={{0,1},{1,0},{2,3},{3,2},{4,5},{5,4},{6,7},{7,6},{8,9},{9,8},{10,11... | collective-permute-start | bytes 786440 | tf_op jit(solution)/shard_map/ppermute | solution.py:269
  14.6 1.2 %collective-permute-start.5 = (s32[4,2048]{1,0:T(4,128)S(1)}, s32[4,2048]{1,0:T(4,128)S(1)}, u32[]{:S(2)}, u32[]{:S(2)}) collective-permute-start(s32[4,2048]{1,0:T(4,128)S(1)} %collective-permute-done.1.refs_9_), channel_id=1, source_target_pairs={{0,1},{1,0},{2,3},{3,2},{4,5},{5,4},{6,7},{7,6},{8,9},{9,8},{10,11... | collective-permute-start | bytes 98312 | tf_op jit(solution)/shard_map/ppermute | solution.py:269
  21.2 16.5 %copy-start.2 = (bf16[1,1,1024,128]{3,2,1,0:T(8,128)(2,1)S(1)}, bf16[1,1,1024,128]{3,2,1,0:T(8,128)(2,1)}, u32[]{:S(2)}) copy-start(bf16[1,1,1024,128]{3,2,1,0:T(8,128)(2,1)} %param.19) | copy-start | bytes 786436
  21.2 16.5 %copy-start.3 = (f32[512,256]{1,0:T(8,128)S(1)}, f32[512,256]{1,0:T(8,128)}, u32[]{:S(2)}) copy-start(f32[512,256]{1,0:T(8,128)} %get-tuple-element.37.refs_5_) | copy-start | bytes 1572868
  21.3 5.1 %collective-permute-start.6 = (f32[4,48,128]{2,1,0:T(8,128)S(1)}, f32[4,48,128]{2,1,0:T(8,128)S(1)}, u32[]{:S(2)}, u32[]{:S(2)}) collective-permute-start(f32[4,48,128]{2,1,0:T(8,128)S(1)} %slice_bitcast_fusion.2), channel_id=1, source_target_pairs={{0,4},{4,0},{8,12},{12,8},{16,20},{20,16},{24,28},{28,24},{1,5},{5... | collective-permute-start | bytes 294920 | tf_op jit(solution)/shard_map/ppermute | solution.py:269
  23.1 3.4 %collective-permute-start.7 = (bf16[128,1024]{1,0:T(8,128)(2,1)S(1)}, bf16[128,1024]{1,0:T(8,128)(2,1)S(1)}, u32[]{:S(2)}, u32[]{:S(2)}) collective-permute-start(bf16[128,1024]{1,0:T(8,128)(2,1)S(1)} %slice_bitcast_fusion.1), channel_id=1, source_target_pairs={{0,1},{1,0},{2,3},{3,2},{4,5},{5,4},{6,7},{7,6},{8,9},{9,8},{10,11... | collective-permute-start | bytes 786440 | tf_op jit(solution)/shard_map/ppermute | solution.py:269
  23.2 14.5 %collective-permute-start.12 = (bf16[128,1024]{1,0:T(8,128)(2,1)S(1)}, bf16[128,1024]{1,0:T(8,128)(2,1)S(1)}, u32[]{:S(2)}, u32[]{:S(2)}) collective-permute-start(bf16[128,1024]{1,0:T(8,128)(2,1)S(1)} %slice_bitcast_fusion), channel_id=1, source_target_pairs={{0,1},{1,0},{2,3},{3,2},{4,5},{5,4},{6,7},{7,6},{8,9},{9,8},{10,11... | collective-permute-start | bytes 786440 | tf_op jit(solution)/shard_map/ppermute | solution.py:269
  26.5 4.2 %collective-permute-start.8 = (f32[2,48,128]{2,1,0:T(8,128)S(1)}, f32[2,48,128]{2,1,0:T(8,128)S(1)}, u32[]{:S(2)}, u32[]{:S(2)}) collective-permute-start(f32[2,48,128]{2,1,0:T(8,128)S(1)} %slice_bitcast_fusion.4), channel_id=1, source_target_pairs={{0,8},{4,12},{8,0},{12,4},{16,24},{20,28},{24,16},{28,20},{1,9},{5... | collective-permute-start | bytes 147464 | tf_op jit(solution)/shard_map/ppermute | solution.py:269
  28.2 7.3 %collective-permute-start.10 = (bf16[128,1024]{1,0:T(8,128)(2,1)S(1)}, bf16[128,1024]{1,0:T(8,128)(2,1)S(1)}, u32[]{:S(2)}, u32[]{:S(2)}) collective-permute-start(bf16[128,1024]{1,0:T(8,128)(2,1)S(1)} %fusion), channel_id=1, source_target_pairs={{0,2},{1,3},{2,0},{3,1},{4,6},{5,7},{6,4},{7,5},{8,10},{9,11},{10,... | collective-permute-start | bytes 786440 | tf_op jit(solution)/shard_map/ppermute | solution.py:269
  30.6 4.8 %collective-permute-start.9 = (f32[1,48,128]{2,1,0:T(8,128)S(1)}, f32[1,48,128]{2,1,0:T(8,128)S(1)}, u32[]{:S(2)}, u32[]{:S(2)}) collective-permute-start(f32[1,48,128]{2,1,0:T(8,128)S(1)} %slice_bitcast_fusion.6), channel_id=1, source_target_pairs={{0,16},{4,20},{8,24},{12,28},{16,0},{20,4},{24,8},{28,12},{1,17},{... | collective-permute-start | bytes 73736 | tf_op jit(solution)/shard_map/ppermute | solution.py:269
  35.5 4.6 %collective-permute-start.11 = (f32[48,128]{1,0:T(8,128)S(1)}, f32[48,128]{1,0:T(8,128)S(1)}, u32[]{:S(2)}, u32[]{:S(2)}) collective-permute-start(f32[48,128]{1,0:T(8,128)S(1)} %bitcast.75), channel_id=1, source_target_pairs={{0,2},{1,3},{2,0},{3,1},{4,6},{5,7},{6,4},{7,5},{8,10},{9,11},{10,... | collective-permute-start | bytes 73736 | tf_op jit(solution)/shard_map/ppermute | solution.py:269
  40.1 1.3 %collective-permute-start.13 = (f32[48,128]{1,0:T(8,128)S(1)}, f32[48,128]{1,0:T(8,128)S(1)}, u32[]{:S(2)}, u32[]{:S(2)}) collective-permute-start(f32[48,128]{1,0:T(8,128)S(1)} %bitcast_add_fusion.refs_0_), channel_id=1, source_target_pairs={{0,1},{1,0},{2,3},{3,2},{4,5},{5,4},{6,7},{7,6},{8,9},{9,8},{10,11... | collective-permute-start | bytes 73736 | tf_op jit(solution)/shard_map/ppermute | solution.py:269

commit v3 on v2

--- a/solution.py
+++ b/solution.py
@@ -93,9 +93,17 @@
         return self.held
 
 
+class Held:
+    def __init__(self, held):
+        self.held = held
+
+    def take(self):
+        return self.held
+
+
 def with_fetches(kernel, kinds, ks, outs, *refs):
     refs = list(refs)
-    count = sum(len(ks) if kind == "many" else 1 for kind in kinds)
+    count = sum(len(ks) if kind in ("many", "each") else 1 for kind in kinds)
     ins, refs = refs[:count], refs[count:]
     results, refs = refs[:outs], refs[outs:]
     given = []
@@ -106,29 +114,28 @@
             held, sems = refs.pop(0), refs.pop(0)
             sources = [ref] + [next(ins) for _ in ks[1:]]
             given.append(Many([(x, held.at[i], sems.at[i]) for i, x in enumerate(sources)], held))
+        elif kind == "each":
+            given.append(Held([ref] + [next(ins) for _ in ks[1:]]))
         elif kind == "edges":
             held, sems = refs.pop(0), refs.pop(0)
             given.append(Many([(ref.at[peer_of(k)], held.at[i], sems.at[i]) for i, k in enumerate(ks)], held))
         elif kind == "copy":
             given.append(Fetched(ref, refs.pop(0), refs.pop(0)))
         else:
-            given.append(ref)
+            given.append(Held(ref))
     kernel(ks, *given, *results, *refs)
 
 
 def back_table(w_out, cot, groups):
-    back_t = (dot_nt(w_out[...], cot[...]) * (1.0 / DEG_NORM)).astype(BF16)
+    back_t = (dot_nt(w_out[...], cot) * (1.0 / DEG_NORM)).astype(BF16)
     return stack_groups(back_t, groups)
 
 
-def run_blocks(ks, counts, src, dsts, edges, table, back, w_src_t, w_edge_t, agg_sum, src_sum, edge_sum, hold):
-    groups = back.shape[1] // edge_sum.shape[0]
-    me = lax.axis_index("graph")
-    sizes = [counts[me, peer_of(k)] for k in ks]
+def block_finder(ks, counts):
+    sizes = [counts[lax.axis_index("graph"), peer_of(k)] for k in ks]
     firsts = [0]
     for size in sizes:
         firsts.append(firsts[-1] + (size + BLOCK - 1) // BLOCK)
-    total = firsts[-1]
 
     def locate(item):
         i = jnp.int32(0)
@@ -142,105 +149,136 @@
             peer = jnp.where(past, peer_of(ks[j]), peer)
             size = jnp.where(past, sizes[j], size)
         start = pl.multiple_of((item - first) * BLOCK, BLOCK)
-        span = pl.ds(start, BLOCK)
         live = lax.broadcasted_iota(jnp.int32, (1, BLOCK), 1) + start < size
-        s = src[pl.ds(peer, 1), span]
-        d = dsts[i, pl.ds(me, 1), span]
-        s_low = jnp.where(live, s % GROUP, -1)
-        d_low = jnp.where(live, d % GROUP, -1)
-        return i, span, s_low, s // GROUP, d_low, d // GROUP
+        return i, peer, pl.ds(start, BLOCK), live
+
+    return firsts[-1], locate
+
+
+def low_high(index, live):
+    return jnp.where(live, index % GROUP, -1), index // GROUP
+
+
+def edge_kernel(
+    ks,
+    atoms,
+    gain,
+    w_out,
+    cots,
+    w_src,
+    w_edge,
+    counts,
+    src,
+    dsts,
+    edges,
+    parts,
+    chunks,
+    dpres,
+    table,
+    back,
+    agg_sum,
+    row_sum,
+    edge_sum,
+    hold,
+):
+    chans = edge_sum.shape[0]
+    groups = back.shape[1] // chans
+    agg_sum[...] = jnp.zeros_like(agg_sum)
+    row_sum[...] = jnp.zeros_like(row_sum)
+    edge_sum[...] = jnp.zeros_like(edge_sum)
+    atoms, gain, w_out, cots = atoms.take(), gain.take(), w_out.take(), cots.take()
+    cots = [cots[i][...] for i in range(len(ks))]
+    w_src_t, w_edge_t = w_src.take()[...].T, w_edge.take()[...].T
+    feats, inv = norm_parts(atoms[...])
+    table[...] = stack_groups((feats * inv * column(gain)).astype(BF16), groups)
+    for i in range(len(ks)):
+        back[i] = back_table(w_out, cots[i], groups)
+    counts, src, dsts, edges = counts.take(), src.take(), dsts.take(), edges.take()
+    whole = edges.shape[0] != len(ks)
+    me = lax.axis_index("graph")
+    total, locate = block_finder(ks, counts)
 
     def gather(item):
-        i, span, s_low, s_high, d_low, d_high = locate(item)
+        i, peer, span, live = locate(item)
+        s_low, s_high = low_high(src[pl.ds(peer, 1), span], live)
+        d_low, d_high = low_high(dsts[i, pl.ds(me, 1), span], live)
         rows = choose(dot(table[...], one_hot(s_low)), s_high, groups).astype(BF16)
-        pre = dot(w_src_t, rows) + dot_nt(w_edge_t, edges[i, span, :])
+        pre = dot(w_src_t, rows) + dot_nt(w_edge_t, edges[peer if whole else i, span, :])
         slot_back = choose(dot(back[i], one_hot(d_low)), d_high, groups)
         sig = 0.5 * jnp.tanh(0.5 * pre) + 0.5
         act = pre * sig
         slope = sig + act - act * sig
-        return act.astype(BF16), (slot_back * slope).astype(BF16)
-
-    def scatter(item, msg, dpre):
-        i, span, s_low, s_high, d_low, d_high = locate(item)
+        return rows, act.astype(BF16), (slot_back * slope).astype(BF16)
+
+    def add_up(item, rows, msg):
+        i, peer, span, live = locate(item)
+        d_low, d_high = low_high(dsts[i, pl.ds(me, 1), span], live)
+        dpre = dpres[i, :, span]
         agg_sum[i] += dot_nt(spread(msg, d_high, groups), one_hot(d_low))
-        edge_sum[...] += dot(dpre, edges[i, span, :])
-        src_sum[...] += dot_nt(spread(dpre, s_high, groups), one_hot(s_low))
+        edge_sum[...] += dot(dpre, edges[peer if whole else i, span, :])
+        row_sum[...] += dot_nt(rows, dpre)
+
+    def put(item, rows, msg, dpre):
+        i, _, span, _ = locate(item)
+        hold[0] = rows
+        hold[1] = msg
+        dpres[i, :, span] = dpre
 
     def step(item, carry):
-        msg, dpre = hold[0], hold[1]
-        next_msg, next_dpre = gather(item)
-        scatter(item - 1, msg, dpre)
-        hold[0] = next_msg
-        hold[1] = next_dpre
+        rows, msg = hold[0], hold[1]
+        fresh = gather(item)
+        add_up(item - 1, rows, msg)
+        put(item, *fresh)
         return carry
 
     @pl.when(total > 0)
     def _():
-        msg, dpre = gather(0)
-        hold[0] = msg
-        hold[1] = dpre
+        put(0, *gather(0))
 
     lax.fori_loop(1, total, step, 0)
 
     @pl.when(total > 0)
     def _():
-        scatter(total - 1, hold[0], hold[1])
-
-
-def slots_of(ks, refs, table, back, parts, agg_sum, src_sum, edge_sum, out_sum, hold):
-    w_out, cots, w_src, w_edge, counts, src, dsts, edges = refs
-    groups = back.shape[1] // edge_sum.shape[0]
-    w_out = w_out.take()
-    cots = cots.take()
-    for i in range(len(ks)):
-        back[i] = back_table(w_out, cots.at[i], groups)
-    agg_sum[...] = jnp.zeros_like(agg_sum)
-    w_src_t, w_edge_t = w_src.take()[...].T, w_edge.take()[...].T
-    counts, src = counts.take(), src.take()
-    dsts, edges = dsts.take(), edges.take()
-    run_blocks(
-        ks, counts, src, dsts, edges, table, back, w_src_t, w_edge_t, agg_sum, src_sum, edge_sum, hold
-    )
+        add_up(total - 1, hold[0], hold[1])
+
+    grad_out = jnp.zeros((chans, chans), F32)
     for i in range(len(ks)):
         part = (unstack_groups(agg_sum[i], groups) * (1.0 / DEG_NORM)).astype(BF16)
         parts[i] = part
-        out_sum[...] += dot(part, cots[i])
-
-
-def edge_kernel(ks, *refs):
-    atoms, gain, *fetched = refs[:10]
-    parts, chunks, src_sum, table, back, agg_sum, edge_sum, out_sum, hold = refs[10:]
-    chans = edge_sum.shape[0]
-    groups = back.shape[1] // chans
-    src_sum[...] = jnp.zeros_like(src_sum)
-    edge_sum[...] = jnp.zeros_like(edge_sum)
-    out_sum[...] = jnp.zeros_like(out_sum)
-    feats, inv = norm_parts(atoms.take()[...])
-    normed = (feats * inv * column(gain.take())).astype(BF16)
-    table[...] = stack_groups(normed, groups)
-    slots_of(ks, fetched, table, back, parts, agg_sum, src_sum, edge_sum, out_sum, hold)
-    high, low = split(unstack_groups(src_sum[...], groups))
-    normed = unstack_groups(table[...], groups)
-    grad_src = dot_nt(normed, high) + dot_nt(normed, low)
-    grad_edge = edge_sum[...].T
-    grad_out = out_sum[...]
+        grad_out = grad_out + dot(part, cots[i])
     batches = chunks.shape[0]
     rows = chans // batches
     left = chunks.shape[1] - 3 * rows
     mine = lax.axis_index("dp")
-    for j in range(batches):
-        place = j ^ mine
-        for n, grad in enumerate((grad_src, grad_edge, grad_out)):
-            chunks[place, n * rows : (n + 1) * rows, :] = grad[j * rows : (j + 1) * rows, :]
-        if left:
-            chunks[place, 3 * rows :, :] = jnp.zeros((left, chans), F32)
-
-
-def atom_kernel(ks, atoms, gain, w_src, w_out, cot, sum_a, sum_b, agg_a, agg_b, layer_out, grad_atoms):
+    for n, grad in enumerate((row_sum[...], edge_sum[...].T, grad_out)):
+        for j in range(batches):
+            chunks[j ^ mine, n * rows : (n + 1) * rows, :] = grad[j * rows : (j + 1) * rows, :]
+    if left:
+        for j in range(batches):
+            chunks[j, 3 * rows :, :] = jnp.zeros((left, chans), F32)
+
+
+def source_kernel(ks, counts, src, dpres, *refs):
+    *before, src_sum = refs
+    groups = src_sum.shape[0] // dpres.held.shape[1]
+    src_sum[...] = before[0].take()[...] if before else jnp.zeros_like(src_sum)
+    counts, src, dpres = counts.take(), src.take(), dpres.take()
+    total, locate = block_finder(ks, counts)
+
+    def step(item, carry):
+        i, peer, span, live = locate(item)
+        s_low, s_high = low_high(src[pl.ds(peer, 1), span], live)
+        src_sum[...] += dot_nt(spread(dpres[i, :, span], s_high, groups), one_hot(s_low))
+        return carry
+
+    lax.fori_loop(0, total, step, 0)
+
+
+def atom_kernel(ks, atoms, gain, w_src, w_out, cot, src_sum, agg_a, agg_b, layer_out, grad_atoms):
     feats_rows = atoms.take()[...]
     feats, inv = norm_parts(feats_rows)
     groups = feats_rows.shape[0] // GROUP
-    high, low = split(unstack_groups(sum_a.take()[...] + sum_b.take()[...], groups))
+    high, low = split(unstack_groups(src_sum.take()[...], groups))
     w_src = w_src.take()[...]
     scaled = column(gain.take()) * (dot(w_src, high) + dot(w_src, low))
     mean = jnp.mean(feats * scaled, axis=0, keepdims=True)
@@ -252,7 +290,7 @@
 
 def weight_kernel(ks, ours, theirs, w_src, gain, grad_src, grad_edge, grad_out, grad_gain):
     rows, chans = grad_src.shape
-    total = ours[...] + theirs[...]
+    total = ours.take()[...] + theirs.take()[...]
     for n, out in enumerate((grad_src, grad_edge, grad_out)):
         out[...] = total[n * rows : (n + 1) * rows, :]
     place = lax.broadcasted_iota(jnp.int32, (rows, chans), 1)
@@ -300,20 +338,25 @@
     vmem = pl.BlockSpec(memory_space=pltpu.VMEM)
     hbm = pl.BlockSpec(memory_space=pltpu.HBM)
 
-    def call(kernel, ks, outs, ins, scratch, name, flops, limit):
-        kinds, flat, buffers = [], [], []
+    def call(kernel, ks, outs, ins, scratch, name, flops, limit, fetch=False):
+        kinds, flat, buffers, here = [], [], [], set()
         for x in ins:
-            if isinstance(x, list):
+            if isinstance(x, list) and not fetch and x[0].dtype == BF16:
+                kinds.append("each")
+                flat += x
+                here.update(id(y) for y in x)
+            elif isinstance(x, list):
                 kinds.append("many")
                 flat += x
                 buffers += [pltpu.VMEM((len(x),) + x[0].shape, x[0].dtype), pltpu.SemaphoreType.DMA((len(x),))]
-            elif x is edges:
+            elif x is edges and fetch:
                 kinds.append("edges")
                 flat.append(x)
                 buffers += [pltpu.VMEM((len(ks),) + x.shape[1:], x.dtype), pltpu.SemaphoreType.DMA((len(ks),))]
-            elif id(x) in here:
+            elif x is not counts and not fetch:
                 kinds.append("here")
                 flat.append(x)
+                here.add(id(x))
             else:
                 kinds.append("copy")
                 flat.append(x)
@@ -330,7 +373,6 @@
             name=name,
         )(*flat)
 
-    here = set()
     tall = (groups * chans, GROUP)
     part_shape = (chans, atom_count)
     unit = 2 * slots * atom_count * chans
@@ -351,9 +393,9 @@
     outs = [
         ((2,) + part_shape, BF16),
         ((batches, chunk_rows, chans), F32),
-        (tall, F32),
+        ((2, chans, slots), BF16),
     ]
-    near_parts, near_chunks, near_sum = call(
+    near_parts, near_chunks, near_dpre = call(
         edge_kernel,
         near,
         outs,
@@ -362,11 +404,12 @@
         "near_edges",
         1,
         NEAR_VMEM_BYTES,
+        fetch=True,
     )
     far, far_dst, near_chunks = lax.optimization_barrier((far, far_dst, near_chunks))
     dst = dst + [far_dst, move(far_dst, "graph", 1)]
     cots = cots[:2] + [far, move(far, "graph", 1)]
-    far_parts, far_chunks, far_sum = call(
+    far_parts, far_chunks, far_dpre = call(
         edge_kernel,
         distant,
         outs,
@@ -378,13 +421,31 @@
     )
     chunks = near_chunks + far_chunks
 
+    def sum_sources(ks, dpre, before, name):
+        (total,) = call(
+            source_kernel,
+            ks,
+            [(tall, F32)],
+            [counts, src, dpre] + before,
+            [],
+            name,
+            unit,
+            FAR_VMEM_BYTES,
+        )
+        return total
+
     given_far = move(far_parts[1], "graph", 1)
-    chunks = reduce_batches(chunks, 1)
-    chunks, given_far = lax.optimization_barrier((chunks, given_far))
+    src_sum = sum_sources(near, near_dpre, [], "near_sources")
+    given_far, src_sum = lax.optimization_barrier((given_far, src_sum))
     far_part = (far_parts[0].astype(F32) + given_far.astype(F32)).astype(BF16)
     arrived = move(far_part, "graph", 2)
     own_part = near_parts[0].astype(F32) + move(near_parts[1], "graph", 1).astype(F32)
-    chunks = reduce_batches(chunks, batches.bit_length() - 2)
+    chunks = reduce_batches(chunks, 1)
+    chunks, src_sum, far_dpre = lax.optimization_barrier((chunks, src_sum, far_dpre))
+    src_sum = sum_sources(distant, far_dpre, [src_sum], "far_sources")
+    chunks = reduce_batches(chunks, 1)
+    chunks, src_sum = lax.optimization_barrier((chunks, src_sum))
+    chunks = reduce_batches(chunks, batches.bit_length() - 3)
     chunks, arrived = lax.optimization_barrier((chunks, arrived))
     total = chunks.reshape(chunk_rows, chans)
     total = total + move(total, "graph", 2)
@@ -393,7 +454,7 @@
         atom_kernel,
         (),
         [(feats.shape, BF16)] * 2,
-        [feats, gain_row, w_src, w_out, cot, near_sum, far_sum, own_part, arrived],
+        [feats, gain_row, w_src, w_out, cot, src_sum, own_part, arrived],
         [],
         "atoms",
         unit // 8,
@@ -402,7 +463,6 @@
 
     total, layer_out, grad_atoms = lax.optimization_barrier((total, layer_out, grad_atoms))
     theirs = move(total, "graph", 1)
-    here |= {id(total), id(theirs)}
     grads = call(
         weight_kernel,
         (),

time: 42.6 us -> 40.2 us (0.944); the launches traced: 42.1 us -> 40.5 us
  starting transfers between devices: 16.7 us -> 10.2 us
  Pallas kernels: 15.1 us -> 19.2 us
  local copies, waits for them, and re-layouts: 0.82 us -> 1.77 us
    ppermute x14, starting transfers between devices: 16.7 us -> 10.2 us  [move(): return lax.ppermute(x, axis, [(i, i ^ bit) for i in range(size)])]
    pallas_call x4 -> x6, Pallas kernels: 15.1 us -> 19.2 us  [call(): pl.pallas_call(functools.partial(with_fetches, kernel, kinds, ks, len(out...]
    squeeze x1, local copies, waits for them, and re-layouts: 0.02 us -> 0.97 us  [body(): near_parts[1]]
  transfers between devices with their start and end apart: 14 -> 14, of which waited for: 7 -> 6; matrix products, arithmetic and copies ran while one was open for 0% -> 3% of each run, Pallas kernels for 21% -> 46%
where the time goes in v3:
time: 40.2 us; the launch traced here: 40.5 us
  Pallas kernels  19.2 us (48%)
  starting transfers between devices  10.2 us (25%)
  waiting for transfers between devices  8.14 us (20%)
  local copies, waits for them, and re-layouts  1.77 us (4%)
  between operations  0.93 us (2%)
    pallas_call x6, Pallas kernels, call(): pl.pallas_call(functools.partial(with_fetches, kernel, kinds, ks, len(out...  19.2 us
    ppermute x14, starting transfers between devices, move(): return lax.ppermute(x, axis, [(i, i ^ bit) for i in range(size)])  10.2 us
    ppermute x14, waiting for transfers between devices, move(): return lax.ppermute(x, axis, [(i, i ^ bit) for i in range(size)])  8.14 us
    squeeze x1, local copies, waits for them, and re-layouts, body(): near_parts[1]  0.97 us
  transfers between devices with their start and end apart: 14, of which 6 were waited for; matrix products, arithmetic and copies ran while one was open for 3% of the time, Pallas kernels for 46%

profile of v3, /device:TPU:0, one launch (start us, length us, event | category | flops | bytes accessed | tf_op | source)
XLA Modules:
  0.0 40.5 jit_solution(14592650219886684081)
XLA Ops:
  0.6 0.0 copy-start.3
  0.6 0.0 copy-start.5
  0.7 0.0 copy-start.6
  0.7 0.0 copy-start
  0.7 0.0 copy-start.7
  0.7 0.0 copy-start.4
  0.7 0.0 copy-start.8
  0.7 0.0 copy-start.1
  0.7 0.5 %collective-permute-start.2 = (bf16[1024,128]{1,0:T(8,128)(2,1)}, bf16[1024,128]{1,0:T(8,128)(2,1)S(1)}, u32[]{:S(2)}, u32[]{:S(2)}) collective-permute-start(bf16[1024,128]{1,0:T(8,128)(2,1)} %bitcast.56), channel_id=1, source_target_pairs={{0,1},{1,0},{2,3},{3,2},{4,5},{5,4},{6,7},{7,6},{8,9},{9,8},{10,11... | collective-permute-start | bytes 786440 | tf_op jit(solution)/shard_map/ppermute | solution.py:307
  1.2 2.6 %collective-permute-start = (bf16[1024,128]{1,0:T(8,128)(2,1)}, bf16[1024,128]{1,0:T(8,128)(2,1)S(1)}, u32[]{:S(2)}, u32[]{:S(2)}) collective-permute-start(bf16[1024,128]{1,0:T(8,128)(2,1)} %bitcast.57), channel_id=1, source_target_pairs={{0,2},{1,3},{2,0},{3,1},{4,6},{5,7},{6,4},{7,5},{8,10},{9,11},{10,... | collective-permute-start | bytes 786440 | tf_op jit(solution)/shard_map/ppermute | solution.py:307
  3.8 0.2 collective-permute-start.3
  4.0 0.3 collective-permute-start.1
  4.2 1.0 %collective-permute-done.3.refs_10_ = s32[4,2048]{1,0:T(4,128)S(1)} collective-permute-done((s32[4,2048]{1,0:T(4,128)}, s32[4,2048]{1,0:T(4,128)S(1)}, u32[]{:S(2)}, u32[]{:S(2)}) %collective-permute-start.3) | collective-permute-done | bytes 32800 | tf_op jit(solution)/shard_map/ppermute | solution.py:307
  5.2 0.0 copy-start.13
  5.2 0.0 collective-permute-done.2.refs_4_
  5.2 0.6 %copy-done.13 = s32[4,2048]{1,0:T(4,128)} copy-done((s32[4,2048]{1,0:T(4,128)}, s32[4,2048]{1,0:T(4,128)S(1)}, u32[]{:S(2)}) %copy-start.13) | copy-done | bytes 32792
  5.8 0.1 copy-done.11
  5.9 7.6 %near_edges.1 = (bf16[2,128,1024]{2,1,0:T(8,128)(2,1)}, f32[8,48,128]{2,1,0:T(8,128)}, bf16[2,128,2048]{2,1,0:T(8,128)(2,1)}) custom-call(bf16[1024,128]{1,0:T(8,128)(2,1)} %bitcast.53, f32[1,128]{1,0:T(1,128)} %bitcast.68, bf16[128,128]{1,0:T(8,128)(2,1)} %refs_3_.1, bf16[1024,128]{1,0:T(8,128)(2,1)} %bitcast.58, bf16[1024,128]{1,0:T(8,128)(2,1)} %copy-done.11, ...), custom_call_target="tpu_custom_call" | custom-call | flops 1 | bytes 1 | tf_op jit(solution)/shard_map/near_edges/pallas_call | solution.py:365
  13.6 0.0 collective-permute-done.1.refs_9_
  13.6 0.0 collective-permute-done.refs_3_
  13.6 0.2 collective-permute-start.4
  13.8 0.3 collective-permute-start.5
  14.2 1.0 %slice_bitcast_fusion = bf16[128,1024]{1,0:T(8,128)(2,1)S(1)} fusion(bf16[2,128,1024]{2,1,0:T(8,128)(2,1)} %get-tuple-element.49), kind=kLoop, calls=%fused_computation.3 | loop fusion | bytes 524288 | tf_op jit(solution)/shard_map/squeeze | solution.py:442
  15.1 0.0 copy-start.12
  15.1 0.0 copy-start.9
  15.2 0.2 collective-permute-start.12
  15.4 0.0 collective-permute-done.5.refs_10_
  15.4 0.0 collective-permute-done.4.refs_4_
  15.4 0.0 copy-done.3
  15.4 0.0 copy-done.5
  15.4 0.0 copy-done.6
  15.4 0.0 copy-done
  15.4 0.0 copy-done.7
  15.4 0.0 copy-done.4
  15.5 0.0 copy-done.8
  15.5 0.0 copy-done.1
  15.5 5.3 %far_edges.1 = (bf16[2,128,1024]{2,1,0:T(8,128)(2,1)S(1)}, f32[8,48,128]{2,1,0:T(8,128)S(1)}, bf16[2,128,2048]{2,1,0:T(8,128)(2,1)S(1)}) custom-call(bf16[1024,128]{1,0:T(8,128)(2,1)S(1)} %bitcast.54, f32[1,128]{1,0:T(1,128)S(1)} %bitcast.69, bf16[128,128]{1,0:T(8,128)(2,1)S(1)} %copy-done.5, bf16[1024,128]{1,0:T(8,128)(2,1)S(1)} %collective-permute-done.refs_3_, ...), custom_call_target="tpu_custom_call" | custom-call | flops 4294967296 | bytes 1048576 | tf_op jit(solution)/shard_map/far_edges/pallas_call | solution.py:365
  20.8 0.0 copy-done.12
  20.9 0.2 collective-permute-start.6
  21.1 0.1 collective-permute-start.7
  21.2 0.0 copy-done.9
  21.2 2.1 %near_sources.1.refs_3_ = f32[512,256]{1,0:T(8,128)S(1)} custom-call(s32[4,4]{1,0:T(4,128)S(1)} %bitcast.66, s32[4,2048]{1,0:T(4,128)S(1)} %bitcast.62, bf16[2,128,2048]{2,1,0:T(8,128)(2,1)S(1)} %copy-done.9), custom_call_target="tpu_custom_call" | custom-call | flops 536870912 | bytes 1048576 | tf_op jit(solution)/shard_map/near_sources/pallas_call | solution.py:365
  23.3 0.0 copy-start.10
  23.3 2.2 %collective-permute-done.6 = f32[4,48,128]{2,1,0:T(8,128)S(1)} collective-permute-done((f32[4,48,128]{2,1,0:T(8,128)S(1)}, f32[4,48,128]{2,1,0:T(8,128)S(1)}, u32[]{:S(2)}, u32[]{:S(2)}) %collective-permute-start.6) | collective-permute-done | bytes 98336 | tf_op jit(solution)/shard_map/ppermute | solution.py:307
  25.6 0.0 copy-start.2
  25.6 0.0 collective-permute-done.7
  25.6 0.1 fusion
  25.7 1.1 %collective-permute-start.8 = (f32[2,48,128]{2,1,0:T(8,128)S(1)}, f32[2,48,128]{2,1,0:T(8,128)S(1)}, u32[]{:S(2)}, u32[]{:S(2)}) collective-permute-start(f32[2,48,128]{2,1,0:T(8,128)S(1)} %slice_bitcast_fusion.4), channel_id=1, source_target_pairs={{0,8},{4,12},{8,0},{12,4},{16,24},{20,28},{24,16},{28,20},{1,9},{5... | collective-permute-start | bytes 147464 | tf_op jit(solution)/shard_map/ppermute | solution.py:307
  26.8 0.4 %collective-permute-start.10 = (bf16[128,1024]{1,0:T(8,128)(2,1)S(1)}, bf16[128,1024]{1,0:T(8,128)(2,1)S(1)}, u32[]{:S(2)}, u32[]{:S(2)}) collective-permute-start(bf16[128,1024]{1,0:T(8,128)(2,1)S(1)} %fusion), channel_id=1, source_target_pairs={{0,2},{1,3},{2,0},{3,1},{4,6},{5,7},{6,4},{7,5},{8,10},{9,11},{10,... | collective-permute-start | bytes 786440 | tf_op jit(solution)/shard_map/ppermute | solution.py:307
  27.2 2.1 %far_sources.1.refs_5_ = f32[512,256]{1,0:T(8,128)S(1)} custom-call(s32[4,4]{1,0:T(4,128)S(1)} %bitcast.67, s32[4,2048]{1,0:T(4,128)S(1)} %bitcast.63, bf16[2,128,2048]{2,1,0:T(8,128)(2,1)S(1)} %get-tuple-element.43.refs_2_, f32[512,256]{1,0:T(8,128)S(1)} %near_sources.1.refs_3_), custom_call_target="tpu_custom_call" | custom-call | flops 536870912 | bytes 1048576 | tf_op jit(solution)/shard_map/far_sources/pallas_call | solution.py:365
  29.3 0.5 %collective-permute-done.8 = f32[2,48,128]{2,1,0:T(8,128)S(1)} collective-permute-done((f32[2,48,128]{2,1,0:T(8,128)S(1)}, f32[2,48,128]{2,1,0:T(8,128)S(1)}, u32[]{:S(2)}, u32[]{:S(2)}) %collective-permute-start.8) | collective-permute-done | bytes 49184 | tf_op jit(solution)/shard_map/ppermute | solution.py:307
  29.8 2.6 %collective-permute-start.9 = (f32[1,48,128]{2,1,0:T(8,128)S(1)}, f32[1,48,128]{2,1,0:T(8,128)S(1)}, u32[]{:S(2)}, u32[]{:S(2)}) collective-permute-start(f32[1,48,128]{2,1,0:T(8,128)S(1)} %slice_bitcast_fusion.6), channel_id=1, source_target_pairs={{0,16},{4,20},{8,24},{12,28},{16,0},{20,4},{24,8},{28,12},{1,17},{... | collective-permute-start | bytes 73736 | tf_op jit(solution)/shard_map/ppermute | solution.py:307
  32.5 2.2 %collective-permute-done.9 = f32[1,48,128]{2,1,0:T(8,128)S(1)} collective-permute-done((f32[1,48,128]{2,1,0:T(8,128)S(1)}, f32[1,48,128]{2,1,0:T(8,128)S(1)}, u32[]{:S(2)}, u32[]{:S(2)}) %collective-permute-start.9) | collective-permute-done | bytes 24608 | tf_op jit(solution)/shard_map/ppermute | solution.py:307
  34.6 0.0 collective-permute-done.10.refs_7_
  34.6 1.4 %collective-permute-start.11 = (f32[48,128]{1,0:T(8,128)S(1)}, f32[48,128]{1,0:T(8,128)S(1)}, u32[]{:S(2)}, u32[]{:S(2)}) collective-permute-start(f32[48,128]{1,0:T(8,128)S(1)} %bitcast.78), channel_id=1, source_target_pairs={{0,2},{1,3},{2,0},{3,1},{4,6},{5,7},{6,4},{7,5},{8,10},{9,11},{10,... | collective-permute-start | bytes 73736 | tf_op jit(solution)/shard_map/ppermute | solution.py:307
  36.0 0.0 collective-permute-done.12
  36.0 0.0 copy-done.10
  36.0 0.1 convert_add_fusion.refs_6_
  36.1 0.0 copy-done.2
  36.1 1.4 %atoms.1 = (bf16[1024,128]{1,0:T(8,128)(2,1)}, bf16[1024,128]{1,0:T(8,128)(2,1)}) custom-call(bf16[1024,128]{1,0:T(8,128)(2,1)S(1)} %bitcast.55, f32[1,128]{1,0:T(1,128)S(1)} %bitcast.70, bf16[128,128]{1,0:T(8,128)(2,1)S(1)} %copy-done.3, bf16[128,128]{1,0:T(8,128)(2,1)S(1)} %copy-done.5, bf16[1024,128]{1,0:T(8,128)(2,1)S(1)} %bitcast.59, ...), custom_call_target="tpu_custom_call" | custom-call | flops 67108864 | bytes 1048576 | tf_op jit(solution)/shard_map/atoms/pallas_call | solution.py:365
  37.5 1.1 %collective-permute-done.11 = f32[48,128]{1,0:T(8,128)S(1)} collective-permute-done((f32[48,128]{1,0:T(8,128)S(1)}, f32[48,128]{1,0:T(8,128)S(1)}, u32[]{:S(2)}, u32[]{:S(2)}) %collective-permute-start.11) | collective-permute-done | bytes 24608 | tf_op jit(solution)/shard_map/ppermute | solution.py:307
  38.5 0.0 collective-permute-start.13
  38.5 1.2 %collective-permute-done.13.refs_1_ = f32[48,128]{1,0:T(8,128)S(1)} collective-permute-done((f32[48,128]{1,0:T(8,128)S(1)}, f32[48,128]{1,0:T(8,128)S(1)}, u32[]{:S(2)}, u32[]{:S(2)}) %collective-permute-start.13) | collective-permute-done | bytes 24608 | tf_op jit(solution)/shard_map/ppermute | solution.py:307
  39.7 0.7 %weights.1 = (f32[16,128]{1,0:T(8,128)}, f32[16,128]{1,0:T(8,128)}, f32[16,128]{1,0:T(8,128)}, f32[1,16]{1,0:T(1,128)}) custom-call(f32[48,128]{1,0:T(8,128)S(1)} %bitcast_add_fusion.refs_0_, f32[48,128]{1,0:T(8,128)S(1)} %collective-permute-done.13.refs_1_, bf16[128,128]{1,0:T(8,128)(2,1)S(1)} %copy-done.3, f32[1,128]{1,0:T(1,128)S(1)} %bitcast.71), custom_call_target="tpu_custom_call" | custom-call | flops 1 | bytes 1 | tf_op jit(solution)/shard_map/weights/pallas_call | solution.py:365
  (10 shorter events, 0.1 us)
Async XLA Ops:
  0.6 14.8 %copy-start.3 = (bf16[128,128]{1,0:T(8,128)(2,1)S(1)}, bf16[128,128]{1,0:T(8,128)(2,1)}, u32[]{:S(2)}) copy-start(bf16[128,128]{1,0:T(8,128)(2,1)} %refs_2_.7) | copy-start | bytes 98308
  0.6 14.8 %copy-start.5 = (bf16[128,128]{1,0:T(8,128)(2,1)S(1)}, bf16[128,128]{1,0:T(8,128)(2,1)}, u32[]{:S(2)}) copy-start(bf16[128,128]{1,0:T(8,128)(2,1)} %refs_3_.1) | copy-start | bytes 98308
  0.7 14.8 %copy-start.6 = (bf16[128,128]{1,0:T(8,128)(2,1)S(1)}, bf16[128,128]{1,0:T(8,128)(2,1)}, u32[]{:S(2)}) copy-start(bf16[128,128]{1,0:T(8,128)(2,1)} %refs_6_.3) | copy-start | bytes 98308
  0.7 14.8 %copy-start = (bf16[1,1,4,2048,128]{4,3,2,1,0:T(8,128)(2,1)S(1)}, bf16[1,1,4,2048,128]{4,3,2,1,0:T(8,128)(2,1)}, u32[]{:S(2)}) copy-start(bf16[1,1,4,2048,128]{4,3,2,1,0:T(8,128)(2,1)} %param.18) | copy-start | bytes 6291460
  0.7 14.8 %copy-start.7 = (s32[1,4,4]{2,1,0:T(4,128)S(1)}, s32[1,4,4]{2,1,0:T(4,128)}, u32[]{:S(2)}) copy-start(s32[1,4,4]{2,1,0:T(4,128)} %param.17) | copy-start | bytes 196
  0.7 14.8 %copy-start.4 = (s32[1,1,4,2048]{3,2,1,0:T(4,128)S(1)}, s32[1,1,4,2048]{3,2,1,0:T(4,128)}, u32[]{:S(2)}) copy-start(s32[1,1,4,2048]{3,2,1,0:T(4,128)} %param.15) | copy-start | bytes 98308
  0.7 14.8 %copy-start.8 = (f32[128]{0:T(128)S(1)}, f32[128]{0:T(128)}, u32[]{:S(2)}) copy-start(f32[128]{0:T(128)} %param.11) | copy-start | bytes 1540
  0.7 14.8 %copy-start.1 = (bf16[1,1,1024,128]{3,2,1,0:T(8,128)(2,1)S(1)}, bf16[1,1,1024,128]{3,2,1,0:T(8,128)(2,1)}, u32[]{:S(2)}) copy-start(bf16[1,1,1024,128]{3,2,1,0:T(8,128)(2,1)} %param.10) | copy-start | bytes 786436
  0.7 4.5 %collective-permute-start.2 = (bf16[1024,128]{1,0:T(8,128)(2,1)}, bf16[1024,128]{1,0:T(8,128)(2,1)S(1)}, u32[]{:S(2)}, u32[]{:S(2)}) collective-permute-start(bf16[1024,128]{1,0:T(8,128)(2,1)} %bitcast.56), channel_id=1, source_target_pairs={{0,1},{1,0},{2,3},{3,2},{4,5},{5,4},{6,7},{7,6},{8,9},{9,8},{10,11... | collective-permute-start | bytes 786440 | tf_op jit(solution)/shard_map/ppermute | solution.py:307
  1.2 12.3 %collective-permute-start = (bf16[1024,128]{1,0:T(8,128)(2,1)}, bf16[1024,128]{1,0:T(8,128)(2,1)S(1)}, u32[]{:S(2)}, u32[]{:S(2)}) collective-permute-start(bf16[1024,128]{1,0:T(8,128)(2,1)} %bitcast.57), channel_id=1, source_target_pairs={{0,2},{1,3},{2,0},{3,1},{4,6},{5,7},{6,4},{7,5},{8,10},{9,11},{10,... | collective-permute-start | bytes 786440 | tf_op jit(solution)/shard_map/ppermute | solution.py:307
  3.8 1.4 %collective-permute-start.3 = (s32[4,2048]{1,0:T(4,128)}, s32[4,2048]{1,0:T(4,128)S(1)}, u32[]{:S(2)}, u32[]{:S(2)}) collective-permute-start(s32[4,2048]{1,0:T(4,128)} %bitcast.79), channel_id=1, source_target_pairs={{0,1},{1,0},{2,3},{3,2},{4,5},{5,4},{6,7},{7,6},{8,9},{9,8},{10,11... | collective-permute-start | bytes 98312 | tf_op jit(solution)/shard_map/ppermute | solution.py:307
  4.0 9.6 %collective-permute-start.1 = (s32[4,2048]{1,0:T(4,128)}, s32[4,2048]{1,0:T(4,128)S(1)}, u32[]{:S(2)}, u32[]{:S(2)}) collective-permute-start(s32[4,2048]{1,0:T(4,128)} %bitcast.80), channel_id=1, source_target_pairs={{0,2},{1,3},{2,0},{3,1},{4,6},{5,7},{6,4},{7,5},{8,10},{9,11},{10,... | collective-permute-start | bytes 98312 | tf_op jit(solution)/shard_map/ppermute | solution.py:307
  5.2 0.6 %copy-start.13 = (s32[4,2048]{1,0:T(4,128)}, s32[4,2048]{1,0:T(4,128)S(1)}, u32[]{:S(2)}) copy-start(s32[4,2048]{1,0:T(4,128)S(1)} %collective-permute-done.3.refs_10_) | copy-start | bytes 98308
  5.2 0.7 %copy-start.11 = (bf16[1024,128]{1,0:T(8,128)(2,1)}, bf16[1024,128]{1,0:T(8,128)(2,1)S(1)}, u32[]{:S(2)}) copy-start(bf16[1024,128]{1,0:T(8,128)(2,1)S(1)} %collective-permute-done.2.refs_4_) | copy-start | bytes 786436
  13.6 1.8 %collective-permute-start.4 = (bf16[1024,128]{1,0:T(8,128)(2,1)S(1)}, bf16[1024,128]{1,0:T(8,128)(2,1)S(1)}, u32[]{:S(2)}, u32[]{:S(2)}) collective-permute-start(bf16[1024,128]{1,0:T(8,128)(2,1)S(1)} %collective-permute-done.refs_3_), channel_id=1, source_target_pairs={{0,1},{1,0},{2,3},{3,2},{4,5},{5,4},{6,7},{7,6},{8,9},{9,8},{10,11... | collective-permute-start | bytes 786440 | tf_op jit(solution)/shard_map/ppermute | solution.py:307
  13.8 1.6 %collective-permute-start.5 = (s32[4,2048]{1,0:T(4,128)S(1)}, s32[4,2048]{1,0:T(4,128)S(1)}, u32[]{:S(2)}, u32[]{:S(2)}) collective-permute-start(s32[4,2048]{1,0:T(4,128)S(1)} %collective-permute-done.1.refs_9_), channel_id=1, source_target_pairs={{0,1},{1,0},{2,3},{3,2},{4,5},{5,4},{6,7},{7,6},{8,9},{9,8},{10,11... | collective-permute-start | bytes 98312 | tf_op jit(solution)/shard_map/ppermute | solution.py:307
  15.1 5.7 %copy-start.12 = (f32[8,48,128]{2,1,0:T(8,128)S(1)}, f32[8,48,128]{2,1,0:T(8,128)}, u32[]{:S(2)}) copy-start(f32[8,48,128]{2,1,0:T(8,128)} %get-tuple-element.34) | copy-start | bytes 589828
  15.1 6.1 %copy-start.9 = (bf16[2,128,2048]{2,1,0:T(8,128)(2,1)S(1)}, bf16[2,128,2048]{2,1,0:T(8,128)(2,1)}, u32[]{:S(2)}) copy-start(bf16[2,128,2048]{2,1,0:T(8,128)(2,1)} %get-tuple-element.39.refs_2_) | copy-start | bytes 3145732
  15.2 20.8 %collective-permute-start.12 = (bf16[128,1024]{1,0:T(8,128)(2,1)S(1)}, bf16[128,1024]{1,0:T(8,128)(2,1)S(1)}, u32[]{:S(2)}, u32[]{:S(2)}) collective-permute-start(bf16[128,1024]{1,0:T(8,128)(2,1)S(1)} %slice_bitcast_fusion), channel_id=1, source_target_pairs={{0,1},{1,0},{2,3},{3,2},{4,5},{5,4},{6,7},{7,6},{8,9},{9,8},{10,11... | collective-permute-start | bytes 786440 | tf_op jit(solution)/shard_map/ppermute | solution.py:307
  20.9 4.7 %collective-permute-start.6 = (f32[4,48,128]{2,1,0:T(8,128)S(1)}, f32[4,48,128]{2,1,0:T(8,128)S(1)}, u32[]{:S(2)}, u32[]{:S(2)}) collective-permute-start(f32[4,48,128]{2,1,0:T(8,128)S(1)} %slice_bitcast_fusion.2), channel_id=1, source_target_pairs={{0,4},{4,0},{8,12},{12,8},{16,20},{20,16},{24,28},{28,24},{1,5},{5... | collective-permute-start | bytes 294920 | tf_op jit(solution)/shard_map/ppermute | solution.py:307
  21.1 4.5 %collective-permute-start.7 = (bf16[128,1024]{1,0:T(8,128)(2,1)S(1)}, bf16[128,1024]{1,0:T(8,128)(2,1)S(1)}, u32[]{:S(2)}, u32[]{:S(2)}) collective-permute-start(bf16[128,1024]{1,0:T(8,128)(2,1)S(1)} %slice_bitcast_fusion.1), channel_id=1, source_target_pairs={{0,1},{1,0},{2,3},{3,2},{4,5},{5,4},{6,7},{7,6},{8,9},{9,8},{10,11... | collective-permute-start | bytes 786440 | tf_op jit(solution)/shard_map/ppermute | solution.py:307
  23.3 12.7 %copy-start.10 = (bf16[2,128,1024]{2,1,0:T(8,128)(2,1)S(1)}, bf16[2,128,1024]{2,1,0:T(8,128)(2,1)}, u32[]{:S(2)}) copy-start(bf16[2,128,1024]{2,1,0:T(8,128)(2,1)} %get-tuple-element.49) | copy-start | bytes 1572868
  25.6 10.5 %copy-start.2 = (bf16[1,1,1024,128]{3,2,1,0:T(8,128)(2,1)S(1)}, bf16[1,1,1024,128]{3,2,1,0:T(8,128)(2,1)}, u32[]{:S(2)}) copy-start(bf16[1,1,1024,128]{3,2,1,0:T(8,128)(2,1)} %param.19) | copy-start | bytes 786436
  25.7 4.2 %collective-permute-start.8 = (f32[2,48,128]{2,1,0:T(8,128)S(1)}, f32[2,48,128]{2,1,0:T(8,128)S(1)}, u32[]{:S(2)}, u32[]{:S(2)}) collective-permute-start(f32[2,48,128]{2,1,0:T(8,128)S(1)} %slice_bitcast_fusion.4), channel_id=1, source_target_pairs={{0,8},{4,12},{8,0},{12,4},{16,24},{20,28},{24,16},{28,20},{1,9},{5... | collective-permute-start | bytes 147464 | tf_op jit(solution)/shard_map/ppermute | solution.py:307
  26.8 7.8 %collective-permute-start.10 = (bf16[128,1024]{1,0:T(8,128)(2,1)S(1)}, bf16[128,1024]{1,0:T(8,128)(2,1)S(1)}, u32[]{:S(2)}, u32[]{:S(2)}) collective-permute-start(bf16[128,1024]{1,0:T(8,128)(2,1)S(1)} %fusion), channel_id=1, source_target_pairs={{0,2},{1,3},{2,0},{3,1},{4,6},{5,7},{6,4},{7,5},{8,10},{9,11},{10,... | collective-permute-start | bytes 786440 | tf_op jit(solution)/shard_map/ppermute | solution.py:307
  29.8 4.8 %collective-permute-start.9 = (f32[1,48,128]{2,1,0:T(8,128)S(1)}, f32[1,48,128]{2,1,0:T(8,128)S(1)}, u32[]{:S(2)}, u32[]{:S(2)}) collective-permute-start(f32[1,48,128]{2,1,0:T(8,128)S(1)} %slice_bitcast_fusion.6), channel_id=1, source_target_pairs={{0,16},{4,20},{8,24},{12,28},{16,0},{20,4},{24,8},{28,12},{1,17},{... | collective-permute-start | bytes 73736 | tf_op jit(solution)/shard_map/ppermute | solution.py:307
  34.6 3.9 %collective-permute-start.11 = (f32[48,128]{1,0:T(8,128)S(1)}, f32[48,128]{1,0:T(8,128)S(1)}, u32[]{:S(2)}, u32[]{:S(2)}) collective-permute-start(f32[48,128]{1,0:T(8,128)S(1)} %bitcast.78), channel_id=1, source_target_pairs={{0,2},{1,3},{2,0},{3,1},{4,6},{5,7},{6,4},{7,5},{8,10},{9,11},{10,... | collective-permute-start | bytes 73736 | tf_op jit(solution)/shard_map/ppermute | solution.py:307
  38.5 1.2 %collective-permute-start.13 = (f32[48,128]{1,0:T(8,128)S(1)}, f32[48,128]{1,0:T(8,128)S(1)}, u32[]{:S(2)}, u32[]{:S(2)}) collective-permute-start(f32[48,128]{1,0:T(8,128)S(1)} %bitcast_add_fusion.refs_0_), channel_id=1, source_target_pairs={{0,1},{1,0},{2,3},{3,2},{4,5},{5,4},{6,7},{7,6},{8,9},{9,8},{10,11... | collective-permute-start | bytes 73736 | tf_op jit(solution)/shard_map/ppermute | solution.py:307

commit v4 on v3

--- a/solution.py
+++ b/solution.py
@@ -171,7 +171,8 @@
     src,
     dsts,
     edges,
-    parts,
+    part_a,
+    part_b,
     chunks,
     dpres,
     table,
@@ -244,7 +245,7 @@
     grad_out = jnp.zeros((chans, chans), F32)
     for i in range(len(ks)):
         part = (unstack_groups(agg_sum[i], groups) * (1.0 / DEG_NORM)).astype(BF16)
-        parts[i] = part
+        (part_a, part_b)[i][...] = part
         grad_out = grad_out + dot(part, cots[i])
     batches = chunks.shape[0]
     rows = chans // batches
@@ -391,11 +392,12 @@
     rows = chans // batches
     chunk_rows = -(-3 * rows // 8) * 8
     outs = [
-        ((2,) + part_shape, BF16),
+        (part_shape, BF16),
+        (part_shape, BF16),
         ((batches, chunk_rows, chans), F32),
         ((2, chans, slots), BF16),
     ]
-    near_parts, near_chunks, near_dpre = call(
+    *near_parts, near_chunks, near_dpre = call(
         edge_kernel,
         near,
         outs,
@@ -409,7 +411,7 @@
     far, far_dst, near_chunks = lax.optimization_barrier((far, far_dst, near_chunks))
     dst = dst + [far_dst, move(far_dst, "graph", 1)]
     cots = cots[:2] + [far, move(far, "graph", 1)]
-    far_parts, far_chunks, far_dpre = call(
+    *far_parts, far_chunks, far_dpre = call(
         edge_kernel,
         distant,
         outs,

time: 40.2 us -> 41 us (1.020); the launches traced: 40.5 us -> 40.7 us
  starting transfers between devices: 10.2 us -> 12.5 us
  Pallas kernels: 19.2 us -> 17.3 us
  local copies, waits for them, and re-layouts: 1.77 us -> 0.78 us
  waiting for transfers between devices: 8.14 us -> 9.05 us
    ppermute x14, starting transfers between devices: 10.2 us -> 12.5 us  [move(): return lax.ppermute(x, axis, [(i, i ^ bit) for i in range(size)])]
    pallas_call x6, Pallas kernels: 19.2 us -> 17.3 us  [call(): pl.pallas_call(functools.partial(with_fetches, kernel, kinds, ks, len(out...]
    squeeze x2 -> x0, local copies, waits for them, and re-layouts: 0.98 us -> none  [the longest x1 0.97 us: body(): near_parts[1]]
    ppermute x14, waiting for transfers between devices: 8.14 us -> 9.05 us  [move(): return lax.ppermute(x, axis, [(i, i ^ bit) for i in range(size)])]
  transfers between devices with their start and end apart: 14 -> 14, of which waited for: 6 -> 6; matrix products, arithmetic and copies ran while one was open for 3% -> 0% of each run, Pallas kernels for 46% -> 28%
where the time goes in v4:
time: 41 us; the launch traced here: 40.7 us
  Pallas kernels  17.3 us (42%)
  starting transfers between devices  12.5 us (30%)
  waiting for transfers between devices  9.05 us (22%)
  between operations  0.94 us (2%)
  local copies, waits for them, and re-layouts  0.78 us (2%)
    pallas_call x6, Pallas kernels, call(): pl.pallas_call(functools.partial(with_fetches, kernel, kinds, ks, len(out...  17.3 us
    ppermute x14, starting transfers between devices, move(): return lax.ppermute(x, axis, [(i, i ^ bit) for i in range(size)])  12.5 us
    ppermute x14, waiting for transfers between devices, move(): return lax.ppermute(x, axis, [(i, i ^ bit) for i in range(size)])  9.05 us
  transfers between devices with their start and end apart: 14, of which 6 were waited for; matrix products, arithmetic and copies ran while one was open for 0% of the time, Pallas kernels for 28%

profile of v4, /device:TPU:0, one launch (start us, length us, event | category | flops | bytes accessed | tf_op | source)
XLA Modules:
  0.0 40.7 jit_solution(12749249585570870085)
XLA Ops:
  0.6 0.0 copy-start.3
  0.6 0.0 copy-start.5
  0.7 0.0 copy-start.6
  0.7 0.0 copy-start
  0.7 0.0 copy-start.7
  0.7 0.0 copy-start.4
  0.7 0.0 copy-start.8
  0.7 0.0 copy-start.1
  0.7 0.5 %collective-permute-start.2 = (bf16[1024,128]{1,0:T(8,128)(2,1)}, bf16[1024,128]{1,0:T(8,128)(2,1)S(1)}, u32[]{:S(2)}, u32[]{:S(2)}) collective-permute-start(bf16[1024,128]{1,0:T(8,128)(2,1)} %bitcast.46), channel_id=1, source_target_pairs={{0,1},{1,0},{2,3},{3,2},{4,5},{5,4},{6,7},{7,6},{8,9},{9,8},{10,11... | collective-permute-start | bytes 786440 | tf_op jit(solution)/shard_map/ppermute | solution.py:308
  1.2 2.6 %collective-permute-start = (bf16[1024,128]{1,0:T(8,128)(2,1)}, bf16[1024,128]{1,0:T(8,128)(2,1)S(1)}, u32[]{:S(2)}, u32[]{:S(2)}) collective-permute-start(bf16[1024,128]{1,0:T(8,128)(2,1)} %bitcast.47), channel_id=1, source_target_pairs={{0,2},{1,3},{2,0},{3,1},{4,6},{5,7},{6,4},{7,5},{8,10},{9,11},{10,... | collective-permute-start | bytes 786440 | tf_op jit(solution)/shard_map/ppermute | solution.py:308
  3.8 0.2 collective-permute-start.3
  4.0 0.3 collective-permute-start.1
  4.2 1.0 %collective-permute-done.3.refs_10_ = s32[4,2048]{1,0:T(4,128)S(1)} collective-permute-done((s32[4,2048]{1,0:T(4,128)}, s32[4,2048]{1,0:T(4,128)S(1)}, u32[]{:S(2)}, u32[]{:S(2)}) %collective-permute-start.3) | collective-permute-done | bytes 32800 | tf_op jit(solution)/shard_map/ppermute | solution.py:308
  5.2 0.0 copy-start.13
  5.2 0.0 collective-permute-done.2.refs_4_
  5.2 0.6 %copy-done.13 = s32[4,2048]{1,0:T(4,128)} copy-done((s32[4,2048]{1,0:T(4,128)}, s32[4,2048]{1,0:T(4,128)S(1)}, u32[]{:S(2)}) %copy-start.13) | copy-done | bytes 32792
  5.8 0.1 copy-done.10
  5.9 6.2 %near_edges.1 = (bf16[128,1024]{1,0:T(8,128)(2,1)}, bf16[128,1024]{1,0:T(8,128)(2,1)}, f32[8,48,128]{2,1,0:T(8,128)}, bf16[2,128,2048]{2,1,0:T(8,128)(2,1)}) custom-call(bf16[1024,128]{1,0:T(8,128)(2,1)} %bitcast.43, f32[1,128]{1,0:T(1,128)} %bitcast.58, bf16[128,128]{1,0:T(8,128)(2,1)} %refs_3_.1, bf16[1024,128]{1,0:T(8,128)(2,1)} %bitcast.48, ...), custom_call_target="tpu_custom_call" | custom-call | flops 1 | bytes 1 | tf_op jit(solution)/shard_map/near_edges/pallas_call | solution.py:366
  12.1 0.0 collective-permute-done.1.refs_9_
  12.2 0.0 collective-permute-done.refs_3_
  12.2 0.0 copy-start.12
  12.2 0.0 copy-start.14
  12.2 0.0 copy-start.9
  12.2 0.2 collective-permute-start.4
  12.4 0.3 collective-permute-start.5
  12.8 1.1 %collective-permute-done.5.refs_10_ = s32[4,2048]{1,0:T(4,128)S(1)} collective-permute-done((s32[4,2048]{1,0:T(4,128)S(1)}, s32[4,2048]{1,0:T(4,128)S(1)}, u32[]{:S(2)}, u32[]{:S(2)}) %collective-permute-start.5) | collective-permute-done | bytes 32800 | tf_op jit(solution)/shard_map/ppermute | solution.py:308
  13.8 0.0 collective-permute-done.4.refs_4_
  13.8 0.0 copy-done.3
  13.8 0.0 copy-done.5
  13.9 0.0 copy-done.6
  13.9 0.0 copy-done
  13.9 0.0 copy-done.7
  13.9 0.0 copy-done.4
  13.9 0.0 copy-done.8
  13.9 0.0 copy-done.1
  13.9 5.3 %far_edges.1 = (bf16[128,1024]{1,0:T(8,128)(2,1)S(1)}, bf16[128,1024]{1,0:T(8,128)(2,1)S(1)}, f32[8,48,128]{2,1,0:T(8,128)S(1)}, bf16[2,128,2048]{2,1,0:T(8,128)(2,1)S(1)}) custom-call(bf16[1024,128]{1,0:T(8,128)(2,1)S(1)} %bitcast.44, f32[1,128]{1,0:T(1,128)S(1)} %bitcast.59, bf16[128,128]{1,0:T(8,128)(2,1)S(1)} %copy-done.5, ...), custom_call_target="tpu_custom_call" | custom-call | flops 4294967296 | bytes 1048576 | tf_op jit(solution)/shard_map/far_edges/pallas_call | solution.py:366
  19.2 0.0 copy-done.12
  19.3 1.6 %collective-permute-start.6 = (f32[4,48,128]{2,1,0:T(8,128)S(1)}, f32[4,48,128]{2,1,0:T(8,128)S(1)}, u32[]{:S(2)}, u32[]{:S(2)}) collective-permute-start(f32[4,48,128]{2,1,0:T(8,128)S(1)} %slice_bitcast_fusion), channel_id=1, source_target_pairs={{0,4},{4,0},{8,12},{12,8},{16,20},{20,16},{24,28},{28,24},{1,5},{5... | collective-permute-start | bytes 294920 | tf_op jit(solution)/shard_map/ppermute | solution.py:308
  20.9 0.0 copy-done.14
  20.9 0.0 collective-permute-start.12
  20.9 0.5 %collective-permute-start.7 = (bf16[128,1024]{1,0:T(8,128)(2,1)S(1)}, bf16[128,1024]{1,0:T(8,128)(2,1)S(1)}, u32[]{:S(2)}, u32[]{:S(2)}) collective-permute-start(bf16[128,1024]{1,0:T(8,128)(2,1)S(1)} %get-tuple-element.40), channel_id=1, source_target_pairs={{0,1},{1,0},{2,3},{3,2},{4,5},{5,4},{6,7},{7,6},{8,9},{9,8},{10,11... | collective-permute-start | bytes 786440 | tf_op jit(solution)/shard_map/ppermute | solution.py:308
  21.4 0.0 copy-done.9
  21.4 1.6 %near_sources.1.refs_3_ = f32[512,256]{1,0:T(8,128)S(1)} custom-call(s32[4,4]{1,0:T(4,128)S(1)} %bitcast.56, s32[4,2048]{1,0:T(4,128)S(1)} %bitcast.52, bf16[2,128,2048]{2,1,0:T(8,128)(2,1)S(1)} %copy-done.9), custom_call_target="tpu_custom_call" | custom-call | flops 536870912 | bytes 1048576 | tf_op jit(solution)/shard_map/near_sources/pallas_call | solution.py:366
  23.0 0.0 copy-start.11
  23.0 1.2 %collective-permute-done.6 = f32[4,48,128]{2,1,0:T(8,128)S(1)} collective-permute-done((f32[4,48,128]{2,1,0:T(8,128)S(1)}, f32[4,48,128]{2,1,0:T(8,128)S(1)}, u32[]{:S(2)}, u32[]{:S(2)}) %collective-permute-start.6) | collective-permute-done | bytes 98336 | tf_op jit(solution)/shard_map/ppermute | solution.py:308
  24.2 0.0 collective-permute-done.7
  24.3 1.6 %collective-permute-start.8 = (f32[2,48,128]{2,1,0:T(8,128)S(1)}, f32[2,48,128]{2,1,0:T(8,128)S(1)}, u32[]{:S(2)}, u32[]{:S(2)}) collective-permute-start(f32[2,48,128]{2,1,0:T(8,128)S(1)} %slice_bitcast_fusion.2), channel_id=1, source_target_pairs={{0,8},{4,12},{8,0},{12,4},{16,24},{20,28},{24,16},{28,20},{1,9},{5... | collective-permute-start | bytes 147464 | tf_op jit(solution)/shard_map/ppermute | solution.py:308
  25.9 0.1 add_convert_fusion
  26.0 2.0 %collective-permute-start.10 = (bf16[128,1024]{1,0:T(8,128)(2,1)S(1)}, bf16[128,1024]{1,0:T(8,128)(2,1)S(1)}, u32[]{:S(2)}, u32[]{:S(2)}) collective-permute-start(bf16[128,1024]{1,0:T(8,128)(2,1)S(1)} %add_convert_fusion), channel_id=1, source_target_pairs={{0,2},{1,3},{2,0},{3,1},{4,6},{5,7},{6,4},{7,5},{8,10},{9,11},{10,... | collective-permute-start | bytes 786440 | tf_op jit(solution)/shard_map/ppermute | solution.py:308
  28.0 2.1 %far_sources.1.refs_5_ = f32[512,256]{1,0:T(8,128)S(1)} custom-call(s32[4,4]{1,0:T(4,128)S(1)} %bitcast.57, s32[4,2048]{1,0:T(4,128)S(1)} %bitcast.53, bf16[2,128,2048]{2,1,0:T(8,128)(2,1)S(1)} %get-tuple-element.45.refs_2_, f32[512,256]{1,0:T(8,128)S(1)} %near_sources.1.refs_3_), custom_call_target="tpu_custom_call" | custom-call | flops 536870912 | bytes 1048576 | tf_op jit(solution)/shard_map/far_sources/pallas_call | solution.py:366
  30.1 0.0 collective-permute-done.8
  30.1 2.1 %collective-permute-start.9 = (f32[1,48,128]{2,1,0:T(8,128)S(1)}, f32[1,48,128]{2,1,0:T(8,128)S(1)}, u32[]{:S(2)}, u32[]{:S(2)}) collective-permute-start(f32[1,48,128]{2,1,0:T(8,128)S(1)} %slice_bitcast_fusion.4), channel_id=1, source_target_pairs={{0,16},{4,20},{8,24},{12,28},{16,0},{20,4},{24,8},{28,12},{1,17},{... | collective-permute-start | bytes 73736 | tf_op jit(solution)/shard_map/ppermute | solution.py:308
  32.2 2.6 %collective-permute-done.9 = f32[1,48,128]{2,1,0:T(8,128)S(1)} collective-permute-done((f32[1,48,128]{2,1,0:T(8,128)S(1)}, f32[1,48,128]{2,1,0:T(8,128)S(1)}, u32[]{:S(2)}, u32[]{:S(2)}) %collective-permute-start.9) | collective-permute-done | bytes 24608 | tf_op jit(solution)/shard_map/ppermute | solution.py:308
  34.9 0.0 collective-permute-done.10.refs_7_
  34.9 0.5 %collective-permute-start.11 = (f32[48,128]{1,0:T(8,128)S(1)}, f32[48,128]{1,0:T(8,128)S(1)}, u32[]{:S(2)}, u32[]{:S(2)}) collective-permute-start(f32[48,128]{1,0:T(8,128)S(1)} %bitcast.68), channel_id=1, source_target_pairs={{0,2},{1,3},{2,0},{3,1},{4,6},{5,7},{6,4},{7,5},{8,10},{9,11},{10,... | collective-permute-start | bytes 73736 | tf_op jit(solution)/shard_map/ppermute | solution.py:308
  35.4 0.0 collective-permute-done.12
  35.4 0.0 copy-done.11
  35.4 0.1 convert_add_fusion.refs_6_
  35.5 0.0 copy-done.2
  35.5 1.4 %atoms.1 = (bf16[1024,128]{1,0:T(8,128)(2,1)}, bf16[1024,128]{1,0:T(8,128)(2,1)}) custom-call(bf16[1024,128]{1,0:T(8,128)(2,1)S(1)} %bitcast.45, f32[1,128]{1,0:T(1,128)S(1)} %bitcast.60, bf16[128,128]{1,0:T(8,128)(2,1)S(1)} %copy-done.3, bf16[128,128]{1,0:T(8,128)(2,1)S(1)} %copy-done.5, bf16[1024,128]{1,0:T(8,128)(2,1)S(1)} %bitcast.49, ...), custom_call_target="tpu_custom_call" | custom-call | flops 67108864 | bytes 1048576 | tf_op jit(solution)/shard_map/atoms/pallas_call | solution.py:366
  36.9 1.9 %collective-permute-done.11 = f32[48,128]{1,0:T(8,128)S(1)} collective-permute-done((f32[48,128]{1,0:T(8,128)S(1)}, f32[48,128]{1,0:T(8,128)S(1)}, u32[]{:S(2)}, u32[]{:S(2)}) %collective-permute-start.11) | collective-permute-done | bytes 24608 | tf_op jit(solution)/shard_map/ppermute | solution.py:308
  38.8 0.0 collective-permute-start.13
  38.8 1.2 %collective-permute-done.13.refs_1_ = f32[48,128]{1,0:T(8,128)S(1)} collective-permute-done((f32[48,128]{1,0:T(8,128)S(1)}, f32[48,128]{1,0:T(8,128)S(1)}, u32[]{:S(2)}, u32[]{:S(2)}) %collective-permute-start.13) | collective-permute-done | bytes 24608 | tf_op jit(solution)/shard_map/ppermute | solution.py:308
  40.0 0.7 %weights.1 = (f32[16,128]{1,0:T(8,128)}, f32[16,128]{1,0:T(8,128)}, f32[16,128]{1,0:T(8,128)}, f32[1,16]{1,0:T(1,128)}) custom-call(f32[48,128]{1,0:T(8,128)S(1)} %bitcast_add_fusion.refs_0_, f32[48,128]{1,0:T(8,128)S(1)} %collective-permute-done.13.refs_1_, bf16[128,128]{1,0:T(8,128)(2,1)S(1)} %copy-done.3, f32[1,128]{1,0:T(1,128)S(1)} %bitcast.61), custom_call_target="tpu_custom_call" | custom-call | flops 1 | bytes 1 | tf_op jit(solution)/shard_map/weights/pallas_call | solution.py:366
  (10 shorter events, 0.1 us)
Async XLA Ops:
  0.6 13.2 %copy-start.3 = (bf16[128,128]{1,0:T(8,128)(2,1)S(1)}, bf16[128,128]{1,0:T(8,128)(2,1)}, u32[]{:S(2)}) copy-start(bf16[128,128]{1,0:T(8,128)(2,1)} %refs_2_.7) | copy-start | bytes 98308
  0.6 13.2 %copy-start.5 = (bf16[128,128]{1,0:T(8,128)(2,1)S(1)}, bf16[128,128]{1,0:T(8,128)(2,1)}, u32[]{:S(2)}) copy-start(bf16[128,128]{1,0:T(8,128)(2,1)} %refs_3_.1) | copy-start | bytes 98308
  0.7 13.2 %copy-start.6 = (bf16[128,128]{1,0:T(8,128)(2,1)S(1)}, bf16[128,128]{1,0:T(8,128)(2,1)}, u32[]{:S(2)}) copy-start(bf16[128,128]{1,0:T(8,128)(2,1)} %refs_6_.3) | copy-start | bytes 98308
  0.7 13.2 %copy-start = (bf16[1,1,4,2048,128]{4,3,2,1,0:T(8,128)(2,1)S(1)}, bf16[1,1,4,2048,128]{4,3,2,1,0:T(8,128)(2,1)}, u32[]{:S(2)}) copy-start(bf16[1,1,4,2048,128]{4,3,2,1,0:T(8,128)(2,1)} %param.18) | copy-start | bytes 6291460
  0.7 13.2 %copy-start.7 = (s32[1,4,4]{2,1,0:T(4,128)S(1)}, s32[1,4,4]{2,1,0:T(4,128)}, u32[]{:S(2)}) copy-start(s32[1,4,4]{2,1,0:T(4,128)} %param.17) | copy-start | bytes 196
  0.7 13.2 %copy-start.4 = (s32[1,1,4,2048]{3,2,1,0:T(4,128)S(1)}, s32[1,1,4,2048]{3,2,1,0:T(4,128)}, u32[]{:S(2)}) copy-start(s32[1,1,4,2048]{3,2,1,0:T(4,128)} %param.15) | copy-start | bytes 98308
  0.7 13.2 %copy-start.8 = (f32[128]{0:T(128)S(1)}, f32[128]{0:T(128)}, u32[]{:S(2)}) copy-start(f32[128]{0:T(128)} %param.11) | copy-start | bytes 1540
  0.7 13.2 %copy-start.1 = (bf16[1,1,1024,128]{3,2,1,0:T(8,128)(2,1)S(1)}, bf16[1,1,1024,128]{3,2,1,0:T(8,128)(2,1)}, u32[]{:S(2)}) copy-start(bf16[1,1,1024,128]{3,2,1,0:T(8,128)(2,1)} %param.10) | copy-start | bytes 786436
  0.7 4.5 %collective-permute-start.2 = (bf16[1024,128]{1,0:T(8,128)(2,1)}, bf16[1024,128]{1,0:T(8,128)(2,1)S(1)}, u32[]{:S(2)}, u32[]{:S(2)}) collective-permute-start(bf16[1024,128]{1,0:T(8,128)(2,1)} %bitcast.46), channel_id=1, source_target_pairs={{0,1},{1,0},{2,3},{3,2},{4,5},{5,4},{6,7},{7,6},{8,9},{9,8},{10,11... | collective-permute-start | bytes 786440 | tf_op jit(solution)/shard_map/ppermute | solution.py:308
  1.2 10.9 %collective-permute-start = (bf16[1024,128]{1,0:T(8,128)(2,1)}, bf16[1024,128]{1,0:T(8,128)(2,1)S(1)}, u32[]{:S(2)}, u32[]{:S(2)}) collective-permute-start(bf16[1024,128]{1,0:T(8,128)(2,1)} %bitcast.47), channel_id=1, source_target_pairs={{0,2},{1,3},{2,0},{3,1},{4,6},{5,7},{6,4},{7,5},{8,10},{9,11},{10,... | collective-permute-start | bytes 786440 | tf_op jit(solution)/shard_map/ppermute | solution.py:308
  3.8 1.4 %collective-permute-start.3 = (s32[4,2048]{1,0:T(4,128)}, s32[4,2048]{1,0:T(4,128)S(1)}, u32[]{:S(2)}, u32[]{:S(2)}) collective-permute-start(s32[4,2048]{1,0:T(4,128)} %bitcast.69), channel_id=1, source_target_pairs={{0,1},{1,0},{2,3},{3,2},{4,5},{5,4},{6,7},{7,6},{8,9},{9,8},{10,11... | collective-permute-start | bytes 98312 | tf_op jit(solution)/shard_map/ppermute | solution.py:308
  4.0 8.2 %collective-permute-start.1 = (s32[4,2048]{1,0:T(4,128)}, s32[4,2048]{1,0:T(4,128)S(1)}, u32[]{:S(2)}, u32[]{:S(2)}) collective-permute-start(s32[4,2048]{1,0:T(4,128)} %bitcast.70), channel_id=1, source_target_pairs={{0,2},{1,3},{2,0},{3,1},{4,6},{5,7},{6,4},{7,5},{8,10},{9,11},{10,... | collective-permute-start | bytes 98312 | tf_op jit(solution)/shard_map/ppermute | solution.py:308
  5.2 0.6 %copy-start.13 = (s32[4,2048]{1,0:T(4,128)}, s32[4,2048]{1,0:T(4,128)S(1)}, u32[]{:S(2)}) copy-start(s32[4,2048]{1,0:T(4,128)S(1)} %collective-permute-done.3.refs_10_) | copy-start | bytes 98308
  5.2 0.7 %copy-start.10 = (bf16[1024,128]{1,0:T(8,128)(2,1)}, bf16[1024,128]{1,0:T(8,128)(2,1)S(1)}, u32[]{:S(2)}) copy-start(bf16[1024,128]{1,0:T(8,128)(2,1)S(1)} %collective-permute-done.2.refs_4_) | copy-start | bytes 786436
  12.2 7.1 %copy-start.12 = (f32[8,48,128]{2,1,0:T(8,128)S(1)}, f32[8,48,128]{2,1,0:T(8,128)}, u32[]{:S(2)}) copy-start(f32[8,48,128]{2,1,0:T(8,128)} %get-tuple-element.36) | copy-start | bytes 589828
  12.2 8.7 %copy-start.14 = (bf16[128,1024]{1,0:T(8,128)(2,1)S(1)}, bf16[128,1024]{1,0:T(8,128)(2,1)}, u32[]{:S(2)}) copy-start(bf16[128,1024]{1,0:T(8,128)(2,1)} %get-tuple-element.53) | copy-start | bytes 786436
  12.2 9.2 %copy-start.9 = (bf16[2,128,2048]{2,1,0:T(8,128)(2,1)S(1)}, bf16[2,128,2048]{2,1,0:T(8,128)(2,1)}, u32[]{:S(2)}) copy-start(bf16[2,128,2048]{2,1,0:T(8,128)(2,1)} %get-tuple-element.41.refs_2_) | copy-start | bytes 3145732
  12.2 1.7 %collective-permute-start.4 = (bf16[1024,128]{1,0:T(8,128)(2,1)S(1)}, bf16[1024,128]{1,0:T(8,128)(2,1)S(1)}, u32[]{:S(2)}, u32[]{:S(2)}) collective-permute-start(bf16[1024,128]{1,0:T(8,128)(2,1)S(1)} %collective-permute-done.refs_3_), channel_id=1, source_target_pairs={{0,1},{1,0},{2,3},{3,2},{4,5},{5,4},{6,7},{7,6},{8,9},{9,8},{10,11... | collective-permute-start | bytes 786440 | tf_op jit(solution)/shard_map/ppermute | solution.py:308
  12.4 1.4 %collective-permute-start.5 = (s32[4,2048]{1,0:T(4,128)S(1)}, s32[4,2048]{1,0:T(4,128)S(1)}, u32[]{:S(2)}, u32[]{:S(2)}) collective-permute-start(s32[4,2048]{1,0:T(4,128)S(1)} %collective-permute-done.1.refs_9_), channel_id=1, source_target_pairs={{0,1},{1,0},{2,3},{3,2},{4,5},{5,4},{6,7},{7,6},{8,9},{9,8},{10,11... | collective-permute-start | bytes 98312 | tf_op jit(solution)/shard_map/ppermute | solution.py:308
  19.3 4.9 %collective-permute-start.6 = (f32[4,48,128]{2,1,0:T(8,128)S(1)}, f32[4,48,128]{2,1,0:T(8,128)S(1)}, u32[]{:S(2)}, u32[]{:S(2)}) collective-permute-start(f32[4,48,128]{2,1,0:T(8,128)S(1)} %slice_bitcast_fusion), channel_id=1, source_target_pairs={{0,4},{4,0},{8,12},{12,8},{16,20},{20,16},{24,28},{28,24},{1,5},{5... | collective-permute-start | bytes 294920 | tf_op jit(solution)/shard_map/ppermute | solution.py:308
  20.9 14.5 %collective-permute-start.12 = (bf16[128,1024]{1,0:T(8,128)(2,1)S(1)}, bf16[128,1024]{1,0:T(8,128)(2,1)S(1)}, u32[]{:S(2)}, u32[]{:S(2)}) collective-permute-start(bf16[128,1024]{1,0:T(8,128)(2,1)S(1)} %copy-done.14), channel_id=1, source_target_pairs={{0,1},{1,0},{2,3},{3,2},{4,5},{5,4},{6,7},{7,6},{8,9},{9,8},{10,11... | collective-permute-start | bytes 786440 | tf_op jit(solution)/shard_map/ppermute | solution.py:308
  20.9 3.4 %collective-permute-start.7 = (bf16[128,1024]{1,0:T(8,128)(2,1)S(1)}, bf16[128,1024]{1,0:T(8,128)(2,1)S(1)}, u32[]{:S(2)}, u32[]{:S(2)}) collective-permute-start(bf16[128,1024]{1,0:T(8,128)(2,1)S(1)} %get-tuple-element.40), channel_id=1, source_target_pairs={{0,1},{1,0},{2,3},{3,2},{4,5},{5,4},{6,7},{7,6},{8,9},{9,8},{10,11... | collective-permute-start | bytes 786440 | tf_op jit(solution)/shard_map/ppermute | solution.py:308
  23.0 12.4 %copy-start.11 = (bf16[128,1024]{1,0:T(8,128)(2,1)S(1)}, bf16[128,1024]{1,0:T(8,128)(2,1)}, u32[]{:S(2)}) copy-start(bf16[128,1024]{1,0:T(8,128)(2,1)} %get-tuple-element.52) | copy-start | bytes 786436
  24.3 5.8 %collective-permute-start.8 = (f32[2,48,128]{2,1,0:T(8,128)S(1)}, f32[2,48,128]{2,1,0:T(8,128)S(1)}, u32[]{:S(2)}, u32[]{:S(2)}) collective-permute-start(f32[2,48,128]{2,1,0:T(8,128)S(1)} %slice_bitcast_fusion.2), channel_id=1, source_target_pairs={{0,8},{4,12},{8,0},{12,4},{16,24},{20,28},{24,16},{28,20},{1,9},{5... | collective-permute-start | bytes 147464 | tf_op jit(solution)/shard_map/ppermute | solution.py:308
  25.9 9.6 %copy-start.2 = (bf16[1,1,1024,128]{3,2,1,0:T(8,128)(2,1)S(1)}, bf16[1,1,1024,128]{3,2,1,0:T(8,128)(2,1)}, u32[]{:S(2)}) copy-start(bf16[1,1,1024,128]{3,2,1,0:T(8,128)(2,1)} %param.19) | copy-start | bytes 786436
  26.0 8.9 %collective-permute-start.10 = (bf16[128,1024]{1,0:T(8,128)(2,1)S(1)}, bf16[128,1024]{1,0:T(8,128)(2,1)S(1)}, u32[]{:S(2)}, u32[]{:S(2)}) collective-permute-start(bf16[128,1024]{1,0:T(8,128)(2,1)S(1)} %add_convert_fusion), channel_id=1, source_target_pairs={{0,2},{1,3},{2,0},{3,1},{4,6},{5,7},{6,4},{7,5},{8,10},{9,11},{10,... | collective-permute-start | bytes 786440 | tf_op jit(solution)/shard_map/ppermute | solution.py:308
  30.1 4.8 %collective-permute-start.9 = (f32[1,48,128]{2,1,0:T(8,128)S(1)}, f32[1,48,128]{2,1,0:T(8,128)S(1)}, u32[]{:S(2)}, u32[]{:S(2)}) collective-permute-start(f32[1,48,128]{2,1,0:T(8,128)S(1)} %slice_bitcast_fusion.4), channel_id=1, source_target_pairs={{0,16},{4,20},{8,24},{12,28},{16,0},{20,4},{24,8},{28,12},{1,17},{... | collective-permute-start | bytes 73736 | tf_op jit(solution)/shard_map/ppermute | solution.py:308
  34.9 3.9 %collective-permute-start.11 = (f32[48,128]{1,0:T(8,128)S(1)}, f32[48,128]{1,0:T(8,128)S(1)}, u32[]{:S(2)}, u32[]{:S(2)}) collective-permute-start(f32[48,128]{1,0:T(8,128)S(1)} %bitcast.68), channel_id=1, source_target_pairs={{0,2},{1,3},{2,0},{3,1},{4,6},{5,7},{6,4},{7,5},{8,10},{9,11},{10,... | collective-permute-start | bytes 73736 | tf_op jit(solution)/shard_map/ppermute | solution.py:308
  38.8 1.2 %collective-permute-start.13 = (f32[48,128]{1,0:T(8,128)S(1)}, f32[48,128]{1,0:T(8,128)S(1)}, u32[]{:S(2)}, u32[]{:S(2)}) collective-permute-start(f32[48,128]{1,0:T(8,128)S(1)} %bitcast_add_fusion.refs_0_), channel_id=1, source_target_pairs={{0,1},{1,0},{2,3},{3,2},{4,5},{5,4},{6,7},{7,6},{8,9},{9,8},{10,11... | collective-permute-start | bytes 73736 | tf_op jit(solution)/shard_map/ppermute | solution.py:308

commit v5 on v4

--- a/solution.py
+++ b/solution.py
@@ -92,12 +92,19 @@
             part.take()
         return self.held
 
+    def take_first(self):
+        self.parts[0].take()
+        return self.held
+
 
 class Held:
     def __init__(self, held):
         self.held = held
 
     def take(self):
+        return self.held
+
+    def take_first(self):
         return self.held
 
 
@@ -187,15 +194,27 @@
     agg_sum[...] = jnp.zeros_like(agg_sum)
     row_sum[...] = jnp.zeros_like(row_sum)
     edge_sum[...] = jnp.zeros_like(edge_sum)
-    atoms, gain, w_out, cots = atoms.take(), gain.take(), w_out.take(), cots.take()
-    cots = [cots[i][...] for i in range(len(ks))]
+    atoms, gain, w_out = atoms.take(), gain.take(), w_out.take()
+    first_cot = cots.take_first()[0][...]
     w_src_t, w_edge_t = w_src.take()[...].T, w_edge.take()[...].T
     feats, inv = norm_parts(atoms[...])
     table[...] = stack_groups((feats * inv * column(gain)).astype(BF16), groups)
-    for i in range(len(ks)):
-        back[i] = back_table(w_out, cots[i], groups)
-    counts, src, dsts, edges = counts.take(), src.take(), dsts.take(), edges.take()
+    back[0] = back_table(w_out, first_cot, groups)
+    counts, src = counts.take(), src.take()
+    late_dsts, late_edges = dsts, edges
+    dsts, edges = dsts.take_first(), edges.take_first()
     whole = edges.shape[0] != len(ks)
+    ready = isinstance(late_edges, Held)
+
+    def take_rest():
+        late_dsts.take()
+        late_edges.take()
+        held_cots = cots.take()
+        for i in range(1, len(ks)):
+            back[i] = back_table(w_out, held_cots[i][...], groups)
+
+    if ready:
+        take_rest()
     me = lax.axis_index("graph")
     total, locate = block_finder(ks, counts)
 
@@ -236,6 +255,9 @@
     def _():
         put(0, *gather(0))
 
+    if not ready:
+        take_rest()
+
     lax.fori_loop(1, total, step, 0)
 
     @pl.when(total > 0)
@@ -246,7 +268,7 @@
     for i in range(len(ks)):
         part = (unstack_groups(agg_sum[i], groups) * (1.0 / DEG_NORM)).astype(BF16)
         (part_a, part_b)[i][...] = part
-        grad_out = grad_out + dot(part, cots[i])
+        grad_out = grad_out + dot(part, cots.take()[i][...])
     batches = chunks.shape[0]
     rows = chans // batches
     left = chunks.shape[1] - 3 * rows

time: 41 us -> 41.1 us (level)
  waiting for transfers between devices: 9.05 us -> 9.51 us
    ppermute x14, waiting for transfers between devices: 9.05 us -> 9.51 us  [move(): return lax.ppermute(x, axis, [(i, i ^ bit) for i in range(size)])]
  transfers between devices with their start and end apart: 14 -> 14, of which waited for: 6 -> 6; matrix products, arithmetic and copies ran while one was open for 0% -> 0% of each run, Pallas kernels for 28% -> 27%
where the time goes in v5:
time: 41.1 us; the launch traced here: 41.2 us
  Pallas kernels  17.5 us (43%)
  starting transfers between devices  12.3 us (30%)
  waiting for transfers between devices  9.51 us (23%)
  between operations  0.94 us (2%)
  local copies, waits for them, and re-layouts  0.78 us (2%)
    pallas_call x6, Pallas kernels, call(): pl.pallas_call(functools.partial(with_fetches, kernel, kinds, ks, len(out...  17.5 us
    ppermute x14, starting transfers between devices, move(): return lax.ppermute(x, axis, [(i, i ^ bit) for i in range(size)])  12.3 us
    ppermute x14, waiting for transfers between devices, move(): return lax.ppermute(x, axis, [(i, i ^ bit) for i in range(size)])  9.51 us
  transfers between devices with their start and end apart: 14, of which 6 were waited for; matrix products, arithmetic and copies ran while one was open for 0% of the time, Pallas kernels for 27%

profile of v5, /device:TPU:0, one launch (start us, length us, event | category | flops | bytes accessed | tf_op | source)
XLA Modules:
  0.0 41.2 jit_solution(7149260465021182203)
XLA Ops:
  0.6 0.0 copy-start.3
  0.6 0.0 copy-start.5
  0.7 0.0 copy-start.6
  0.7 0.0 copy-start
  0.7 0.0 copy-start.7
  0.7 0.0 copy-start.4
  0.7 0.0 copy-start.8
  0.7 0.0 copy-start.1
  0.7 0.5 %collective-permute-start.2 = (bf16[1024,128]{1,0:T(8,128)(2,1)}, bf16[1024,128]{1,0:T(8,128)(2,1)S(1)}, u32[]{:S(2)}, u32[]{:S(2)}) collective-permute-start(bf16[1024,128]{1,0:T(8,128)(2,1)} %bitcast.46), channel_id=1, source_target_pairs={{0,1},{1,0},{2,3},{3,2},{4,5},{5,4},{6,7},{7,6},{8,9},{9,8},{10,11... | collective-permute-start | bytes 786440 | tf_op jit(solution)/shard_map/ppermute | solution.py:330
  1.2 2.6 %collective-permute-start = (bf16[1024,128]{1,0:T(8,128)(2,1)}, bf16[1024,128]{1,0:T(8,128)(2,1)S(1)}, u32[]{:S(2)}, u32[]{:S(2)}) collective-permute-start(bf16[1024,128]{1,0:T(8,128)(2,1)} %bitcast.47), channel_id=1, source_target_pairs={{0,2},{1,3},{2,0},{3,1},{4,6},{5,7},{6,4},{7,5},{8,10},{9,11},{10,... | collective-permute-start | bytes 786440 | tf_op jit(solution)/shard_map/ppermute | solution.py:330
  3.8 0.2 collective-permute-start.3
  4.0 0.3 collective-permute-start.1
  4.2 1.0 %collective-permute-done.3.refs_10_ = s32[4,2048]{1,0:T(4,128)S(1)} collective-permute-done((s32[4,2048]{1,0:T(4,128)}, s32[4,2048]{1,0:T(4,128)S(1)}, u32[]{:S(2)}, u32[]{:S(2)}) %collective-permute-start.3) | collective-permute-done | bytes 32800 | tf_op jit(solution)/shard_map/ppermute | solution.py:330
  5.2 0.0 copy-start.13
  5.2 0.0 collective-permute-done.2.refs_4_
  5.2 0.6 %copy-done.13 = s32[4,2048]{1,0:T(4,128)} copy-done((s32[4,2048]{1,0:T(4,128)}, s32[4,2048]{1,0:T(4,128)S(1)}, u32[]{:S(2)}) %copy-start.13) | copy-done | bytes 32792
  5.8 0.1 copy-done.10
  5.9 6.2 %near_edges.1 = (bf16[128,1024]{1,0:T(8,128)(2,1)}, bf16[128,1024]{1,0:T(8,128)(2,1)}, f32[8,48,128]{2,1,0:T(8,128)}, bf16[2,128,2048]{2,1,0:T(8,128)(2,1)}) custom-call(bf16[1024,128]{1,0:T(8,128)(2,1)} %bitcast.43, f32[1,128]{1,0:T(1,128)} %bitcast.58, bf16[128,128]{1,0:T(8,128)(2,1)} %refs_3_.1, bf16[1024,128]{1,0:T(8,128)(2,1)} %bitcast.48, ...), custom_call_target="tpu_custom_call" | custom-call | flops 1 | bytes 1 | tf_op jit(solution)/shard_map/near_edges/pallas_call | solution.py:388
  12.1 0.0 collective-permute-done.1.refs_9_
  12.1 0.0 collective-permute-done.refs_3_
  12.1 0.0 copy-start.12
  12.2 0.0 copy-start.14
  12.2 0.0 copy-start.9
  12.2 0.2 collective-permute-start.4
  12.4 0.3 collective-permute-start.5
  12.8 1.1 %collective-permute-done.5.refs_10_ = s32[4,2048]{1,0:T(4,128)S(1)} collective-permute-done((s32[4,2048]{1,0:T(4,128)S(1)}, s32[4,2048]{1,0:T(4,128)S(1)}, u32[]{:S(2)}, u32[]{:S(2)}) %collective-permute-start.5) | collective-permute-done | bytes 32800 | tf_op jit(solution)/shard_map/ppermute | solution.py:330
  13.8 0.0 collective-permute-done.4.refs_4_
  13.8 0.0 copy-done.3
  13.8 0.0 copy-done.5
  13.8 0.0 copy-done.6
  13.8 0.0 copy-done
  13.9 0.0 copy-done.7
  13.9 0.0 copy-done.4
  13.9 0.0 copy-done.8
  13.9 0.0 copy-done.1
  13.9 5.5 %far_edges.1 = (bf16[128,1024]{1,0:T(8,128)(2,1)S(1)}, bf16[128,1024]{1,0:T(8,128)(2,1)S(1)}, f32[8,48,128]{2,1,0:T(8,128)S(1)}, bf16[2,128,2048]{2,1,0:T(8,128)(2,1)S(1)}) custom-call(bf16[1024,128]{1,0:T(8,128)(2,1)S(1)} %bitcast.44, f32[1,128]{1,0:T(1,128)S(1)} %bitcast.59, bf16[128,128]{1,0:T(8,128)(2,1)S(1)} %copy-done.5, ...), custom_call_target="tpu_custom_call" | custom-call | flops 4294967296 | bytes 1048576 | tf_op jit(solution)/shard_map/far_edges/pallas_call | solution.py:388
  19.4 0.0 copy-done.12
  19.4 1.6 %collective-permute-start.6 = (f32[4,48,128]{2,1,0:T(8,128)S(1)}, f32[4,48,128]{2,1,0:T(8,128)S(1)}, u32[]{:S(2)}, u32[]{:S(2)}) collective-permute-start(f32[4,48,128]{2,1,0:T(8,128)S(1)} %slice_bitcast_fusion), channel_id=1, source_target_pairs={{0,4},{4,0},{8,12},{12,8},{16,20},{20,16},{24,28},{28,24},{1,5},{5... | collective-permute-start | bytes 294920 | tf_op jit(solution)/shard_map/ppermute | solution.py:330
  21.1 0.0 copy-done.14
  21.1 0.0 collective-permute-start.12
  21.1 0.5 %collective-permute-start.7 = (bf16[128,1024]{1,0:T(8,128)(2,1)S(1)}, bf16[128,1024]{1,0:T(8,128)(2,1)S(1)}, u32[]{:S(2)}, u32[]{:S(2)}) collective-permute-start(bf16[128,1024]{1,0:T(8,128)(2,1)S(1)} %get-tuple-element.40), channel_id=1, source_target_pairs={{0,1},{1,0},{2,3},{3,2},{4,5},{5,4},{6,7},{7,6},{8,9},{9,8},{10,11... | collective-permute-start | bytes 786440 | tf_op jit(solution)/shard_map/ppermute | solution.py:330
  21.6 0.0 copy-done.9
  21.6 1.6 %near_sources.1.refs_3_ = f32[512,256]{1,0:T(8,128)S(1)} custom-call(s32[4,4]{1,0:T(4,128)S(1)} %bitcast.56, s32[4,2048]{1,0:T(4,128)S(1)} %bitcast.52, bf16[2,128,2048]{2,1,0:T(8,128)(2,1)S(1)} %copy-done.9), custom_call_target="tpu_custom_call" | custom-call | flops 536870912 | bytes 1048576 | tf_op jit(solution)/shard_map/near_sources/pallas_call | solution.py:388
  23.2 0.0 copy-start.11
  23.2 1.2 %collective-permute-done.6 = f32[4,48,128]{2,1,0:T(8,128)S(1)} collective-permute-done((f32[4,48,128]{2,1,0:T(8,128)S(1)}, f32[4,48,128]{2,1,0:T(8,128)S(1)}, u32[]{:S(2)}, u32[]{:S(2)}) %collective-permute-start.6) | collective-permute-done | bytes 98336 | tf_op jit(solution)/shard_map/ppermute | solution.py:330
  24.4 0.0 collective-permute-done.7
  24.4 1.6 %collective-permute-start.8 = (f32[2,48,128]{2,1,0:T(8,128)S(1)}, f32[2,48,128]{2,1,0:T(8,128)S(1)}, u32[]{:S(2)}, u32[]{:S(2)}) collective-permute-start(f32[2,48,128]{2,1,0:T(8,128)S(1)} %slice_bitcast_fusion.2), channel_id=1, source_target_pairs={{0,8},{4,12},{8,0},{12,4},{16,24},{20,28},{24,16},{28,20},{1,9},{5... | collective-permute-start | bytes 147464 | tf_op jit(solution)/shard_map/ppermute | solution.py:330
  26.0 0.1 add_convert_fusion
  26.1 2.1 %collective-permute-start.10 = (bf16[128,1024]{1,0:T(8,128)(2,1)S(1)}, bf16[128,1024]{1,0:T(8,128)(2,1)S(1)}, u32[]{:S(2)}, u32[]{:S(2)}) collective-permute-start(bf16[128,1024]{1,0:T(8,128)(2,1)S(1)} %add_convert_fusion), channel_id=1, source_target_pairs={{0,2},{1,3},{2,0},{3,1},{4,6},{5,7},{6,4},{7,5},{8,10},{9,11},{10,... | collective-permute-start | bytes 786440 | tf_op jit(solution)/shard_map/ppermute | solution.py:330
  28.3 2.1 %far_sources.1.refs_5_ = f32[512,256]{1,0:T(8,128)S(1)} custom-call(s32[4,4]{1,0:T(4,128)S(1)} %bitcast.57, s32[4,2048]{1,0:T(4,128)S(1)} %bitcast.53, bf16[2,128,2048]{2,1,0:T(8,128)(2,1)S(1)} %get-tuple-element.45.refs_2_, f32[512,256]{1,0:T(8,128)S(1)} %near_sources.1.refs_3_), custom_call_target="tpu_custom_call" | custom-call | flops 536870912 | bytes 1048576 | tf_op jit(solution)/shard_map/far_sources/pallas_call | solution.py:388
  30.4 0.0 collective-permute-done.8
  30.4 1.9 %collective-permute-start.9 = (f32[1,48,128]{2,1,0:T(8,128)S(1)}, f32[1,48,128]{2,1,0:T(8,128)S(1)}, u32[]{:S(2)}, u32[]{:S(2)}) collective-permute-start(f32[1,48,128]{2,1,0:T(8,128)S(1)} %slice_bitcast_fusion.4), channel_id=1, source_target_pairs={{0,16},{4,20},{8,24},{12,28},{16,0},{20,4},{24,8},{28,12},{1,17},{... | collective-permute-start | bytes 73736 | tf_op jit(solution)/shard_map/ppermute | solution.py:330
  32.3 3.0 %collective-permute-done.9 = f32[1,48,128]{2,1,0:T(8,128)S(1)} collective-permute-done((f32[1,48,128]{2,1,0:T(8,128)S(1)}, f32[1,48,128]{2,1,0:T(8,128)S(1)}, u32[]{:S(2)}, u32[]{:S(2)}) %collective-permute-start.9) | collective-permute-done | bytes 24608 | tf_op jit(solution)/shard_map/ppermute | solution.py:330
  35.3 0.0 collective-permute-done.10.refs_7_
  35.4 0.4 collective-permute-start.11
  35.8 0.0 collective-permute-done.12
  35.8 0.0 copy-done.11
  35.8 0.1 convert_add_fusion.refs_6_
  35.8 0.0 copy-done.2
  35.8 1.4 %atoms.1 = (bf16[1024,128]{1,0:T(8,128)(2,1)}, bf16[1024,128]{1,0:T(8,128)(2,1)}) custom-call(bf16[1024,128]{1,0:T(8,128)(2,1)S(1)} %bitcast.45, f32[1,128]{1,0:T(1,128)S(1)} %bitcast.60, bf16[128,128]{1,0:T(8,128)(2,1)S(1)} %copy-done.3, bf16[128,128]{1,0:T(8,128)(2,1)S(1)} %copy-done.5, bf16[1024,128]{1,0:T(8,128)(2,1)S(1)} %bitcast.49, ...), custom_call_target="tpu_custom_call" | custom-call | flops 67108864 | bytes 1048576 | tf_op jit(solution)/shard_map/atoms/pallas_call | solution.py:388
  37.2 2.0 %collective-permute-done.11 = f32[48,128]{1,0:T(8,128)S(1)} collective-permute-done((f32[48,128]{1,0:T(8,128)S(1)}, f32[48,128]{1,0:T(8,128)S(1)}, u32[]{:S(2)}, u32[]{:S(2)}) %collective-permute-start.11) | collective-permute-done | bytes 24608 | tf_op jit(solution)/shard_map/ppermute | solution.py:330
  39.2 0.0 collective-permute-start.13
  39.3 1.2 %collective-permute-done.13.refs_1_ = f32[48,128]{1,0:T(8,128)S(1)} collective-permute-done((f32[48,128]{1,0:T(8,128)S(1)}, f32[48,128]{1,0:T(8,128)S(1)}, u32[]{:S(2)}, u32[]{:S(2)}) %collective-permute-start.13) | collective-permute-done | bytes 24608 | tf_op jit(solution)/shard_map/ppermute | solution.py:330
  40.4 0.7 %weights.1 = (f32[16,128]{1,0:T(8,128)}, f32[16,128]{1,0:T(8,128)}, f32[16,128]{1,0:T(8,128)}, f32[1,16]{1,0:T(1,128)}) custom-call(f32[48,128]{1,0:T(8,128)S(1)} %bitcast_add_fusion.refs_0_, f32[48,128]{1,0:T(8,128)S(1)} %collective-permute-done.13.refs_1_, bf16[128,128]{1,0:T(8,128)(2,1)S(1)} %copy-done.3, f32[1,128]{1,0:T(1,128)S(1)} %bitcast.61), custom_call_target="tpu_custom_call" | custom-call | flops 1 | bytes 1 | tf_op jit(solution)/shard_map/weights/pallas_call | solution.py:388
  (10 shorter events, 0.1 us)
Async XLA Ops:
  0.6 13.2 %copy-start.3 = (bf16[128,128]{1,0:T(8,128)(2,1)S(1)}, bf16[128,128]{1,0:T(8,128)(2,1)}, u32[]{:S(2)}) copy-start(bf16[128,128]{1,0:T(8,128)(2,1)} %refs_2_.7) | copy-start | bytes 98308
  0.6 13.2 %copy-start.5 = (bf16[128,128]{1,0:T(8,128)(2,1)S(1)}, bf16[128,128]{1,0:T(8,128)(2,1)}, u32[]{:S(2)}) copy-start(bf16[128,128]{1,0:T(8,128)(2,1)} %refs_3_.1) | copy-start | bytes 98308
  0.7 13.2 %copy-start.6 = (bf16[128,128]{1,0:T(8,128)(2,1)S(1)}, bf16[128,128]{1,0:T(8,128)(2,1)}, u32[]{:S(2)}) copy-start(bf16[128,128]{1,0:T(8,128)(2,1)} %refs_6_.3) | copy-start | bytes 98308
  0.7 13.2 %copy-start = (bf16[1,1,4,2048,128]{4,3,2,1,0:T(8,128)(2,1)S(1)}, bf16[1,1,4,2048,128]{4,3,2,1,0:T(8,128)(2,1)}, u32[]{:S(2)}) copy-start(bf16[1,1,4,2048,128]{4,3,2,1,0:T(8,128)(2,1)} %param.18) | copy-start | bytes 6291460
  0.7 13.2 %copy-start.7 = (s32[1,4,4]{2,1,0:T(4,128)S(1)}, s32[1,4,4]{2,1,0:T(4,128)}, u32[]{:S(2)}) copy-start(s32[1,4,4]{2,1,0:T(4,128)} %param.17) | copy-start | bytes 196
  0.7 13.2 %copy-start.4 = (s32[1,1,4,2048]{3,2,1,0:T(4,128)S(1)}, s32[1,1,4,2048]{3,2,1,0:T(4,128)}, u32[]{:S(2)}) copy-start(s32[1,1,4,2048]{3,2,1,0:T(4,128)} %param.15) | copy-start | bytes 98308
  0.7 13.2 %copy-start.8 = (f32[128]{0:T(128)S(1)}, f32[128]{0:T(128)}, u32[]{:S(2)}) copy-start(f32[128]{0:T(128)} %param.11) | copy-start | bytes 1540
  0.7 13.2 %copy-start.1 = (bf16[1,1,1024,128]{3,2,1,0:T(8,128)(2,1)S(1)}, bf16[1,1,1024,128]{3,2,1,0:T(8,128)(2,1)}, u32[]{:S(2)}) copy-start(bf16[1,1,1024,128]{3,2,1,0:T(8,128)(2,1)} %param.10) | copy-start | bytes 786436
  0.7 4.5 %collective-permute-start.2 = (bf16[1024,128]{1,0:T(8,128)(2,1)}, bf16[1024,128]{1,0:T(8,128)(2,1)S(1)}, u32[]{:S(2)}, u32[]{:S(2)}) collective-permute-start(bf16[1024,128]{1,0:T(8,128)(2,1)} %bitcast.46), channel_id=1, source_target_pairs={{0,1},{1,0},{2,3},{3,2},{4,5},{5,4},{6,7},{7,6},{8,9},{9,8},{10,11... | collective-permute-start | bytes 786440 | tf_op jit(solution)/shard_map/ppermute | solution.py:330
  1.2 10.9 %collective-permute-start = (bf16[1024,128]{1,0:T(8,128)(2,1)}, bf16[1024,128]{1,0:T(8,128)(2,1)S(1)}, u32[]{:S(2)}, u32[]{:S(2)}) collective-permute-start(bf16[1024,128]{1,0:T(8,128)(2,1)} %bitcast.47), channel_id=1, source_target_pairs={{0,2},{1,3},{2,0},{3,1},{4,6},{5,7},{6,4},{7,5},{8,10},{9,11},{10,... | collective-permute-start | bytes 786440 | tf_op jit(solution)/shard_map/ppermute | solution.py:330
  3.8 1.4 %collective-permute-start.3 = (s32[4,2048]{1,0:T(4,128)}, s32[4,2048]{1,0:T(4,128)S(1)}, u32[]{:S(2)}, u32[]{:S(2)}) collective-permute-start(s32[4,2048]{1,0:T(4,128)} %bitcast.69), channel_id=1, source_target_pairs={{0,1},{1,0},{2,3},{3,2},{4,5},{5,4},{6,7},{7,6},{8,9},{9,8},{10,11... | collective-permute-start | bytes 98312 | tf_op jit(solution)/shard_map/ppermute | solution.py:330
  4.0 8.2 %collective-permute-start.1 = (s32[4,2048]{1,0:T(4,128)}, s32[4,2048]{1,0:T(4,128)S(1)}, u32[]{:S(2)}, u32[]{:S(2)}) collective-permute-start(s32[4,2048]{1,0:T(4,128)} %bitcast.70), channel_id=1, source_target_pairs={{0,2},{1,3},{2,0},{3,1},{4,6},{5,7},{6,4},{7,5},{8,10},{9,11},{10,... | collective-permute-start | bytes 98312 | tf_op jit(solution)/shard_map/ppermute | solution.py:330
  5.2 0.6 %copy-start.13 = (s32[4,2048]{1,0:T(4,128)}, s32[4,2048]{1,0:T(4,128)S(1)}, u32[]{:S(2)}) copy-start(s32[4,2048]{1,0:T(4,128)S(1)} %collective-permute-done.3.refs_10_) | copy-start | bytes 98308
  5.2 0.7 %copy-start.10 = (bf16[1024,128]{1,0:T(8,128)(2,1)}, bf16[1024,128]{1,0:T(8,128)(2,1)S(1)}, u32[]{:S(2)}) copy-start(bf16[1024,128]{1,0:T(8,128)(2,1)S(1)} %collective-permute-done.2.refs_4_) | copy-start | bytes 786436
  12.1 7.2 %copy-start.12 = (f32[8,48,128]{2,1,0:T(8,128)S(1)}, f32[8,48,128]{2,1,0:T(8,128)}, u32[]{:S(2)}) copy-start(f32[8,48,128]{2,1,0:T(8,128)} %get-tuple-element.36) | copy-start | bytes 589828
  12.2 8.9 %copy-start.14 = (bf16[128,1024]{1,0:T(8,128)(2,1)S(1)}, bf16[128,1024]{1,0:T(8,128)(2,1)}, u32[]{:S(2)}) copy-start(bf16[128,1024]{1,0:T(8,128)(2,1)} %get-tuple-element.53) | copy-start | bytes 786436
  12.2 9.4 %copy-start.9 = (bf16[2,128,2048]{2,1,0:T(8,128)(2,1)S(1)}, bf16[2,128,2048]{2,1,0:T(8,128)(2,1)}, u32[]{:S(2)}) copy-start(bf16[2,128,2048]{2,1,0:T(8,128)(2,1)} %get-tuple-element.41.refs_2_) | copy-start | bytes 3145732
  12.2 1.7 %collective-permute-start.4 = (bf16[1024,128]{1,0:T(8,128)(2,1)S(1)}, bf16[1024,128]{1,0:T(8,128)(2,1)S(1)}, u32[]{:S(2)}, u32[]{:S(2)}) collective-permute-start(bf16[1024,128]{1,0:T(8,128)(2,1)S(1)} %collective-permute-done.refs_3_), channel_id=1, source_target_pairs={{0,1},{1,0},{2,3},{3,2},{4,5},{5,4},{6,7},{7,6},{8,9},{9,8},{10,11... | collective-permute-start | bytes 786440 | tf_op jit(solution)/shard_map/ppermute | solution.py:330
  12.4 1.4 %collective-permute-start.5 = (s32[4,2048]{1,0:T(4,128)S(1)}, s32[4,2048]{1,0:T(4,128)S(1)}, u32[]{:S(2)}, u32[]{:S(2)}) collective-permute-start(s32[4,2048]{1,0:T(4,128)S(1)} %collective-permute-done.1.refs_9_), channel_id=1, source_target_pairs={{0,1},{1,0},{2,3},{3,2},{4,5},{5,4},{6,7},{7,6},{8,9},{9,8},{10,11... | collective-permute-start | bytes 98312 | tf_op jit(solution)/shard_map/ppermute | solution.py:330
  19.4 5.0 %collective-permute-start.6 = (f32[4,48,128]{2,1,0:T(8,128)S(1)}, f32[4,48,128]{2,1,0:T(8,128)S(1)}, u32[]{:S(2)}, u32[]{:S(2)}) collective-permute-start(f32[4,48,128]{2,1,0:T(8,128)S(1)} %slice_bitcast_fusion), channel_id=1, source_target_pairs={{0,4},{4,0},{8,12},{12,8},{16,20},{20,16},{24,28},{28,24},{1,5},{5... | collective-permute-start | bytes 294920 | tf_op jit(solution)/shard_map/ppermute | solution.py:330
  21.1 14.7 %collective-permute-start.12 = (bf16[128,1024]{1,0:T(8,128)(2,1)S(1)}, bf16[128,1024]{1,0:T(8,128)(2,1)S(1)}, u32[]{:S(2)}, u32[]{:S(2)}) collective-permute-start(bf16[128,1024]{1,0:T(8,128)(2,1)S(1)} %copy-done.14), channel_id=1, source_target_pairs={{0,1},{1,0},{2,3},{3,2},{4,5},{5,4},{6,7},{7,6},{8,9},{9,8},{10,11... | collective-permute-start | bytes 786440 | tf_op jit(solution)/shard_map/ppermute | solution.py:330
  21.1 3.4 %collective-permute-start.7 = (bf16[128,1024]{1,0:T(8,128)(2,1)S(1)}, bf16[128,1024]{1,0:T(8,128)(2,1)S(1)}, u32[]{:S(2)}, u32[]{:S(2)}) collective-permute-start(bf16[128,1024]{1,0:T(8,128)(2,1)S(1)} %get-tuple-element.40), channel_id=1, source_target_pairs={{0,1},{1,0},{2,3},{3,2},{4,5},{5,4},{6,7},{7,6},{8,9},{9,8},{10,11... | collective-permute-start | bytes 786440 | tf_op jit(solution)/shard_map/ppermute | solution.py:330
  23.2 12.6 %copy-start.11 = (bf16[128,1024]{1,0:T(8,128)(2,1)S(1)}, bf16[128,1024]{1,0:T(8,128)(2,1)}, u32[]{:S(2)}) copy-start(bf16[128,1024]{1,0:T(8,128)(2,1)} %get-tuple-element.52) | copy-start | bytes 786436
  24.4 5.9 %collective-permute-start.8 = (f32[2,48,128]{2,1,0:T(8,128)S(1)}, f32[2,48,128]{2,1,0:T(8,128)S(1)}, u32[]{:S(2)}, u32[]{:S(2)}) collective-permute-start(f32[2,48,128]{2,1,0:T(8,128)S(1)} %slice_bitcast_fusion.2), channel_id=1, source_target_pairs={{0,8},{4,12},{8,0},{12,4},{16,24},{20,28},{24,16},{28,20},{1,9},{5... | collective-permute-start | bytes 147464 | tf_op jit(solution)/shard_map/ppermute | solution.py:330
  26.0 9.8 %copy-start.2 = (bf16[1,1,1024,128]{3,2,1,0:T(8,128)(2,1)S(1)}, bf16[1,1,1024,128]{3,2,1,0:T(8,128)(2,1)}, u32[]{:S(2)}) copy-start(bf16[1,1,1024,128]{3,2,1,0:T(8,128)(2,1)} %param.19) | copy-start | bytes 786436
  26.1 9.2 %collective-permute-start.10 = (bf16[128,1024]{1,0:T(8,128)(2,1)S(1)}, bf16[128,1024]{1,0:T(8,128)(2,1)S(1)}, u32[]{:S(2)}, u32[]{:S(2)}) collective-permute-start(bf16[128,1024]{1,0:T(8,128)(2,1)S(1)} %add_convert_fusion), channel_id=1, source_target_pairs={{0,2},{1,3},{2,0},{3,1},{4,6},{5,7},{6,4},{7,5},{8,10},{9,11},{10,... | collective-permute-start | bytes 786440 | tf_op jit(solution)/shard_map/ppermute | solution.py:330
  30.4 4.9 %collective-permute-start.9 = (f32[1,48,128]{2,1,0:T(8,128)S(1)}, f32[1,48,128]{2,1,0:T(8,128)S(1)}, u32[]{:S(2)}, u32[]{:S(2)}) collective-permute-start(f32[1,48,128]{2,1,0:T(8,128)S(1)} %slice_bitcast_fusion.4), channel_id=1, source_target_pairs={{0,16},{4,20},{8,24},{12,28},{16,0},{20,4},{24,8},{28,12},{1,17},{... | collective-permute-start | bytes 73736 | tf_op jit(solution)/shard_map/ppermute | solution.py:330
  35.4 3.9 %collective-permute-start.11 = (f32[48,128]{1,0:T(8,128)S(1)}, f32[48,128]{1,0:T(8,128)S(1)}, u32[]{:S(2)}, u32[]{:S(2)}) collective-permute-start(f32[48,128]{1,0:T(8,128)S(1)} %bitcast.68), channel_id=1, source_target_pairs={{0,2},{1,3},{2,0},{3,1},{4,6},{5,7},{6,4},{7,5},{8,10},{9,11},{10,... | collective-permute-start | bytes 73736 | tf_op jit(solution)/shard_map/ppermute | solution.py:330
  39.2 1.2 %collective-permute-start.13 = (f32[48,128]{1,0:T(8,128)S(1)}, f32[48,128]{1,0:T(8,128)S(1)}, u32[]{:S(2)}, u32[]{:S(2)}) collective-permute-start(f32[48,128]{1,0:T(8,128)S(1)} %bitcast_add_fusion.refs_0_), channel_id=1, source_target_pairs={{0,1},{1,0},{2,3},{3,2},{4,5},{5,4},{6,7},{7,6},{8,9},{9,8},{10,11... | collective-permute-start | bytes 73736 | tf_op jit(solution)/shard_map/ppermute | solution.py:330

commit v6 on v4

--- a/solution.py
+++ b/solution.py
@@ -313,7 +313,7 @@
         batches, rows, width = chunks.shape
         bit = lax.axis_size("dp") // batches
         pair = chunks.reshape(batches // 2, 2, rows, width)
-        chunks = pair[:, 0] + move(pair[:, 1], "dp", bit)
+        chunks = pair[:, 0] + move(pair[:, 1].astype(BF16), "dp", bit).astype(F32)
     return chunks
 
 

time: 41 us -> 39.4 us (0.961)
  starting transfers between devices: 12.5 us -> 15 us
  waiting for transfers between devices: 9.05 us -> 6.98 us
  Pallas kernels: 17.3 us -> 15.4 us
    ppermute x14, starting transfers between devices: 12.5 us -> 15 us  [move(): return lax.ppermute(x, axis, [(i, i ^ bit) for i in range(size)])]
    ppermute x14, waiting for transfers between devices: 9.05 us -> 6.98 us  [move(): return lax.ppermute(x, axis, [(i, i ^ bit) for i in range(size)])]
    pallas_call x6, Pallas kernels: 17.3 us -> 15.4 us  [call(): pl.pallas_call(functools.partial(with_fetches, kernel, kinds, ks, len(out...]
  transfers between devices with their start and end apart: 14 -> 14, of which waited for: 6 -> 6; matrix products, arithmetic and copies ran while one was open for 0% -> 1% of each run, Pallas kernels for 28% -> 37%
where the time goes in v6:
time: 39.4 us; the launch traced here: 39.2 us
  Pallas kernels  15.4 us (39%)
  starting transfers between devices  15 us (38%)
  waiting for transfers between devices  6.98 us (18%)
  between operations  0.92 us (2%)
  local copies, waits for them, and re-layouts  0.78 us (2%)
    pallas_call x6, Pallas kernels, call(): pl.pallas_call(functools.partial(with_fetches, kernel, kinds, ks, len(out...  15.4 us
    ppermute x14, starting transfers between devices, move(): return lax.ppermute(x, axis, [(i, i ^ bit) for i in range(size)])  15 us
    ppermute x14, waiting for transfers between devices, move(): return lax.ppermute(x, axis, [(i, i ^ bit) for i in range(size)])  6.98 us
  transfers between devices with their start and end apart: 14, of which 6 were waited for; matrix products, arithmetic and copies ran while one was open for 1% of the time, Pallas kernels for 37%

profile of v6, /device:TPU:0, one launch (start us, length us, event | category | flops | bytes accessed | tf_op | source)
XLA Modules:
  0.0 39.2 jit_solution(11463621730059579159)
XLA Ops:
  0.6 0.0 copy-start.3
  0.6 0.0 copy-start.5
  0.7 0.0 copy-start.6
  0.7 0.0 copy-start
  0.7 0.0 copy-start.7
  0.7 0.0 copy-start.4
  0.7 0.0 copy-start.8
  0.7 0.0 copy-start.1
  0.7 0.5 %collective-permute-start.2 = (bf16[1024,128]{1,0:T(8,128)(2,1)}, bf16[1024,128]{1,0:T(8,128)(2,1)S(1)}, u32[]{:S(2)}, u32[]{:S(2)}) collective-permute-start(bf16[1024,128]{1,0:T(8,128)(2,1)} %bitcast.38), channel_id=1, source_target_pairs={{0,1},{1,0},{2,3},{3,2},{4,5},{5,4},{6,7},{7,6},{8,9},{9,8},{10,11... | collective-permute-start | bytes 786440 | tf_op jit(solution)/shard_map/ppermute | solution.py:308
  1.2 2.6 %collective-permute-start = (bf16[1024,128]{1,0:T(8,128)(2,1)}, bf16[1024,128]{1,0:T(8,128)(2,1)S(1)}, u32[]{:S(2)}, u32[]{:S(2)}) collective-permute-start(bf16[1024,128]{1,0:T(8,128)(2,1)} %bitcast.39), channel_id=1, source_target_pairs={{0,2},{1,3},{2,0},{3,1},{4,6},{5,7},{6,4},{7,5},{8,10},{9,11},{10,... | collective-permute-start | bytes 786440 | tf_op jit(solution)/shard_map/ppermute | solution.py:308
  3.8 0.2 collective-permute-start.3
  4.0 0.3 collective-permute-start.1
  4.2 1.0 %collective-permute-done.3.refs_10_ = s32[4,2048]{1,0:T(4,128)S(1)} collective-permute-done((s32[4,2048]{1,0:T(4,128)}, s32[4,2048]{1,0:T(4,128)S(1)}, u32[]{:S(2)}, u32[]{:S(2)}) %collective-permute-start.3) | collective-permute-done | bytes 32800 | tf_op jit(solution)/shard_map/ppermute | solution.py:308
  5.2 0.0 copy-start.13
  5.2 0.0 collective-permute-done.2.refs_4_
  5.2 0.0 copy-start.10
  5.2 0.6 %copy-done.13 = s32[4,2048]{1,0:T(4,128)} copy-done((s32[4,2048]{1,0:T(4,128)}, s32[4,2048]{1,0:T(4,128)S(1)}, u32[]{:S(2)}) %copy-start.13) | copy-done | bytes 32792
  5.8 0.1 copy-done.10
  5.9 6.2 %near_edges.1 = (bf16[128,1024]{1,0:T(8,128)(2,1)}, bf16[128,1024]{1,0:T(8,128)(2,1)}, f32[8,48,128]{2,1,0:T(8,128)}, bf16[2,128,2048]{2,1,0:T(8,128)(2,1)}) custom-call(bf16[1024,128]{1,0:T(8,128)(2,1)} %bitcast.35, f32[1,128]{1,0:T(1,128)} %bitcast.50, bf16[128,128]{1,0:T(8,128)(2,1)} %refs_3_.1, bf16[1024,128]{1,0:T(8,128)(2,1)} %bitcast.40, ...), custom_call_target="tpu_custom_call" | custom-call | flops 1 | bytes 1 | tf_op jit(solution)/shard_map/near_edges/pallas_call | solution.py:366
  12.1 0.0 collective-permute-done.1.refs_9_
  12.1 0.0 collective-permute-done.refs_3_
  12.2 0.2 collective-permute-start.4
  12.4 0.3 collective-permute-start.5
  12.7 0.0 copy-start.12
  12.7 0.0 copy-start.9
  12.7 0.2 collective-permute-start.12
  12.9 0.9 %collective-permute-done.5.refs_10_ = s32[4,2048]{1,0:T(4,128)S(1)} collective-permute-done((s32[4,2048]{1,0:T(4,128)S(1)}, s32[4,2048]{1,0:T(4,128)S(1)}, u32[]{:S(2)}, u32[]{:S(2)}) %collective-permute-start.5) | collective-permute-done | bytes 32800 | tf_op jit(solution)/shard_map/ppermute | solution.py:308
  13.8 0.0 collective-permute-done.4.refs_4_
  13.8 0.0 copy-done.3
  13.8 0.0 copy-done.5
  13.8 0.0 copy-done.6
  13.8 0.0 copy-done
  13.8 0.0 copy-done.7
  13.8 0.0 copy-done.4
  13.9 0.0 copy-done.8
  13.9 0.0 copy-done.1
  13.9 3.9 %far_edges.1 = (bf16[128,1024]{1,0:T(8,128)(2,1)S(1)}, bf16[128,1024]{1,0:T(8,128)(2,1)S(1)}, f32[8,48,128]{2,1,0:T(8,128)S(1)}, bf16[2,128,2048]{2,1,0:T(8,128)(2,1)S(1)}) custom-call(bf16[1024,128]{1,0:T(8,128)(2,1)S(1)} %bitcast.36, f32[1,128]{1,0:T(1,128)S(1)} %bitcast.51, bf16[128,128]{1,0:T(8,128)(2,1)S(1)} %copy-done.5, ...), custom_call_target="tpu_custom_call" | custom-call | flops 4294967296 | bytes 1048576 | tf_op jit(solution)/shard_map/far_edges/pallas_call | solution.py:366
  17.8 0.0 copy-done.12
  17.9 1.6 %collective-permute-start.6 = (bf16[4,48,128]{2,1,0:T(8,128)(2,1)S(1)}, bf16[4,48,128]{2,1,0:T(8,128)(2,1)S(1)}, u32[]{:S(2)}, u32[]{:S(2)}) collective-permute-start(bf16[4,48,128]{2,1,0:T(8,128)(2,1)S(1)} %fusion.1), channel_id=1, source_target_pairs={{0,4},{4,0},{8,12},{12,8},{16,20},{20,16},{24,28},{28,24},{1,5},{5... | collective-permute-start | bytes 147464 | tf_op jit(solution)/shard_map/ppermute | solution.py:308
  19.5 0.0 collective-permute-start.7
  19.5 0.0 copy-done.9
  19.5 1.6 %near_sources.1.refs_3_ = f32[512,256]{1,0:T(8,128)S(1)} custom-call(s32[4,4]{1,0:T(4,128)S(1)} %bitcast.48, s32[4,2048]{1,0:T(4,128)S(1)} %bitcast.44, bf16[2,128,2048]{2,1,0:T(8,128)(2,1)S(1)} %copy-done.9), custom_call_target="tpu_custom_call" | custom-call | flops 536870912 | bytes 1048576 | tf_op jit(solution)/shard_map/near_sources/pallas_call | solution.py:366
  21.1 0.0 copy-start.11
  21.1 0.9 %collective-permute-done.6 = bf16[4,48,128]{2,1,0:T(8,128)(2,1)S(1)} collective-permute-done((bf16[4,48,128]{2,1,0:T(8,128)(2,1)S(1)}, bf16[4,48,128]{2,1,0:T(8,128)(2,1)S(1)}, u32[]{:S(2)}, u32[]{:S(2)}) %collective-permute-start.6) | collective-permute-done | bytes 49184 | tf_op jit(solution)/shard_map/ppermute | solution.py:308
  22.0 0.0 collective-permute-done.7
  22.1 0.0 copy-start.2
  22.1 2.8 %collective-permute-start.8 = (bf16[2,48,128]{2,1,0:T(8,128)(2,1)S(1)}, bf16[2,48,128]{2,1,0:T(8,128)(2,1)S(1)}, u32[]{:S(2)}, u32[]{:S(2)}) collective-permute-start(bf16[2,48,128]{2,1,0:T(8,128)(2,1)S(1)} %fusion.3), channel_id=1, source_target_pairs={{0,8},{4,12},{8,0},{12,4},{16,24},{20,28},{24,16},{28,20},{1,9},{5... | collective-permute-start | bytes 73736 | tf_op jit(solution)/shard_map/ppermute | solution.py:308
  24.8 0.1 add_convert_fusion
  24.9 2.2 %collective-permute-start.10 = (bf16[128,1024]{1,0:T(8,128)(2,1)S(1)}, bf16[128,1024]{1,0:T(8,128)(2,1)S(1)}, u32[]{:S(2)}, u32[]{:S(2)}) collective-permute-start(bf16[128,1024]{1,0:T(8,128)(2,1)S(1)} %add_convert_fusion), channel_id=1, source_target_pairs={{0,2},{1,3},{2,0},{3,1},{4,6},{5,7},{6,4},{7,5},{8,10},{9,11},{10,... | collective-permute-start | bytes 786440 | tf_op jit(solution)/shard_map/ppermute | solution.py:308
  27.1 1.6 %far_sources.1.refs_5_ = f32[512,256]{1,0:T(8,128)S(1)} custom-call(s32[4,4]{1,0:T(4,128)S(1)} %bitcast.49, s32[4,2048]{1,0:T(4,128)S(1)} %bitcast.45, bf16[2,128,2048]{2,1,0:T(8,128)(2,1)S(1)} %get-tuple-element.45.refs_2_, f32[512,256]{1,0:T(8,128)S(1)} %near_sources.1.refs_3_), custom_call_target="tpu_custom_call" | custom-call | flops 536870912 | bytes 1048576 | tf_op jit(solution)/shard_map/far_sources/pallas_call | solution.py:366
  28.7 0.0 collective-permute-done.8
  28.7 2.5 %collective-permute-start.9 = (bf16[1,48,128]{2,1,0:T(8,128)(2,1)S(1)}, bf16[1,48,128]{2,1,0:T(8,128)(2,1)S(1)}, u32[]{:S(2)}, u32[]{:S(2)}) collective-permute-start(bf16[1,48,128]{2,1,0:T(8,128)(2,1)S(1)} %fusion.5), channel_id=1, source_target_pairs={{0,16},{4,20},{8,24},{12,28},{16,0},{20,4},{24,8},{28,12},{1,17},{... | collective-permute-start | bytes 36872 | tf_op jit(solution)/shard_map/ppermute | solution.py:308
  31.2 2.2 %collective-permute-done.9 = bf16[1,48,128]{2,1,0:T(8,128)(2,1)S(1)} collective-permute-done((bf16[1,48,128]{2,1,0:T(8,128)(2,1)S(1)}, bf16[1,48,128]{2,1,0:T(8,128)(2,1)S(1)}, u32[]{:S(2)}, u32[]{:S(2)}) %collective-permute-start.9) | collective-permute-done | bytes 12320 | tf_op jit(solution)/shard_map/ppermute | solution.py:308
  33.4 0.0 collective-permute-done.10.refs_7_
  33.4 1.7 %collective-permute-start.11 = (f32[48,128]{1,0:T(8,128)S(1)}, f32[48,128]{1,0:T(8,128)S(1)}, u32[]{:S(2)}, u32[]{:S(2)}) collective-permute-start(f32[48,128]{1,0:T(8,128)S(1)} %bitcast.60), channel_id=1, source_target_pairs={{0,2},{1,3},{2,0},{3,1},{4,6},{5,7},{6,4},{7,5},{8,10},{9,11},{10,... | collective-permute-start | bytes 73736 | tf_op jit(solution)/shard_map/ppermute | solution.py:308
  35.1 0.0 collective-permute-done.12
  35.1 0.0 copy-done.11
  35.1 0.1 convert_add_fusion.refs_6_
  35.2 0.0 copy-done.2
  35.2 1.4 %atoms.1 = (bf16[1024,128]{1,0:T(8,128)(2,1)}, bf16[1024,128]{1,0:T(8,128)(2,1)}) custom-call(bf16[1024,128]{1,0:T(8,128)(2,1)S(1)} %bitcast.37, f32[1,128]{1,0:T(1,128)S(1)} %bitcast.52, bf16[128,128]{1,0:T(8,128)(2,1)S(1)} %copy-done.3, bf16[128,128]{1,0:T(8,128)(2,1)S(1)} %copy-done.5, bf16[1024,128]{1,0:T(8,128)(2,1)S(1)} %bitcast.41, ...), custom_call_target="tpu_custom_call" | custom-call | flops 67108864 | bytes 1048576 | tf_op jit(solution)/shard_map/atoms/pallas_call | solution.py:366
  36.6 0.7 %collective-permute-done.11 = f32[48,128]{1,0:T(8,128)S(1)} collective-permute-done((f32[48,128]{1,0:T(8,128)S(1)}, f32[48,128]{1,0:T(8,128)S(1)}, u32[]{:S(2)}, u32[]{:S(2)}) %collective-permute-start.11) | collective-permute-done | bytes 24608 | tf_op jit(solution)/shard_map/ppermute | solution.py:308
  37.3 0.0 collective-permute-start.13
  37.3 1.2 %collective-permute-done.13.refs_1_ = f32[48,128]{1,0:T(8,128)S(1)} collective-permute-done((f32[48,128]{1,0:T(8,128)S(1)}, f32[48,128]{1,0:T(8,128)S(1)}, u32[]{:S(2)}, u32[]{:S(2)}) %collective-permute-start.13) | collective-permute-done | bytes 24608 | tf_op jit(solution)/shard_map/ppermute | solution.py:308
  38.5 0.7 %weights.1 = (f32[16,128]{1,0:T(8,128)}, f32[16,128]{1,0:T(8,128)}, f32[16,128]{1,0:T(8,128)}, f32[1,16]{1,0:T(1,128)}) custom-call(f32[48,128]{1,0:T(8,128)S(1)} %bitcast_add_fusion.refs_0_, f32[48,128]{1,0:T(8,128)S(1)} %collective-permute-done.13.refs_1_, bf16[128,128]{1,0:T(8,128)(2,1)S(1)} %copy-done.3, f32[1,128]{1,0:T(1,128)S(1)} %bitcast.53), custom_call_target="tpu_custom_call" | custom-call | flops 1 | bytes 1 | tf_op jit(solution)/shard_map/weights/pallas_call | solution.py:366
  (8 shorter events, 0.1 us)
Async XLA Ops:
  0.6 13.2 %copy-start.3 = (bf16[128,128]{1,0:T(8,128)(2,1)S(1)}, bf16[128,128]{1,0:T(8,128)(2,1)}, u32[]{:S(2)}) copy-start(bf16[128,128]{1,0:T(8,128)(2,1)} %refs_2_.7) | copy-start | bytes 98308
  0.6 13.2 %copy-start.5 = (bf16[128,128]{1,0:T(8,128)(2,1)S(1)}, bf16[128,128]{1,0:T(8,128)(2,1)}, u32[]{:S(2)}) copy-start(bf16[128,128]{1,0:T(8,128)(2,1)} %refs_3_.1) | copy-start | bytes 98308
  0.7 13.2 %copy-start.6 = (bf16[128,128]{1,0:T(8,128)(2,1)S(1)}, bf16[128,128]{1,0:T(8,128)(2,1)}, u32[]{:S(2)}) copy-start(bf16[128,128]{1,0:T(8,128)(2,1)} %refs_6_.3) | copy-start | bytes 98308
  0.7 13.2 %copy-start = (bf16[1,1,4,2048,128]{4,3,2,1,0:T(8,128)(2,1)S(1)}, bf16[1,1,4,2048,128]{4,3,2,1,0:T(8,128)(2,1)}, u32[]{:S(2)}) copy-start(bf16[1,1,4,2048,128]{4,3,2,1,0:T(8,128)(2,1)} %param.18) | copy-start | bytes 6291460
  0.7 13.2 %copy-start.7 = (s32[1,4,4]{2,1,0:T(4,128)S(1)}, s32[1,4,4]{2,1,0:T(4,128)}, u32[]{:S(2)}) copy-start(s32[1,4,4]{2,1,0:T(4,128)} %param.17) | copy-start | bytes 196
  0.7 13.2 %copy-start.4 = (s32[1,1,4,2048]{3,2,1,0:T(4,128)S(1)}, s32[1,1,4,2048]{3,2,1,0:T(4,128)}, u32[]{:S(2)}) copy-start(s32[1,1,4,2048]{3,2,1,0:T(4,128)} %param.15) | copy-start | bytes 98308
  0.7 13.2 %copy-start.8 = (f32[128]{0:T(128)S(1)}, f32[128]{0:T(128)}, u32[]{:S(2)}) copy-start(f32[128]{0:T(128)} %param.11) | copy-start | bytes 1540
  0.7 13.2 %copy-start.1 = (bf16[1,1,1024,128]{3,2,1,0:T(8,128)(2,1)S(1)}, bf16[1,1,1024,128]{3,2,1,0:T(8,128)(2,1)}, u32[]{:S(2)}) copy-start(bf16[1,1,1024,128]{3,2,1,0:T(8,128)(2,1)} %param.10) | copy-start | bytes 786436
  0.7 4.5 %collective-permute-start.2 = (bf16[1024,128]{1,0:T(8,128)(2,1)}, bf16[1024,128]{1,0:T(8,128)(2,1)S(1)}, u32[]{:S(2)}, u32[]{:S(2)}) collective-permute-start(bf16[1024,128]{1,0:T(8,128)(2,1)} %bitcast.38), channel_id=1, source_target_pairs={{0,1},{1,0},{2,3},{3,2},{4,5},{5,4},{6,7},{7,6},{8,9},{9,8},{10,11... | collective-permute-start | bytes 786440 | tf_op jit(solution)/shard_map/ppermute | solution.py:308
  1.2 10.9 %collective-permute-start = (bf16[1024,128]{1,0:T(8,128)(2,1)}, bf16[1024,128]{1,0:T(8,128)(2,1)S(1)}, u32[]{:S(2)}, u32[]{:S(2)}) collective-permute-start(bf16[1024,128]{1,0:T(8,128)(2,1)} %bitcast.39), channel_id=1, source_target_pairs={{0,2},{1,3},{2,0},{3,1},{4,6},{5,7},{6,4},{7,5},{8,10},{9,11},{10,... | collective-permute-start | bytes 786440 | tf_op jit(solution)/shard_map/ppermute | solution.py:308
  3.8 1.4 %collective-permute-start.3 = (s32[4,2048]{1,0:T(4,128)}, s32[4,2048]{1,0:T(4,128)S(1)}, u32[]{:S(2)}, u32[]{:S(2)}) collective-permute-start(s32[4,2048]{1,0:T(4,128)} %bitcast.61), channel_id=1, source_target_pairs={{0,1},{1,0},{2,3},{3,2},{4,5},{5,4},{6,7},{7,6},{8,9},{9,8},{10,11... | collective-permute-start | bytes 98312 | tf_op jit(solution)/shard_map/ppermute | solution.py:308
  4.0 8.2 %collective-permute-start.1 = (s32[4,2048]{1,0:T(4,128)}, s32[4,2048]{1,0:T(4,128)S(1)}, u32[]{:S(2)}, u32[]{:S(2)}) collective-permute-start(s32[4,2048]{1,0:T(4,128)} %bitcast.62), channel_id=1, source_target_pairs={{0,2},{1,3},{2,0},{3,1},{4,6},{5,7},{6,4},{7,5},{8,10},{9,11},{10,... | collective-permute-start | bytes 98312 | tf_op jit(solution)/shard_map/ppermute | solution.py:308
  5.2 0.6 %copy-start.13 = (s32[4,2048]{1,0:T(4,128)}, s32[4,2048]{1,0:T(4,128)S(1)}, u32[]{:S(2)}) copy-start(s32[4,2048]{1,0:T(4,128)S(1)} %collective-permute-done.3.refs_10_) | copy-start | bytes 98308
  5.2 0.7 %copy-start.10 = (bf16[1024,128]{1,0:T(8,128)(2,1)}, bf16[1024,128]{1,0:T(8,128)(2,1)S(1)}, u32[]{:S(2)}) copy-start(bf16[1024,128]{1,0:T(8,128)(2,1)S(1)} %collective-permute-done.2.refs_4_) | copy-start | bytes 786436
  12.2 1.7 %collective-permute-start.4 = (bf16[1024,128]{1,0:T(8,128)(2,1)S(1)}, bf16[1024,128]{1,0:T(8,128)(2,1)S(1)}, u32[]{:S(2)}, u32[]{:S(2)}) collective-permute-start(bf16[1024,128]{1,0:T(8,128)(2,1)S(1)} %collective-permute-done.refs_3_), channel_id=1, source_target_pairs={{0,1},{1,0},{2,3},{3,2},{4,5},{5,4},{6,7},{7,6},{8,9},{9,8},{10,11... | collective-permute-start | bytes 786440 | tf_op jit(solution)/shard_map/ppermute | solution.py:308
  12.4 1.4 %collective-permute-start.5 = (s32[4,2048]{1,0:T(4,128)S(1)}, s32[4,2048]{1,0:T(4,128)S(1)}, u32[]{:S(2)}, u32[]{:S(2)}) collective-permute-start(s32[4,2048]{1,0:T(4,128)S(1)} %collective-permute-done.1.refs_9_), channel_id=1, source_target_pairs={{0,1},{1,0},{2,3},{3,2},{4,5},{5,4},{6,7},{7,6},{8,9},{9,8},{10,11... | collective-permute-start | bytes 98312 | tf_op jit(solution)/shard_map/ppermute | solution.py:308
  12.7 5.1 %copy-start.12 = (f32[8,48,128]{2,1,0:T(8,128)S(1)}, f32[8,48,128]{2,1,0:T(8,128)}, u32[]{:S(2)}) copy-start(f32[8,48,128]{2,1,0:T(8,128)} %get-tuple-element.36) | copy-start | bytes 589828
  12.7 6.7 %copy-start.9 = (bf16[2,128,2048]{2,1,0:T(8,128)(2,1)S(1)}, bf16[2,128,2048]{2,1,0:T(8,128)(2,1)}, u32[]{:S(2)}) copy-start(bf16[2,128,2048]{2,1,0:T(8,128)(2,1)} %get-tuple-element.41.refs_2_) | copy-start | bytes 3145732
  12.7 22.4 %collective-permute-start.12 = (bf16[128,1024]{1,0:T(8,128)(2,1)}, bf16[128,1024]{1,0:T(8,128)(2,1)S(1)}, u32[]{:S(2)}, u32[]{:S(2)}) collective-permute-start(bf16[128,1024]{1,0:T(8,128)(2,1)} %get-tuple-element.53), channel_id=1, source_target_pairs={{0,1},{1,0},{2,3},{3,2},{4,5},{5,4},{6,7},{7,6},{8,9},{9,8},{10,11... | collective-permute-start | bytes 786440 | tf_op jit(solution)/shard_map/ppermute | solution.py:308
  17.9 4.2 %collective-permute-start.6 = (bf16[4,48,128]{2,1,0:T(8,128)(2,1)S(1)}, bf16[4,48,128]{2,1,0:T(8,128)(2,1)S(1)}, u32[]{:S(2)}, u32[]{:S(2)}) collective-permute-start(bf16[4,48,128]{2,1,0:T(8,128)(2,1)S(1)} %fusion.1), channel_id=1, source_target_pairs={{0,4},{4,0},{8,12},{12,8},{16,20},{20,16},{24,28},{28,24},{1,5},{5... | collective-permute-start | bytes 147464 | tf_op jit(solution)/shard_map/ppermute | solution.py:308
  19.5 2.6 %collective-permute-start.7 = (bf16[128,1024]{1,0:T(8,128)(2,1)S(1)}, bf16[128,1024]{1,0:T(8,128)(2,1)S(1)}, u32[]{:S(2)}, u32[]{:S(2)}) collective-permute-start(bf16[128,1024]{1,0:T(8,128)(2,1)S(1)} %get-tuple-element.40), channel_id=1, source_target_pairs={{0,1},{1,0},{2,3},{3,2},{4,5},{5,4},{6,7},{7,6},{8,9},{9,8},{10,11... | collective-permute-start | bytes 786440 | tf_op jit(solution)/shard_map/ppermute | solution.py:308
  21.1 14.1 %copy-start.11 = (bf16[128,1024]{1,0:T(8,128)(2,1)S(1)}, bf16[128,1024]{1,0:T(8,128)(2,1)}, u32[]{:S(2)}) copy-start(bf16[128,1024]{1,0:T(8,128)(2,1)} %get-tuple-element.52) | copy-start | bytes 786436
  22.1 13.1 %copy-start.2 = (bf16[1,1,1024,128]{3,2,1,0:T(8,128)(2,1)S(1)}, bf16[1,1,1024,128]{3,2,1,0:T(8,128)(2,1)}, u32[]{:S(2)}) copy-start(bf16[1,1,1024,128]{3,2,1,0:T(8,128)(2,1)} %param.19) | copy-start | bytes 786436
  22.1 6.6 %collective-permute-start.8 = (bf16[2,48,128]{2,1,0:T(8,128)(2,1)S(1)}, bf16[2,48,128]{2,1,0:T(8,128)(2,1)S(1)}, u32[]{:S(2)}, u32[]{:S(2)}) collective-permute-start(bf16[2,48,128]{2,1,0:T(8,128)(2,1)S(1)} %fusion.3), channel_id=1, source_target_pairs={{0,8},{4,12},{8,0},{12,4},{16,24},{20,28},{24,16},{28,20},{1,9},{5... | collective-permute-start | bytes 73736 | tf_op jit(solution)/shard_map/ppermute | solution.py:308
  24.9 8.5 %collective-permute-start.10 = (bf16[128,1024]{1,0:T(8,128)(2,1)S(1)}, bf16[128,1024]{1,0:T(8,128)(2,1)S(1)}, u32[]{:S(2)}, u32[]{:S(2)}) collective-permute-start(bf16[128,1024]{1,0:T(8,128)(2,1)S(1)} %add_convert_fusion), channel_id=1, source_target_pairs={{0,2},{1,3},{2,0},{3,1},{4,6},{5,7},{6,4},{7,5},{8,10},{9,11},{10,... | collective-permute-start | bytes 786440 | tf_op jit(solution)/shard_map/ppermute | solution.py:308
  28.7 4.7 %collective-permute-start.9 = (bf16[1,48,128]{2,1,0:T(8,128)(2,1)S(1)}, bf16[1,48,128]{2,1,0:T(8,128)(2,1)S(1)}, u32[]{:S(2)}, u32[]{:S(2)}) collective-permute-start(bf16[1,48,128]{2,1,0:T(8,128)(2,1)S(1)} %fusion.5), channel_id=1, source_target_pairs={{0,16},{4,20},{8,24},{12,28},{16,0},{20,4},{24,8},{28,12},{1,17},{... | collective-permute-start | bytes 36872 | tf_op jit(solution)/shard_map/ppermute | solution.py:308
  33.4 3.9 %collective-permute-start.11 = (f32[48,128]{1,0:T(8,128)S(1)}, f32[48,128]{1,0:T(8,128)S(1)}, u32[]{:S(2)}, u32[]{:S(2)}) collective-permute-start(f32[48,128]{1,0:T(8,128)S(1)} %bitcast.60), channel_id=1, source_target_pairs={{0,2},{1,3},{2,0},{3,1},{4,6},{5,7},{6,4},{7,5},{8,10},{9,11},{10,... | collective-permute-start | bytes 73736 | tf_op jit(solution)/shard_map/ppermute | solution.py:308
  37.3 1.2 %collective-permute-start.13 = (f32[48,128]{1,0:T(8,128)S(1)}, f32[48,128]{1,0:T(8,128)S(1)}, u32[]{:S(2)}, u32[]{:S(2)}) collective-permute-start(f32[48,128]{1,0:T(8,128)S(1)} %bitcast_add_fusion.refs_0_), channel_id=1, source_target_pairs={{0,1},{1,0},{2,3},{3,2},{4,5},{5,4},{6,7},{7,6},{8,9},{9,8},{10,11... | collective-permute-start | bytes 73736 | tf_op jit(solution)/shard_map/ppermute | solution.py:308
